TPU v7x, 512 devices: a whole 4x4x16 slice. The times are simulated.
512 devices in a mesh: gx: 16 (over z), gy: 32 (over y, x, core).
Axes of the slice: x: 4, y: 4, z: 16, core: 2. Of those that a mesh axis runs over, the one named last changes fastest.
Arguments:
- fields: float32 [3, 2, 4096, 4096], P(None, None, 'gx', 'gy'), may hold values from -6 to 6
- pole_state: float32 [2, 2, 4096, 4096], P(None, None, 'gx', 'gy'), may hold values from -6 to 6
- stretch_state: float32 [4, 2, 4096, 4096], P(None, None, 'gx', 'gy'), may hold values from -6 to 6
- inverse_permittivity: float32 [4096, 4096], P('gx', 'gy'), may hold values from 0.3 to 1
- pole_rates: bfloat16 [3, 4096, 4096], P(None, 'gx', 'gy'), may hold values from 0.19921875 to 4
- x_profile: float32 [3, 4096], P(None, 'gx'), may hold values from 0.02 to 3, as said below
- y_profile: float32 [3, 4096], P(None, 'gy'), may hold values from 0.02 to 3, as said below
Outputs:
- next_fields: float32 [3, 2, 4096, 4096], P(None, None, 'gx', 'gy')
- next_poles: float32 [2, 2, 4096, 4096], P(None, None, 'gx', 'gy')
- next_stretch: float32 [4, 2, 4096, 4096], P(None, None, 'gx', 'gy')
Inputs may be any that keep to these rules, and one draw needn't show every extreme that they name: `x_profile`: row 0 lies in 0.05 to 1, row 1 in 1 to 3, row 2 in 0.02 to 0.3. `y_profile`: row 0 lies in 0.05 to 1, row 1 in 1 to 3, row 2 in 0.02 to 0.3.
All inputs are finite; a program needn't handle non-finite values.
Results may differ from a plain program's by a relative error of at most 0.0003.
Values sent between devices are 32-bit elements; how exact they have to be, the bound alone decides.
No kernel may reach another device: no remote copies, remote signals or barrier semaphores. Data moves between devices by JAX's collectives and lax.ppermute only.
A program may use at most 64 MiB of HBM per device.

v0:
```python
import math

import jax
import jax.numpy as jnp
from jax import lax
from jax.sharding import PartitionSpec as P

section_step = 0.25
highest = lax.Precision.HIGHEST


def from_partner(value, axis, distance):
    mask = 2**distance
    pairs = [(source, source ^ mask) for source in range(lax.axis_size(axis))]
    return lax.ppermute(value, axis, pairs)


def phases(row_count, col_count, period, orient):
    product = (
        jnp.arange(row_count, dtype=jnp.int32)[:, None]
        * jnp.arange(col_count, dtype=jnp.int32)[None, :]
        % period
    )
    angles = orient * 2.0 * math.pi / period * product.astype(jnp.float32)
    return (jnp.cos(angles), jnp.sin(angles))


def along(matrix, values, placing):
    if placing == "last":
        return jnp.einsum("...m,km->...k", values, matrix, precision=highest)
    return jnp.einsum("km,...mb->...kb", matrix, values, precision=highest)


def complex_apply(matrices, packed, placing):
    real_mat, imag_mat = matrices
    real_part = along(real_mat, packed[0], placing) - along(imag_mat, packed[1], placing)
    imag_part = along(real_mat, packed[1], placing) + along(imag_mat, packed[0], placing)
    return jnp.stack([real_part, imag_part])


def rotate(packed, cosine, sine_part):
    return jnp.stack(
        [packed[0] * cosine - packed[1] * sine_part, packed[0] * sine_part + packed[1] * cosine]
    )


def wavenumber(freq_index, period):
    signed = jnp.where(freq_index < period // 2, freq_index, freq_index - period)
    signed = jnp.where(freq_index == period // 2, 0, signed)
    return signed.astype(jnp.float32) * (2.0 * math.pi / period)


def times_ik(packed, wave_vec):
    return jnp.stack([-wave_vec * packed[1], wave_vec * packed[0]])


def middle(packed, first_index, count, local_len, placing):
    period = local_len * count
    layout = (local_len, 1)
    local_pos = jnp.arange(local_len, dtype=jnp.int32).reshape(layout)
    twists = (local_pos * first_index % period).astype(jnp.float32) * (2.0 * math.pi / period)
    cosine = jnp.cos(twists)
    sine_part = jnp.sin(twists)
    packed = rotate(packed, cosine, -sine_part)
    spectrum = complex_apply(phases(local_len, local_len, local_len, -1.0), packed, placing)
    spectrum = times_ik(spectrum, wavenumber(first_index + count * local_pos, period))
    back_real, back_imag = phases(local_len, local_len, local_len, 1.0)
    packed = complex_apply((back_real / local_len, back_imag / local_len), spectrum, placing)
    return rotate(packed, cosine, sine_part)


def reversed_bits(position, count):
    levels = count.bit_length() - 1
    result = jnp.zeros((), jnp.int32)
    for bit_pos in range(levels):
        result = result + position // (1 << bit_pos) % 2 * (1 << levels - 1 - bit_pos)
    return result


def butterfly_forward(packed, position, count, swapper):
    levels = count.bit_length() - 1
    for bit_pos in reversed(range(levels)):
        half_span = 1 << bit_pos
        partner = swapper(packed, bit_pos)
        offset = (position % half_span).astype(jnp.float32) * (-math.pi / half_span)
        is_upper = position // half_span % 2 == 1
        lower_value = packed + partner
        upper_value = rotate(partner - packed, jnp.cos(offset), jnp.sin(offset))
        packed = jnp.where(is_upper, upper_value, lower_value)
    return packed


def butterfly_backward(packed, position, count, swapper):
    levels = count.bit_length() - 1
    for bit_pos in range(levels):
        half_span = 1 << bit_pos
        partner = swapper(packed, bit_pos)
        offset = (position % half_span).astype(jnp.float32) * (math.pi / half_span)
        cosine = jnp.cos(offset)
        sine_part = jnp.sin(offset)
        is_upper = position // half_span % 2 == 1
        lower_value = 0.5 * (packed + rotate(partner, cosine, sine_part))
        upper_value = 0.5 * (partner - rotate(packed, cosine, sine_part))
        packed = jnp.where(is_upper, upper_value, lower_value)
    return packed


def line_derivative(packed):
    period = packed.shape[-1]
    blocks = period // 128
    leading = packed.shape[:-1]
    blocked = packed.reshape(leading + (blocks, 128))
    blocked = complex_apply(phases(blocks, blocks, blocks, -1.0), blocked, "second")
    twist_cos, twist_sin = phases(blocks, 128, period, -1.0)
    blocked = rotate(blocked, twist_cos, twist_sin)
    blocked = complex_apply(phases(128, 128, 128, -1.0), blocked, "last")
    first_part = jnp.arange(blocks, dtype=jnp.int32)[:, None]
    second_part = jnp.arange(128, dtype=jnp.int32)[None, :]
    blocked = times_ik(blocked, wavenumber(first_part + blocks * second_part, period))
    inverse_real, inverse_imag = phases(128, 128, 128, 1.0)
    blocked = complex_apply((inverse_real / 128, inverse_imag / 128), blocked, "last")
    blocked = rotate(blocked, twist_cos, -twist_sin)
    inverse_real, inverse_imag = phases(blocks, blocks, blocks, 1.0)
    blocked = complex_apply((inverse_real / blocks, inverse_imag / blocks), blocked, "second")
    return blocked.reshape(packed.shape)


def advance(
    fields,
    pole_state,
    stretch_state,
    inverse_permittivity,
    pole_rates,
    x_profile,
    y_profile,
    ez_dx,
    hy_dx,
    ez_dy,
    hx_dy,
):
    conduct_x = x_profile[0][None, :, None]
    stretch_x = x_profile[1][None, :, None]
    shift_x = x_profile[2][None, :, None]
    conduct_y = y_profile[0][None, None, :]
    stretch_y = y_profile[1][None, None, :]
    shift_y = y_profile[2][None, None, :]
    ez_x_term = ez_dx / stretch_x + stretch_state[0]
    hy_x_term = hy_dx / stretch_x + stretch_state[1]
    ez_y_term = ez_dy / stretch_y + stretch_state[2]
    hx_y_term = hx_dy / stretch_y + stretch_state[3]
    decay_x = conduct_x / stretch_x + shift_x
    decay_y = conduct_y / stretch_y + shift_y
    feed_x = conduct_x / (stretch_x * stretch_x)
    feed_y = conduct_y / (stretch_y * stretch_y)
    stretch_rate = jnp.stack(
        [
            -decay_x * stretch_state[0] - feed_x * ez_dx,
            -decay_x * stretch_state[1] - feed_x * hy_dx,
            -decay_y * stretch_state[2] - feed_y * ez_dy,
            -decay_y * stretch_state[3] - feed_y * hx_dy,
        ]
    )
    inverse_eps = inverse_permittivity[None]
    damping = pole_rates[0].astype(jnp.float32)[None]
    resonance = pole_rates[1].astype(jnp.float32)[None]
    plasma = pole_rates[2].astype(jnp.float32)[None]
    polar = pole_state[0]
    current = pole_state[1]
    field_rate = jnp.stack([inverse_eps * (hy_x_term - hx_y_term - current), -ez_y_term, ez_x_term])
    pole_rate = jnp.stack([current, -damping * current - resonance * polar + plasma * fields[0]])
    return (
        fields + section_step * field_rate,
        pole_state + section_step * pole_rate,
        stretch_state + section_step * stretch_rate,
    )


def shards(
    fields, pole_state, stretch_state, inverse_permittivity, pole_rates, x_profile, y_profile
):
    x_count = lax.axis_size("gx")
    x_index = lax.axis_index("gx")
    local_x = fields.shape[2]
    x_packed = jnp.stack([fields[0], fields[2]])
    y_packed = jnp.stack([fields[0], fields[1]])
    x_spectra = butterfly_forward(
        x_packed, x_index, x_count, lambda values, bit_pos: from_partner(values, "gx", bit_pos)
    )
    x_spectra = middle(x_spectra, reversed_bits(x_index, x_count), x_count, local_x, "second")
    x_deriv = butterfly_backward(
        x_spectra, x_index, x_count, lambda values, bit_pos: from_partner(values, "gx", bit_pos)
    )
    y_lines = line_derivative(
        lax.all_to_all(y_packed, "gy", split_axis=2, concat_axis=3, tiled=True)
    )
    y_deriv = lax.all_to_all(y_lines, "gy", split_axis=3, concat_axis=2, tiled=True)
    next_fields, next_poles, next_stretch = advance(
        fields,
        pole_state,
        stretch_state,
        inverse_permittivity,
        pole_rates,
        x_profile,
        y_profile,
        x_deriv[0],
        x_deriv[1],
        y_deriv[0],
        y_deriv[1],
    )
    return (next_fields, next_poles, next_stretch)


def solution(mesh):
    return jax.shard_map(
        shards,
        mesh=mesh,
        in_specs=(
            P(None, None, "gx", "gy"),
            P(None, None, "gx", "gy"),
            P(None, None, "gx", "gy"),
            P("gx", "gy"),
            P(None, "gx", "gy"),
            P(None, "gx"),
            P(None, "gy"),
        ),
        out_specs=(P(None, None, "gx", "gy"), P(None, None, "gx", "gy"), P(None, None, "gx", "gy")),
        check_vma=False,
    )
```

profile of v0, /device:TPU:99, one launch (start us, length us, event | category | flops | bytes accessed | tf_op | source)
XLA Modules:
  0.0 346.3 jit_solution(12825197674467183239)
XLA Ops:
  0.7 1.1 stack.123
  1.7 1.2 copy.123
  2.9 7.9 %all-to-all-start = ((f32[2,2,256,128]{3,1,0,2:T(2,128)}), f32[2,2,256,128]{3,1,0,2:T(2,128)S(1)}, u32[]{:S(2)}, u32[]{:S(2)}) async-start(f32[2,2,256,128]{3,1,0,2:T(2,128)} %copy.123), calls=%async_computation | async-start | bytes 1048576 | tf_op jit(solution)/shard_map/all_to_all | solution.py:194
  10.9 1.4 copy.100
  12.3 0.9 bitcast_convert_fusion.1
  13.2 0.9 negate_bitcast_fusion
  14.0 1.2 copy.95
  15.7 0.9 pad_maximum_fusion
  16.6 12.7 %collective-permute-start = (f32[2,2,256,128]{2,3,1,0:T(8,128)S(1)}, f32[2,2,256,128]{2,3,1,0:T(8,128)S(1)}, u32[]{:S(2)}, u32[]{:S(2)}) collective-permute-start(f32[2,2,256,128]{2,3,1,0:T(8,128)S(1)} %get-tuple-element.66), channel_id=1, source_target_pairs={{0,256},{32,288},{64,320},{96,352},{128,384},{160,416},{192,448},{... | collective-permute-start | bytes 1572872 | tf_op jit(solution)/shard_map/ppermute | solution.py:15
  33.8 29.7 %collective-permute-done = f32[2,2,256,128]{2,3,1,0:T(8,128)S(1)} collective-permute-done((f32[2,2,256,128]{2,3,1,0:T(8,128)S(1)}, f32[2,2,256,128]{2,3,1,0:T(8,128)S(1)}, u32[]{:S(2)}, u32[]{:S(2)}) %collective-permute-start) | collective-permute-done | bytes 524320 | tf_op jit(solution)/shard_map/ppermute | solution.py:15
  63.7 7.8 %collective-permute-start.1 = (f32[2,2,256,128]{2,3,1,0:T(8,128)S(1)}, f32[2,2,256,128]{2,3,1,0:T(8,128)S(1)}, u32[]{:S(2)}, u32[]{:S(2)}) collective-permute-start(f32[2,2,256,128]{2,3,1,0:T(8,128)S(1)} %maximum_select_fusion), channel_id=1, source_target_pairs={{0,128},{32,160},{64,192},{96,224},{128,0},{160,32},{192,64},{224,... | collective-permute-start | bytes 1572872 | tf_op jit(solution)/shard_map/ppermute | solution.py:15
  72.2 0.6 fusion.3
  73.4 46.0 %collective-permute-done.1 = f32[2,2,256,128]{2,3,1,0:T(8,128)S(1)} collective-permute-done((f32[2,2,256,128]{2,3,1,0:T(8,128)S(1)}, f32[2,2,256,128]{2,3,1,0:T(8,128)S(1)}, u32[]{:S(2)}, u32[]{:S(2)}) %collective-permute-start.1) | collective-permute-done | bytes 524320 | tf_op jit(solution)/shard_map/ppermute | solution.py:15
  119.8 1.9 collective-permute-start.2
  123.6 23.2 %collective-permute-done.2 = f32[2,2,256,128]{2,3,1,0:T(8,128)S(1)} collective-permute-done((f32[2,2,256,128]{2,3,1,0:T(8,128)S(1)}, f32[2,2,256,128]{2,3,1,0:T(8,128)S(1)}, u32[]{:S(2)}, u32[]{:S(2)}) %collective-permute-start.2) | collective-permute-done | bytes 524320 | tf_op jit(solution)/shard_map/ppermute | solution.py:15
  147.1 2.1 collective-permute-start.3
  150.3 1.2 fusion.1
  151.5 9.6 %collective-permute-done.3 = f32[2,2,256,128]{2,3,1,0:T(8,128)S(1)} collective-permute-done((f32[2,2,256,128]{2,3,1,0:T(8,128)S(1)}, f32[2,2,256,128]{2,3,1,0:T(8,128)S(1)}, u32[]{:S(2)}, u32[]{:S(2)}) %collective-permute-start.3) | collective-permute-done | bytes 524320 | tf_op jit(solution)/shard_map/ppermute | solution.py:15
  161.4 1.4 fusion.46
  162.7 1.4 fusion.44
  164.1 1.4 fusion.5
  165.5 1.4 fusion.38
  166.8 1.4 fusion.7
  168.2 1.4 fusion.40
  169.6 1.4 convolution_add_fusion.4
  171.0 2.3 fusion.35
  173.3 0.8 pad_maximum_fusion.1
  174.1 2.2 collective-permute-start.4
  176.8 1.0 stack.124
  177.8 1.2 fusion
  179.0 1.7 stack.125
  180.7 6.7 %collective-permute-done.4 = f32[2,2,256,128]{2,3,1,0:T(8,128)S(1)} collective-permute-done((f32[2,2,256,128]{2,3,1,0:T(8,128)}, f32[2,2,256,128]{2,3,1,0:T(8,128)S(1)}, u32[]{:S(2)}, u32[]{:S(2)}) %collective-permute-start.4) | collective-permute-done | bytes 524320 | tf_op jit(solution)/shard_map/ppermute | solution.py:15
  187.4 2.0 fusion.11
  189.4 5.0 %collective-permute-start.5 = (f32[2,2,256,128]{2,3,1,0:T(8,128)}, f32[2,2,256,128]{2,3,1,0:T(8,128)}, u32[]{:S(2)}, u32[]{:S(2)}) collective-permute-start(f32[2,2,256,128]{2,3,1,0:T(8,128)} %fusion.11), channel_id=1, source_target_pairs={{0,64},{32,96},{64,0},{96,32},{128,192},{160,224},{192,128},{224,1... | collective-permute-start | bytes 1572872 | tf_op jit(solution)/shard_map/ppermute | solution.py:15
  194.4 1.8 pad_maximum_fusion.2
  196.2 9.8 %copy.90 = f32[2,2,8,4096]{2,1,0,3:T(2,128)} copy(f32[2,2,8,4096]{3,2,1,0:T(8,128)} %pad_maximum_fusion.2) | data formatting | bytes 1048576 | tf_op jit(solution)/shard_map/stack | solution.py:38
  206.0 15.6 %reshape.308 = f32[32,1,4096]{2,1,0:T(1,128)} reshape(f32[4096,2,2,8]{3,2,1,0:T(2,128)} %bitcast.198) | data formatting | bytes 1048576
  221.6 9.3 %all-to-all-start.1 = ((f32[32,1,4096]{2,1,0:T(1,128)}), f32[32,1,4096]{2,1,0:T(1,128)}, u32[]{:S(2)}, u32[]{:S(2)}) async-start(f32[32,1,4096]{2,1,0:T(1,128)} %reshape.308), calls=%async_computation.1 | async-start | bytes 1048576 | tf_op jit(solution)/shard_map/all_to_all | solution.py:196
  230.9 1.1 multiply_subtract_fusion.11
  232.0 1.1 multiply_subtract_fusion.10
  233.1 1.4 fusion.14
  234.5 1.9 collective-permute-start.6
  237.4 1.6 copy.86
  238.9 1.0 copy.83
  239.9 2.0 copy.110
  242.0 1.2 add_negate_fusion.1
  243.7 2.9 reduce
  246.7 14.1 %reshape.309 = f32[4096,2,2,8]{3,2,1,0:T(2,128)} reshape(f32[32,4096]{1,0:T(8,128)S(1)} %reduce) | data formatting | bytes 1048576
  260.8 7.7 %copy.122 = f32[2,2,8,32,128]{4,3,2,1,0:T(8,128)} copy(f32[2,2,8,32,128]{2,1,0,4,3:T(2,128)} %bitcast.199) | data formatting | bytes 1048576 | tf_op jit(solution)/shard_map/all_to_all | solution.py:196
  268.5 12.6 %collective-permute-done.6 = f32[2,2,256,128]{2,3,1,0:T(8,128)} collective-permute-done((f32[2,2,256,128]{2,3,1,0:T(8,128)S(1)}, f32[2,2,256,128]{2,3,1,0:T(8,128)}, u32[]{:S(2)}, u32[]{:S(2)}) %collective-permute-start.6) | collective-permute-done | bytes 524320 | tf_op jit(solution)/shard_map/ppermute | solution.py:15
  281.1 1.1 multiply_subtract_fusion.8
  282.2 1.2 fusion.17
  283.4 23.1 %collective-permute-start.7 = (f32[2,2,256,128]{2,3,1,0:T(8,128)S(1)}, f32[2,2,256,128]{2,3,1,0:T(8,128)S(1)}, u32[]{:S(2)}, u32[]{:S(2)}) collective-permute-start(f32[2,2,256,128]{2,3,1,0:T(8,128)S(1)} %fusion.17), channel_id=1, source_target_pairs={{0,256},{32,288},{64,320},{96,352},{128,384},{160,416},{192,448},{... | collective-permute-start | bytes 1572872 | tf_op jit(solution)/shard_map/ppermute | solution.py:15
  306.5 1.8 fusion.276
  308.2 0.9 copy.128
  309.1 1.8 copy.97
  310.9 1.8 copy.129
  312.7 1.8 copy.93
  314.5 1.8 multiply_subtract_fusion.1
  316.3 24.0 %collective-permute-done.7 = f32[2,2,256,128]{2,3,1,0:T(8,128)S(1)} collective-permute-done((f32[2,2,256,128]{2,3,1,0:T(8,128)S(1)}, f32[2,2,256,128]{2,3,1,0:T(8,128)S(1)}, u32[]{:S(2)}, u32[]{:S(2)}) %collective-permute-start.7) | collective-permute-done | bytes 524320 | tf_op jit(solution)/shard_map/ppermute | solution.py:15
  340.5 1.9 multiply_subtract_fusion.3
  342.6 1.3 copy.111
  343.9 1.2 fusion.9
  345.1 1.1 copy.109
  (57 shorter events, 11.3 us)
Async XLA Ops:
  0.6 29.8 %copy-start.2 = (f32[3,128]{1,0:T(4,128)S(1)}, f32[3,128]{1,0:T(4,128)}, u32[]{:S(2)}) copy-start(f32[3,128]{1,0:T(4,128)} %param.13) | copy-start | bytes 4612
  0.6 29.8 %copy-start.1 = (f32[3,256]{1,0:T(4,128)S(1)}, f32[3,256]{1,0:T(4,128)}, u32[]{:S(2)}) copy-start(f32[3,256]{1,0:T(4,128)} %param.12) | copy-start | bytes 9220
  2.9 28.1 %all-to-all-start = ((f32[2,2,256,128]{3,1,0,2:T(2,128)}), f32[2,2,256,128]{3,1,0,2:T(2,128)S(1)}, u32[]{:S(2)}, u32[]{:S(2)}) async-start(f32[2,2,256,128]{3,1,0,2:T(2,128)} %copy.123), calls=%async_computation | async-start | bytes 1048576 | tf_op jit(solution)/shard_map/all_to_all | solution.py:194
  16.6 46.9 %collective-permute-start = (f32[2,2,256,128]{2,3,1,0:T(8,128)S(1)}, f32[2,2,256,128]{2,3,1,0:T(8,128)S(1)}, u32[]{:S(2)}, u32[]{:S(2)}) collective-permute-start(f32[2,2,256,128]{2,3,1,0:T(8,128)S(1)} %get-tuple-element.66), channel_id=1, source_target_pairs={{0,256},{32,288},{64,320},{96,352},{128,384},{160,416},{192,448},{... | collective-permute-start | bytes 1572872 | tf_op jit(solution)/shard_map/ppermute | solution.py:15
  63.7 55.7 %collective-permute-start.1 = (f32[2,2,256,128]{2,3,1,0:T(8,128)S(1)}, f32[2,2,256,128]{2,3,1,0:T(8,128)S(1)}, u32[]{:S(2)}, u32[]{:S(2)}) collective-permute-start(f32[2,2,256,128]{2,3,1,0:T(8,128)S(1)} %maximum_select_fusion), channel_id=1, source_target_pairs={{0,128},{32,160},{64,192},{96,224},{128,0},{160,32},{192,64},{224,... | collective-permute-start | bytes 1572872 | tf_op jit(solution)/shard_map/ppermute | solution.py:15
  119.8 27.0 %collective-permute-start.2 = (f32[2,2,256,128]{2,3,1,0:T(8,128)S(1)}, f32[2,2,256,128]{2,3,1,0:T(8,128)S(1)}, u32[]{:S(2)}, u32[]{:S(2)}) collective-permute-start(f32[2,2,256,128]{2,3,1,0:T(8,128)S(1)} %maximum_select_fusion.1), channel_id=1, source_target_pairs={{0,64},{32,96},{64,0},{96,32},{128,192},{160,224},{192,128},{224,1... | collective-permute-start | bytes 1572872 | tf_op jit(solution)/shard_map/ppermute | solution.py:15
  147.1 14.0 %collective-permute-start.3 = (f32[2,2,256,128]{2,3,1,0:T(8,128)S(1)}, f32[2,2,256,128]{2,3,1,0:T(8,128)S(1)}, u32[]{:S(2)}, u32[]{:S(2)}) collective-permute-start(f32[2,2,256,128]{2,3,1,0:T(8,128)S(1)} %maximum_select_fusion.2), channel_id=1, source_target_pairs={{0,32},{32,0},{64,96},{96,64},{128,160},{160,128},{192,224},{224,1... | collective-permute-start | bytes 1572872 | tf_op jit(solution)/shard_map/ppermute | solution.py:15
  174.1 13.3 %collective-permute-start.4 = (f32[2,2,256,128]{2,3,1,0:T(8,128)}, f32[2,2,256,128]{2,3,1,0:T(8,128)S(1)}, u32[]{:S(2)}, u32[]{:S(2)}) collective-permute-start(f32[2,2,256,128]{2,3,1,0:T(8,128)} %pad_maximum_fusion.1), channel_id=1, source_target_pairs={{0,32},{32,0},{64,96},{96,64},{128,160},{160,128},{192,224},{224,1... | collective-permute-start | bytes 1572872 | tf_op jit(solution)/shard_map/ppermute | solution.py:15
  187.4 34.2 %copy-start = (f32[1,2,256,128]{2,3,1,0:T(8,128)}, f32[1,2,256,128]{2,3,1,0:T(8,128)S(1)}, u32[]{:S(2)}) copy-start(f32[1,2,256,128]{2,3,1,0:T(8,128)S(1)} %get-tuple-element.46) | copy-start | bytes 786436
  189.4 42.6 %collective-permute-start.5 = (f32[2,2,256,128]{2,3,1,0:T(8,128)}, f32[2,2,256,128]{2,3,1,0:T(8,128)}, u32[]{:S(2)}, u32[]{:S(2)}) collective-permute-start(f32[2,2,256,128]{2,3,1,0:T(8,128)} %fusion.11), channel_id=1, source_target_pairs={{0,64},{32,96},{64,0},{96,32},{128,192},{160,224},{192,128},{224,1... | collective-permute-start | bytes 1572872 | tf_op jit(solution)/shard_map/ppermute | solution.py:15
  221.6 21.6 %all-to-all-start.1 = ((f32[32,1,4096]{2,1,0:T(1,128)}), f32[32,1,4096]{2,1,0:T(1,128)}, u32[]{:S(2)}, u32[]{:S(2)}) async-start(f32[32,1,4096]{2,1,0:T(1,128)} %reshape.308), calls=%async_computation.1 | async-start | bytes 1048576 | tf_op jit(solution)/shard_map/all_to_all | solution.py:196
  234.5 46.6 %collective-permute-start.6 = (f32[2,2,256,128]{2,3,1,0:T(8,128)S(1)}, f32[2,2,256,128]{2,3,1,0:T(8,128)}, u32[]{:S(2)}, u32[]{:S(2)}) collective-permute-start(f32[2,2,256,128]{2,3,1,0:T(8,128)S(1)} %fusion.14), channel_id=1, source_target_pairs={{0,128},{32,160},{64,192},{96,224},{128,0},{160,32},{192,64},{224,... | collective-permute-start | bytes 1572872 | tf_op jit(solution)/shard_map/ppermute | solution.py:15
  283.4 56.9 %collective-permute-start.7 = (f32[2,2,256,128]{2,3,1,0:T(8,128)S(1)}, f32[2,2,256,128]{2,3,1,0:T(8,128)S(1)}, u32[]{:S(2)}, u32[]{:S(2)}) collective-permute-start(f32[2,2,256,128]{2,3,1,0:T(8,128)S(1)} %fusion.17), channel_id=1, source_target_pairs={{0,256},{32,288},{64,320},{96,352},{128,384},{160,416},{192,448},{... | collective-permute-start | bytes 1572872 | tf_op jit(solution)/shard_map/ppermute | solution.py:15
where the time goes:
time: 348 us; the launch traced here: 346 us
  waiting for transfers between devices  152 us (44%)
  starting transfers between devices  73.9 us (21%)
  local copies, waits for them, and re-layouts  72.1 us (21%)
  other arithmetic  24.2 us (7%)
  matrix products  21.9 us (6%)
    ppermute x8, waiting for transfers between devices, from_partner(): return lax.ppermute(value, axis, pairs)  152 us
    ppermute x8, starting transfers between devices, from_partner(): return lax.ppermute(value, axis, pairs)  56.7 us
    unnamed x16, local copies, waits for them, and re-layouts  40.6 us
    dot_general x16, matrix products, along(): return jnp.einsum('km,...mb->...kb', matrix, values, precision=highest)  16.9 us
    another operation x3, local copies, waits for them, and re-layouts, complex_apply(): return jnp.stack([real_part, imag_part])  12.5 us
    all_to_all x1, starting transfers between devices, shards(): lax.all_to_all(y_lines, 'gy', split_axis=3, concat_axis=2, tiled=True)  9.29 us
    all_to_all x2, local copies, waits for them, and re-layouts, shards(): lax.all_to_all(y_lines, 'gy', split_axis=3, concat_axis=2, tiled=True)  8.17 us
    all_to_all x1, starting transfers between devices, shards(): lax.all_to_all(y_packed, 'gy', split_axis=2, concat_axis=3, tiled=True)  7.93 us
  transfers between devices with their start and end apart: 10, of which 7 were waited for; matrix products, arithmetic and copies ran while one was open for 27% of the time, Pallas kernels for 0%

commit v1 on v0

v1 whole, which is shorter than its diff:
```python
import functools
import math

import jax
import jax.numpy as jnp
import ml_dtypes
import numpy as np
from jax import lax
from jax.experimental import pallas as pl
from jax.experimental.pallas import tpu as pltpu
from jax.sharding import PartitionSpec as P

section_step = 0.25
PERIOD = 4096
BLOCKS = 16
WIDE = PERIOD // BLOCKS
RES = BLOCKS // 2 + 1
VMEM_LIMIT = 16 * 1024 * 1024


@functools.lru_cache(maxsize=None)
def circulant_blocks():
    table = np.zeros(PERIOD, np.float64)
    for n in range(1, PERIOD):
        if n != PERIOD // 2:
            sign = -1.0 if n % 2 else 1.0
            table[n] = math.pi / PERIOD * sign / math.tan(math.pi * n / PERIOD)
    row = np.arange(WIDE)
    offset = row[None, :] - row[:, None]
    return [table[(WIDE * d + offset) % PERIOD] for d in range(BLOCKS)]


def split_parts(parts):
    high = parts.astype(np.float32).astype(ml_dtypes.bfloat16)
    low = (parts - high.astype(np.float64)).astype(np.float32).astype(ml_dtypes.bfloat16)
    return np.stack([high, low], 1)


@functools.lru_cache(maxsize=None)
def residue_matrices():
    blocks = circulant_blocks()
    parts = np.zeros((RES, WIDE, 2 * WIDE), np.float64)
    for r in range(RES):
        for d in range(BLOCKS):
            turn = 2.0 * math.pi * (r * d % BLOCKS) / BLOCKS
            parts[r, :, :WIDE] += blocks[d] * (math.cos(turn) / BLOCKS)
            parts[r, :, WIDE:] -= blocks[d] * (math.sin(turn) / BLOCKS)
    return split_parts(parts)


def turned(value, turn):
    real, imag = value
    turn = turn % 1.0
    if turn == 0.0:
        return real, imag
    if turn == 0.5:
        return -real, (None if imag is None else -imag)
    if turn == 0.75:
        return imag, -real
    if turn == 0.25:
        return (None if imag is None else -imag), real
    cosine, sine = math.cos(2.0 * math.pi * turn), math.sin(2.0 * math.pi * turn)
    if imag is None:
        return real * cosine, real * sine
    return real * cosine - imag * sine, real * sine + imag * cosine


def plus(a, b):
    if b is None:
        return a
    return b if a is None else a + b


def minus(a, b):
    if b is None:
        return a
    return -b if a is None else a - b


def real_dft(values):
    count = len(values)
    if count == 2:
        return [(values[0] + values[1], None), (values[0] - values[1], None)]
    even, odd = real_dft(values[0::2]), real_dft(values[1::2])
    half, quarter = count // 2, count // 4
    result = [None] * (half + 1)
    for k in range(quarter + 1):
        spun = turned(odd[k], -k / count)
        result[k] = (plus(even[k][0], spun[0]), plus(even[k][1], spun[1]))
        mirror = (minus(even[k][0], spun[0]), minus(spun[1], even[k][1]))
        if k < quarter:
            result[half - k] = mirror
    return result


def real_inverse(spectrum):
    count = 2 * (len(spectrum) - 1)
    half, quarter = count // 2, count // 4
    if count == 2:
        return [spectrum[0][0] + spectrum[1][0], spectrum[0][0] - spectrum[1][0]]
    evens, odds = [], []
    for r in range(quarter + 1):
        low, high = spectrum[r], spectrum[half - r]
        total = (plus(low[0], high[0]), minus(low[1], high[1]))
        differ = (minus(low[0], high[0]), plus(low[1], high[1]))
        evens.append(total)
        odds.append(turned(differ, r / count))
    result = [None] * count
    result[0::2] = real_inverse(evens)
    result[1::2] = real_inverse(odds)
    return result


def forward_part(read, spectra, group, half):
    rows, lanes = pl.ds(16 * group, 16), pl.ds(128 * half, 128)
    residues = real_dft([read(p, rows, half) for p in range(BLOCKS)])
    for r, (real, imag) in enumerate(residues):
        for place, part in enumerate((real, imag)):
            if part is None:
                part = jnp.zeros_like(real)
            high = part.astype(jnp.bfloat16)
            low = (part - high.astype(jnp.float32)).astype(jnp.bfloat16)
            spectra[r, pl.ds(32 * place + 16 * group, 16), lanes] = high
            spectra[r, pl.ds(64 + 32 * place + 16 * group, 16), lanes] = low


def multiply_part(r, spectra, matrix, products):
    lines = spectra[r]
    main = jnp.dot(lines, matrix[r, 0], preferred_element_type=jnp.float32)
    rest = jnp.dot(lines[:64], matrix[r, 1], preferred_element_type=jnp.float32)
    both = main[:64] + main[64:] + rest
    products[r, 0] = both[:32, :WIDE] - both[32:, WIDE:]
    products[r, 1] = both[:32, WIDE:] + both[32:, :WIDE]


def inverse_part(write, products, group, half):
    rows, lanes = pl.ds(16 * group, 16), pl.ds(128 * half, 128)
    spectrum = []
    for r in range(RES):
        real = products[r, 0, rows, lanes]
        imag = None if r in (0, RES - 1) else products[r, 1, rows, lanes]
        spectrum.append((real, imag))
    for p, value in enumerate(real_inverse(spectrum)):
        write(p, rows, half, value)


def x_lines_kernel(lines_ref, after_ref, matrix_ref, out_ref, matrix, spectra, products, arrived):
    copies = [pltpu.make_async_copy(matrix_ref.at[r], matrix.at[r], arrived.at[r]) for r in range(RES)]
    for copy in copies:
        copy.start()

    def read(p, rows, h):
        return lines_ref[p, rows, pl.ds(128 * h, 128)]

    def write(p, rows, h, value):
        out_ref[p, rows, pl.ds(128 * h, 128)] = value

    parts = [(group, half) for group in range(2) for half in range(2)]
    for part in parts:
        forward_part(read, spectra, *part)
    for r, copy in enumerate(copies):
        copy.wait()
        multiply_part(r, spectra, matrix, products)
    for part in parts:
        inverse_part(write, products, *part)


@functools.lru_cache(maxsize=None)
def ring_matrices():
    blocks = circulant_blocks()
    parts = np.zeros((7, WIDE, 4 * WIDE), np.float64)
    for place, shift in enumerate((0, 1, 2, 3, -3, -2, -1)):
        for d in range(4):
            block = blocks[(4 * d + shift) % BLOCKS] / 4.0
            parts[place, :, :WIDE] += block
            parts[place, :, WIDE : 2 * WIDE] += block * (1 - 2 * (d % 2))
            parts[place, :, 2 * WIDE : 3 * WIDE] += 2.0 * block * (1, 0, -1, 0)[d]
            parts[place, :, 3 * WIDE :] -= 2.0 * block * (0, 1, 0, -1)[d]
    return split_parts(parts)


def y_lines_kernel(
    coords_ref, p0, p1, p2, p3, after_ref, matrix_ref, o0, o1, o2, o3, matrix, lines, sums, arrived
):
    copies = []
    for k in range(4):
        which = jnp.where(coords_ref[1] >= k, k, k + 3)
        copies.append(pltpu.make_async_copy(matrix_ref.at[which], matrix.at[k], arrived.at[k]))
    for copy in copies:
        copy.start()

    for k, piece in enumerate((p0, p1, p2, p3)):
        slot = k % 2
        for group in range(8):
            at = pl.ds(16 * group, 16)
            w0, w1, w2, w3 = (piece[i, at, :] for i in (0, 3, 2, 1))
            values = (w0 + w2 + (w1 + w3), w0 + w2 - (w1 + w3), w0 - w2, w3 - w1)
            for value, offset, gap in zip(values, (0, 256, 512, 640), (128, 128, 256, 256)):
                high = value.astype(jnp.bfloat16)
                lines[slot, pl.ds(offset + 16 * group, 16), :] = high
                low = (value - high.astype(jnp.float32)).astype(jnp.bfloat16)
                lines[slot, pl.ds(offset + gap + 16 * group, 16), :] = low
        copies[k].wait()

        def product(offset, count, columns):
            main = jnp.dot(
                lines[slot, offset : offset + 2 * count, :],
                matrix[k, 0, :, columns],
                preferred_element_type=jnp.float32,
            )
            rest = jnp.dot(
                lines[slot, offset : offset + count, :],
                matrix[k, 1, :, columns],
                preferred_element_type=jnp.float32,
            )
            return main[:count] + main[count:] + rest

        both = product(512, 256, slice(2 * WIDE, 4 * WIDE))
        terms = (
            product(0, 128, slice(0, WIDE)),
            product(256, 128, slice(WIDE, 2 * WIDE)),
            both[:128, :WIDE] - both[128:, WIDE:],
            both[:128, WIDE:] + both[128:, :WIDE],
        )
        if k == 0:
            for i, term in enumerate(terms):
                sums[i] = term
        elif k < 3:
            for i, term in enumerate(terms):
                sums[i] += term
        else:
            z0, z2, real, imag = (sums[i] + term for i, term in enumerate(terms))
            o0[...] = z0 + z2 + real
            o1[...] = z0 - z2 - imag
            o2[...] = z0 + z2 - real
            o3[...] = z0 - z2 + imag


def whole(shape):
    return pl.BlockSpec(shape, lambda *_: (0,) * len(shape))


def any_place():
    return pl.BlockSpec(memory_space=pl.ANY)


def in_hbm():
    return pl.BlockSpec(memory_space=pltpu.HBM)


def in_vmem():
    return pl.BlockSpec(memory_space=pltpu.VMEM)


def x_lines(lines, after, matrices):
    return pl.pallas_call(
        x_lines_kernel,
        in_specs=[in_vmem(), any_place(), in_hbm()],
        out_specs=in_vmem(),
        out_shape=jax.ShapeDtypeStruct((BLOCKS, 32, WIDE), jnp.float32),
        scratch_shapes=[
            pltpu.VMEM((RES, 2, WIDE, 2 * WIDE), jnp.bfloat16),
            pltpu.VMEM((RES, 128, WIDE), jnp.bfloat16),
            pltpu.VMEM((RES, 2, 32, WIDE), jnp.float32),
            pltpu.SemaphoreType.DMA((RES,)),
        ],
        cost_estimate=pl.CostEstimate(flops=900_000_000, bytes_accessed=1_000_000, transcendentals=0),
        compiler_params=pltpu.CompilerParams(vmem_limit_bytes=VMEM_LIMIT),
        name="x_lines",
    )(lines, after, matrices)


def y_lines(coords, pieces, after, matrices):
    quarter = jax.ShapeDtypeStruct((128, WIDE), jnp.float32)
    return pl.pallas_call(
        y_lines_kernel,
        in_specs=[pl.BlockSpec(memory_space=pltpu.SMEM)] + [in_vmem()] * 4 + [any_place(), in_hbm()],
        out_specs=[in_vmem()] * 4,
        out_shape=[quarter] * 4,
        scratch_shapes=[
            pltpu.VMEM((4, 2, WIDE, 4 * WIDE), jnp.bfloat16),
            pltpu.VMEM((2, 1024, WIDE), jnp.bfloat16),
            pltpu.VMEM((4, 128, WIDE), jnp.float32),
            pltpu.SemaphoreType.DMA((4,)),
        ],
        cost_estimate=pl.CostEstimate(flops=100_000_000_000, bytes_accessed=7_000_000, transcendentals=0),
        compiler_params=pltpu.CompilerParams(vmem_limit_bytes=VMEM_LIMIT),
        name="y_lines",
    )(coords, *pieces, after, matrices)


def pack_kernel(coords_ref, field_ref, x_ref, own_ref, sent_ref):
    core = coords_ref[2]
    own_rows = pl.ds(pl.multiple_of(core * 128, 128), 128)
    sent_rows = pl.ds(pl.multiple_of(128 - core * 128, 128), 128)
    for i in range(4):
        x_ref[:, 8 * i : 8 * i + 8, :] = field_ref[i // 2 * 2, i % 2].T.reshape(16, 8, 256)
        own_ref[i // 2, i % 2] = field_ref[i // 2, i % 2, own_rows, :]
        sent_ref[i // 2, i % 2] = field_ref[i // 2, i % 2, sent_rows, :]


def pack(coords, fields):
    half = jax.ShapeDtypeStruct((2, 2, 128, 128), jnp.float32)
    return pl.pallas_call(
        pack_kernel,
        in_specs=[pl.BlockSpec(memory_space=pltpu.SMEM), in_vmem()],
        out_specs=[in_vmem()] * 3,
        out_shape=[jax.ShapeDtypeStruct((16, 32, 256), jnp.float32), half, half],
        cost_estimate=pl.CostEstimate(flops=0, bytes_accessed=2_000_000, transcendentals=0),
        compiler_params=pltpu.CompilerParams(vmem_limit_bytes=VMEM_LIMIT),
        name="pack",
    )(coords, fields)


def y_pack_kernel(coords_ref, own_ref, other_ref, *out_refs):
    own_y, core = coords_ref[0], coords_ref[2]
    here = pl.ds(pl.multiple_of(core * 128, 128), 128)
    there = pl.ds(pl.multiple_of(128 - core * 128, 128), 128)
    for j in range(4):
        rows = pl.ds(pl.multiple_of(((own_y + j) & 3) * 32, 32), 32)
        for i in range(4):
            out_refs[j][32 * i : 32 * i + 32, here] = own_ref[i // 2, i % 2, rows, :]
            out_refs[j][32 * i : 32 * i + 32, there] = other_ref[i // 2, i % 2, rows, :]


def y_pack(coords, own, other):
    quarter = jax.ShapeDtypeStruct((128, WIDE), jnp.float32)
    return pl.pallas_call(
        y_pack_kernel,
        in_specs=[pl.BlockSpec(memory_space=pltpu.SMEM), in_vmem(), in_vmem()],
        out_specs=[in_vmem()] * 4,
        out_shape=[quarter] * 4,
        cost_estimate=pl.CostEstimate(flops=0, bytes_accessed=1_000_000, transcendentals=0),
        compiler_params=pltpu.CompilerParams(vmem_limit_bytes=VMEM_LIMIT),
        name="y_pack",
    )(coords, own, other)


def shifted(value, axis, distance):
    pairs = []
    for i in range(32):
        at = [i // 8, i // 2 % 4, i % 2]
        at[axis] = (at[axis] + distance) % 4
        pairs.append((i, at[0] * 8 + at[1] * 2 + at[2]))
    return lax.ppermute(value, "gy", pairs)


def other_core(value):
    return lax.ppermute(value, "gy", [(i, i ^ 1) for i in range(32)])


def ring_swap(quarters):
    moved = {j: shifted(quarters[j], 0, j) for j in (1, 3, 2)}
    return [quarters[0]] + [moved[j] for j in (1, 2, 3)]


def ring_gather(held):
    moved = {j: shifted(held, 1, j) for j in (1, 3, 2)}
    return [held] + [moved[j] for j in (1, 2, 3)]


def advance_kernel(
    coords_ref, fields, poles, stretch, inverse_eps, rates, x_prof, y_prof, x_deriv, q0, q1, q2, q3, other,
    next_fields, next_poles, next_stretch, y_deriv
):
    part, plane = pl.program_id(0), pl.program_id(1)
    own_y, core = coords_ref[0], coords_ref[2]

    @pl.when((part == 0) & (plane == 0))
    def _():
        lanes = pl.ds(pl.multiple_of(core * 128, 128), 128)
        for j, quarter in enumerate((q0, q1, q2, q3)):
            start = ((own_y - j) & 3) * 32
            own_rows = pl.ds(pl.multiple_of(core * 128 + start, 32), 32)
            other_rows = pl.ds(pl.multiple_of(128 - core * 128 + start, 32), 32)
            for i in range(4):
                y_deriv[i, own_rows, :] = quarter[32 * i : 32 * i + 32, lanes]
                y_deriv[i, other_rows, :] = other[j, 32 * i : 32 * i + 32, :]

    here = pl.ds(pl.multiple_of(part * 128, 128), 128)
    ez_dx = x_deriv[:, 0, 0].reshape(128, 128).T
    hy_dx = x_deriv[:, 1, 0].reshape(128, 128).T
    ez_dy = y_deriv[plane, here, :]
    hx_dy = y_deriv[2 + plane, here, :]
    conduct_x, stretch_x, shift_x = x_prof[:, 0:1], x_prof[:, 1:2], x_prof[:, 2:3]
    conduct_y, stretch_y, shift_y = y_prof[0:1, :], y_prof[1:2, :], y_prof[2:3, :]
    over_x, over_y = 1.0 / stretch_x, 1.0 / stretch_y
    decay_x = conduct_x / stretch_x + shift_x
    decay_y = conduct_y / stretch_y + shift_y
    feed_x = conduct_x / (stretch_x * stretch_x)
    feed_y = conduct_y / (stretch_y * stretch_y)
    s0, s1, s2, s3 = (stretch[i, 0] for i in range(4))
    ez_x_term = ez_dx * over_x + s0
    hy_x_term = hy_dx * over_x + s1
    ez_y_term = ez_dy * over_y + s2
    hx_y_term = hx_dy * over_y + s3
    next_stretch[0, 0] = s0 - section_step * (decay_x * s0 + feed_x * ez_dx)
    next_stretch[1, 0] = s1 - section_step * (decay_x * s1 + feed_x * hy_dx)
    next_stretch[2, 0] = s2 - section_step * (decay_y * s2 + feed_y * ez_dy)
    next_stretch[3, 0] = s3 - section_step * (decay_y * s3 + feed_y * hx_dy)
    polar, current = poles[0, 0], poles[1, 0]
    ez = fields[0, 0]
    next_fields[0, 0] = ez + section_step * (inverse_eps[...] * (hy_x_term - hx_y_term - current))
    next_fields[1, 0] = fields[1, 0] - section_step * ez_y_term
    next_fields[2, 0] = fields[2, 0] + section_step * ez_x_term
    damping, resonance, plasma = (rates[i].astype(jnp.float32) for i in range(3))
    next_poles[0, 0] = polar + section_step * current
    next_poles[1, 0] = current + section_step * (plasma * ez - damping * current - resonance * polar)


def advance(coords, fields, pole_state, stretch_state, inverse_permittivity, pole_rates, x_profile, y_profile, x_deriv, quarters, other):
    def state(count):
        return pl.BlockSpec((count, 1, 128, 128), lambda i, j, *_: (0, j, i, 0))

    return pl.pallas_call(
        advance_kernel,
        grid_spec=pltpu.PrefetchScalarGridSpec(
            num_scalar_prefetch=1,
            grid=(2, 2),
            in_specs=[
                state(3),
                state(2),
                state(4),
                pl.BlockSpec((128, 128), lambda i, j, *_: (i, 0)),
                pl.BlockSpec((3, 128, 128), lambda i, j, *_: (0, i, 0)),
                pl.BlockSpec((128, 3), lambda i, j, *_: (i, 0)),
                whole((3, 128)),
                pl.BlockSpec((16, 2, 1, 8, 128), lambda i, j, *_: (0, 0, j, 0, i)),
            ]
            + [whole((128, WIDE))] * 4
            + [whole((4, 128, 128))],
            out_specs=[state(3), state(2), state(4)],
            scratch_shapes=[pltpu.VMEM((4, 256, 128), jnp.float32)],
        ),
        out_shape=[
            jax.ShapeDtypeStruct((count, 2, 256, 128), jnp.float32) for count in (3, 2, 4)
        ],
        cost_estimate=pl.CostEstimate(flops=3_000_000, bytes_accessed=6_000_000, transcendentals=0),
        compiler_params=pltpu.CompilerParams(vmem_limit_bytes=VMEM_LIMIT),
        name="advance",
    )(coords, fields, pole_state, stretch_state, inverse_permittivity, pole_rates, x_profile.T, y_profile,
        x_deriv.reshape(16, 2, 2, 8, 256), *quarters, other)


def swap_x(lines):
    return lax.all_to_all(lines, "gx", split_axis=0, concat_axis=0, tiled=True)


def y_return(coords, quarters):
    quarters = ring_swap(quarters)
    core = coords[2]
    sent = jnp.stack([lax.dynamic_slice_in_dim(q, 128 - core * 128, 128, 1) for q in quarters])
    return quarters, other_core(sent)


def place():
    me = lax.axis_index("gy").astype(jnp.int32)
    return jnp.stack([me // 8, me // 2 % 4, me % 2])


def shards(fields, pole_state, stretch_state, inverse_permittivity, pole_rates, x_profile, y_profile):
    coords = place()
    x_mats, y_mats = jnp.asarray(residue_matrices()), jnp.asarray(ring_matrices())
    x_packed, own, sent = pack(coords, fields)
    x_sorted = swap_x(x_packed)
    y_held = jnp.stack(ring_swap(y_pack(coords, own, other_core(sent))))
    y_pieces = ring_gather(y_held)
    x_lined = x_lines(x_sorted, y_held, x_mats)
    x_deriv = swap_x(x_lined)
    quarters, other = y_return(coords, y_lines(coords, y_pieces, x_lined, y_mats))
    return tuple(
        advance(
            coords, fields, pole_state, stretch_state, inverse_permittivity, pole_rates, x_profile, y_profile,
            x_deriv, quarters, other,
        )
    )


def solution(mesh):
    return jax.shard_map(
        shards,
        mesh=mesh,
        in_specs=(
            P(None, None, "gx", "gy"),
            P(None, None, "gx", "gy"),
            P(None, None, "gx", "gy"),
            P("gx", "gy"),
            P(None, "gx", "gy"),
            P(None, "gx"),
            P(None, "gy"),
        ),
        out_specs=(P(None, None, "gx", "gy"), P(None, None, "gx", "gy"), P(None, None, "gx", "gy")),
        check_vma=False,
    )
```

time: 348 us -> 106 us (0.30)
  the two profiles are of different devices: /device:TPU:99 before, /device:TPU:1 now
where the time goes in v1:
time: 106 us; the launch traced here: 105 us
  starting transfers between devices  65.2 us (62%)
  Pallas kernels  14.8 us (14%)
  waiting for transfers between devices  13.1 us (12%)
  local copies, waits for them, and re-layouts  9.88 us (9%)
    ppermute x9, starting transfers between devices, shifted(): return lax.ppermute(value, 'gy', pairs)  31 us
    all_to_all x2, starting transfers between devices, swap_x(): return lax.all_to_all(lines, 'gx', split_axis=0, concat_axis=0, tiled=True)  27.5 us
    ppermute x9, waiting for transfers between devices, shifted(): return lax.ppermute(value, 'gy', pairs)  10.7 us
    unnamed x25, local copies, waits for them, and re-layouts  9.84 us
    ppermute x2, starting transfers between devices, other_core(): return lax.ppermute(value, 'gy', [(i, i ^ 1) for i in range(32)])  6.73 us
    pallas_call x1, Pallas kernels, y_lines(): pl.pallas_call(y_lines_kernel, in_specs=[pl.BlockSpec(memory_space=pltpu....  4.72 us
    pallas_call x1, Pallas kernels, advance(): pl.pallas_call(advance_kernel, grid_spec=pltpu.PrefetchScalarGridSpec(num...  4.19 us
    pallas_call x1, Pallas kernels, x_lines(): pl.pallas_call(x_lines_kernel, in_specs=[in_vmem(), any_place(), in_hbm()...  3.81 us
  transfers between devices with their start and end apart: 13, of which 7 were waited for; matrix products, arithmetic and copies ran while one was open for 1% of the time, Pallas kernels for 9%

profile of v1, /device:TPU:1, one launch (start us, length us, event | category | flops | bytes accessed | tf_op | source)
XLA Modules:
  0.0 104.8 jit_solution(11756179876372896743)
XLA Ops:
  0.7 0.1 pad_add_fusion.coords_ref
  0.7 0.0 copy-start.1
  0.7 1.1 %copy-done.1 = f32[3,2,256,128]{3,2,1,0:T(8,128)S(1)} copy-done((f32[3,2,256,128]{3,2,1,0:T(8,128)S(1)}, f32[3,2,256,128]{3,2,1,0:T(8,128)}, u32[]{:S(2)}) %copy-start.1) | copy-done | bytes 786456
  1.9 1.5 %pack.1 = (f32[16,32,256]{2,1,0:T(8,128)}, f32[2,2,128,128]{3,2,1,0:T(8,128)S(1)}, f32[2,2,128,128]{3,2,1,0:T(8,128)S(1)}) custom-call(s32[3]{0:T(128)S(1)} %pad_add_fusion.coords_ref, f32[3,2,256,128]{3,2,1,0:T(8,128)S(1)} %copy-done.1), custom_call_target="tpu_custom_call" | custom-call | bytes 2000000 | tf_op jit(solution)/shard_map/pack/pallas_call | solution.py:304
  3.4 15.7 %all-to-all-start = ((f32[16,32,256]{2,1,0:T(8,128)}), f32[16,32,256]{2,1,0:T(8,128)S(1)}, u32[]{:S(2)}, u32[]{:S(2)}) async-start(f32[16,32,256]{2,1,0:T(8,128)} %get-tuple-element.14), calls=%async_computation | async-start | bytes 1048576 | tf_op jit(solution)/shard_map/all_to_all | solution.py:446
  19.2 2.9 %collective-permute-start = (f32[2,2,128,128]{3,2,1,0:T(8,128)S(1)}, f32[2,2,128,128]{3,2,1,0:T(8,128)S(1)}, u32[]{:S(2)}, u32[]{:S(2)}) collective-permute-start(f32[2,2,128,128]{3,2,1,0:T(8,128)S(1)} %get-tuple-element.16), channel_id=1, source_target_pairs={{0,1},{1,0},{2,3},{3,2},{4,5},{5,4},{6,7},{7,6},{8,9},{9,8},{10,11... | collective-permute-start | bytes 786440 | tf_op jit(solution)/shard_map/ppermute | solution.py:349
  22.0 1.1 %collective-permute-done.other_ref = f32[2,2,128,128]{3,2,1,0:T(8,128)S(1)} collective-permute-done((f32[2,2,128,128]{3,2,1,0:T(8,128)S(1)}, f32[2,2,128,128]{3,2,1,0:T(8,128)S(1)}, u32[]{:S(2)}, u32[]{:S(2)}) %collective-permute-start) | collective-permute-done | bytes 262176 | tf_op jit(solution)/shard_map/ppermute | solution.py:349
  23.2 0.6 y_pack.1
  23.8 3.2 %collective-permute-start.1 = (f32[128,256]{1,0:T(8,128)S(1)}, f32[128,256]{1,0:T(8,128)S(1)}, u32[]{:S(2)}, u32[]{:S(2)}) collective-permute-start(f32[128,256]{1,0:T(8,128)S(1)} %get-tuple-element.18), channel_id=1, source_target_pairs={{0,8},{1,9},{2,10},{3,11},{4,12},{5,13},{6,14},{7,15},{8,16},{9,17... | collective-permute-start | bytes 393224 | tf_op jit(solution)/shard_map/ppermute | solution.py:345
  27.0 4.5 %collective-permute-start.2 = (f32[128,256]{1,0:T(8,128)S(1)}, f32[128,256]{1,0:T(8,128)S(1)}, u32[]{:S(2)}, u32[]{:S(2)}) collective-permute-start(f32[128,256]{1,0:T(8,128)S(1)} %get-tuple-element.19), channel_id=1, source_target_pairs={{0,16},{1,17},{2,18},{3,19},{4,20},{5,21},{6,22},{7,23},{8,24},{9,... | collective-permute-start | bytes 393224 | tf_op jit(solution)/shard_map/ppermute | solution.py:345
  31.5 3.0 %collective-permute-start.3 = (f32[128,256]{1,0:T(8,128)S(1)}, f32[128,256]{1,0:T(8,128)S(1)}, u32[]{:S(2)}, u32[]{:S(2)}) collective-permute-start(f32[128,256]{1,0:T(8,128)S(1)} %get-tuple-element.20), channel_id=1, source_target_pairs={{0,24},{1,25},{2,26},{3,27},{4,28},{5,29},{6,30},{7,31},{8,0},{9,1... | collective-permute-start | bytes 393224 | tf_op jit(solution)/shard_map/ppermute | solution.py:345
  34.5 0.0 collective-permute-done.1
  34.5 1.3 %collective-permute-done.2 = f32[128,256]{1,0:T(8,128)S(1)} collective-permute-done((f32[128,256]{1,0:T(8,128)S(1)}, f32[128,256]{1,0:T(8,128)S(1)}, u32[]{:S(2)}, u32[]{:S(2)}) %collective-permute-start.2) | collective-permute-done | bytes 131104 | tf_op jit(solution)/shard_map/ppermute | solution.py:345
  35.9 1.7 %collective-permute-done.3 = f32[128,256]{1,0:T(8,128)S(1)} collective-permute-done((f32[128,256]{1,0:T(8,128)S(1)}, f32[128,256]{1,0:T(8,128)S(1)}, u32[]{:S(2)}, u32[]{:S(2)}) %collective-permute-start.3) | collective-permute-done | bytes 131104 | tf_op jit(solution)/shard_map/ppermute | solution.py:345
  37.6 3.1 %collective-permute-start.4 = (f32[4,128,256]{2,1,0:T(8,128)S(1)}, f32[4,128,256]{2,1,0:T(8,128)}, u32[]{:S(2)}, u32[]{:S(2)}) collective-permute-start(f32[4,128,256]{2,1,0:T(8,128)S(1)} %pad_maximum_fusion.after_ref.p0), channel_id=1, source_target_pairs={{0,2},{1,3},{2,4},{3,5},{4,6},{5,7},{6,0},{7,1},{8,10},{9,11},{10,... | collective-permute-start | bytes 1572872 | tf_op jit(solution)/shard_map/ppermute | solution.py:345
  40.7 4.4 %collective-permute-start.5 = (f32[4,128,256]{2,1,0:T(8,128)S(1)}, f32[4,128,256]{2,1,0:T(8,128)}, u32[]{:S(2)}, u32[]{:S(2)}) collective-permute-start(f32[4,128,256]{2,1,0:T(8,128)S(1)} %pad_maximum_fusion.after_ref.p0), channel_id=1, source_target_pairs={{0,4},{1,5},{2,6},{3,7},{4,0},{5,1},{6,2},{7,3},{8,12},{9,13},{10,... | collective-permute-start | bytes 1572872 | tf_op jit(solution)/shard_map/ppermute | solution.py:345
  45.1 3.1 %collective-permute-start.6 = (f32[4,128,256]{2,1,0:T(8,128)S(1)}, f32[4,128,256]{2,1,0:T(8,128)}, u32[]{:S(2)}, u32[]{:S(2)}) collective-permute-start(f32[4,128,256]{2,1,0:T(8,128)S(1)} %pad_maximum_fusion.after_ref.p0), channel_id=1, source_target_pairs={{0,6},{1,7},{2,0},{3,1},{4,2},{5,3},{6,4},{7,5},{8,14},{9,15},{10,... | collective-permute-start | bytes 1572872 | tf_op jit(solution)/shard_map/ppermute | solution.py:345
  48.1 0.0 all-to-all-done.lines_ref
  48.1 0.0 copy-start
  48.2 2.3 %copy-done = bf16[9,2,256,512]{3,2,1,0:T(8,128)(2,1)S(1)} copy-done((bf16[9,2,256,512]{3,2,1,0:T(8,128)(2,1)S(1)}, bf16[9,2,256,512]{3,2,1,0:T(8,128)(2,1)}, u32[]{:S(2)}) %copy-start) | copy-done | bytes 4718616
  50.5 3.8 %x_lines.1.after_ref = f32[16,32,256]{2,1,0:T(8,128)} custom-call(f32[16,32,256]{2,1,0:T(8,128)S(1)} %all-to-all-done.lines_ref, f32[4,128,256]{2,1,0:T(8,128)S(1)} %pad_maximum_fusion.after_ref.p0, bf16[9,2,256,512]{3,2,1,0:T(8,128)(2,1)S(1)} %copy-done), custom_call_target="tpu_custom_call" | custom-call | flops 900000000 | bytes 1000000 | tf_op jit(solution)/shard_map/x_lines/pallas_call | solution.py:256
  54.3 0.0 copy-start.11
  54.3 11.7 %all-to-all-start.1 = ((f32[16,32,256]{2,1,0:T(8,128)}), f32[16,32,256]{2,1,0:T(8,128)S(1)}, u32[]{:S(2)}, u32[]{:S(2)}) async-start(f32[16,32,256]{2,1,0:T(8,128)} %x_lines.1.after_ref), calls=%async_computation.1 | async-start | bytes 1048576 | tf_op jit(solution)/shard_map/all_to_all | solution.py:446
  66.1 0.0 copy-start.2
  66.1 0.0 copy-start.3
  66.1 0.0 copy-start.4
  66.1 0.0 copy-start.7
  66.1 0.0 collective-permute-done.4.p1
  66.1 0.0 collective-permute-done.5.p2
  66.1 1.1 %collective-permute-done.6.p3 = f32[4,128,256]{2,1,0:T(8,128)} collective-permute-done((f32[4,128,256]{2,1,0:T(8,128)S(1)}, f32[4,128,256]{2,1,0:T(8,128)}, u32[]{:S(2)}, u32[]{:S(2)}) %collective-permute-start.6) | collective-permute-done | bytes 524320 | tf_op jit(solution)/shard_map/ppermute | solution.py:345
  67.2 0.0 copy-start.10
  67.2 3.1 %copy-done.10 = bf16[7,2,256,1024]{3,2,1,0:T(8,128)(2,1)S(1)} copy-done((bf16[7,2,256,1024]{3,2,1,0:T(8,128)(2,1)S(1)}, bf16[7,2,256,1024]{3,2,1,0:T(8,128)(2,1)}, u32[]{:S(2)}) %copy-start.10) | copy-done | bytes 7340056
  70.3 4.7 %y_lines.1 = (f32[128,256]{1,0:T(8,128)S(1)}, f32[128,256]{1,0:T(8,128)S(1)}, f32[128,256]{1,0:T(8,128)S(1)}, f32[128,256]{1,0:T(8,128)}) custom-call(s32[3]{0:T(128)S(1)} %pad_add_fusion.coords_ref, f32[4,128,256]{2,1,0:T(8,128)S(1)} %pad_maximum_fusion.after_ref.p0, f32[4,128,256]{2,1,0:T(8,128)} %collective-permute-done.4.p1, ...), custom_call_target="tpu_custom_call" | custom-call | flops 99999997952 | bytes 7000000 | tf_op jit(solution)/shard_map/y_lines/pallas_call | solution.py:275
  75.0 0.0 copy-start.8
  75.1 0.6 copy-done.8
  75.7 0.0 copy-start.9
  75.7 0.6 copy-done.9
  76.4 4.2 %collective-permute-start.9 = (f32[128,256]{1,0:T(8,128)}, f32[128,256]{1,0:T(8,128)S(1)}, u32[]{:S(2)}, u32[]{:S(2)}) collective-permute-start(f32[128,256]{1,0:T(8,128)} %get-tuple-element.24), channel_id=1, source_target_pairs={{0,24},{1,25},{2,26},{3,27},{4,28},{5,29},{6,30},{7,31},{8,0},{9,1... | collective-permute-start | bytes 393224 | tf_op jit(solution)/shard_map/ppermute | solution.py:345
  80.5 3.6 %collective-permute-start.8 = (f32[128,256]{1,0:T(8,128)}, f32[128,256]{1,0:T(8,128)S(1)}, u32[]{:S(2)}, u32[]{:S(2)}) collective-permute-start(f32[128,256]{1,0:T(8,128)} %copy-done.9), channel_id=1, source_target_pairs={{0,16},{1,17},{2,18},{3,19},{4,20},{5,21},{6,22},{7,23},{8,24},{9,... | collective-permute-start | bytes 393224 | tf_op jit(solution)/shard_map/ppermute | solution.py:345
  84.2 1.9 %collective-permute-start.7 = (f32[128,256]{1,0:T(8,128)}, f32[128,256]{1,0:T(8,128)S(1)}, u32[]{:S(2)}, u32[]{:S(2)}) collective-permute-start(f32[128,256]{1,0:T(8,128)} %copy-done.8), channel_id=1, source_target_pairs={{0,8},{1,9},{2,10},{3,11},{4,12},{5,13},{6,14},{7,15},{8,16},{9,17... | collective-permute-start | bytes 393224 | tf_op jit(solution)/shard_map/ppermute | solution.py:345
  86.1 0.0 collective-permute-done.9.q3
  86.1 2.1 %collective-permute-done.8.q2 = f32[128,256]{1,0:T(8,128)S(1)} collective-permute-done((f32[128,256]{1,0:T(8,128)}, f32[128,256]{1,0:T(8,128)S(1)}, u32[]{:S(2)}, u32[]{:S(2)}) %collective-permute-start.8) | collective-permute-done | bytes 131104 | tf_op jit(solution)/shard_map/ppermute | solution.py:345
  88.3 4.4 %collective-permute-done.7.q1 = f32[128,256]{1,0:T(8,128)S(1)} collective-permute-done((f32[128,256]{1,0:T(8,128)}, f32[128,256]{1,0:T(8,128)S(1)}, u32[]{:S(2)}, u32[]{:S(2)}) %collective-permute-start.7) | collective-permute-done | bytes 131104 | tf_op jit(solution)/shard_map/ppermute | solution.py:345
  92.7 0.7 pad_maximum_fusion.1
  93.4 3.9 %collective-permute-start.10 = (f32[4,128,128]{2,1,0:T(8,128)}, f32[4,128,128]{2,1,0:T(8,128)}, u32[]{:S(2)}, u32[]{:S(2)}) collective-permute-start(f32[4,128,128]{2,1,0:T(8,128)} %pad_maximum_fusion.1), channel_id=1, source_target_pairs={{0,1},{1,0},{2,3},{3,2},{4,5},{5,4},{6,7},{7,6},{8,9},{9,8},{10,11... | collective-permute-start | bytes 786440 | tf_op jit(solution)/shard_map/ppermute | solution.py:349
  97.3 0.0 copy-done.11
  97.3 0.1 copy.12
  97.4 1.3 %collective-permute-done.10.other = f32[4,128,128]{2,1,0:T(8,128)} collective-permute-done((f32[4,128,128]{2,1,0:T(8,128)}, f32[4,128,128]{2,1,0:T(8,128)}, u32[]{:S(2)}, u32[]{:S(2)}) %collective-permute-start.10) | collective-permute-done | bytes 262176 | tf_op jit(solution)/shard_map/ppermute | solution.py:349
  98.8 0.0 all-to-all-done.1
  98.8 0.0 copy-done.2
  98.8 0.0 copy-done.3
  98.8 0.0 copy-done.4
  98.8 0.0 copy-done.7
  98.8 0.0 copy-start.5
  98.8 0.9 copy-done.5
  99.7 0.0 copy-start.6
  99.7 0.9 copy-done.6
  100.6 4.2 %advance.1 = (f32[3,2,256,128]{3,2,1,0:T(8,128)}, f32[2,2,256,128]{3,2,1,0:T(8,128)}, f32[4,2,256,128]{3,2,1,0:T(8,128)}) custom-call(s32[3]{0:T(128)S(1)} %pad_add_fusion.coords_ref, f32[3,2,256,128]{3,2,1,0:T(8,128)S(1)} %copy-done.2, f32[2,2,256,128]{3,2,1,0:T(8,128)S(1)} %copy-done.4, f32[4,2,256,128]{3,2,1,0:T(8,128)S(1)} %copy-done.3, ...), custom_call_target="tpu_custom_call" | custom-call | flops 3000000 | bytes 6000000 | tf_op jit(solution)/shard_map/advance/pallas_call | solution.py:415
  (5 shorter events, 0.1 us)
Async XLA Ops:
  0.7 1.1 %copy-start.1 = (f32[3,2,256,128]{3,2,1,0:T(8,128)S(1)}, f32[3,2,256,128]{3,2,1,0:T(8,128)}, u32[]{:S(2)}) copy-start(f32[3,2,256,128]{3,2,1,0:T(8,128)} %fields.1) | copy-start | bytes 2359300
  3.4 44.7 %all-to-all-start = ((f32[16,32,256]{2,1,0:T(8,128)}), f32[16,32,256]{2,1,0:T(8,128)S(1)}, u32[]{:S(2)}, u32[]{:S(2)}) async-start(f32[16,32,256]{2,1,0:T(8,128)} %get-tuple-element.14), calls=%async_computation | async-start | bytes 1048576 | tf_op jit(solution)/shard_map/all_to_all | solution.py:446
  19.2 4.0 %collective-permute-start = (f32[2,2,128,128]{3,2,1,0:T(8,128)S(1)}, f32[2,2,128,128]{3,2,1,0:T(8,128)S(1)}, u32[]{:S(2)}, u32[]{:S(2)}) collective-permute-start(f32[2,2,128,128]{3,2,1,0:T(8,128)S(1)} %get-tuple-element.16), channel_id=1, source_target_pairs={{0,1},{1,0},{2,3},{3,2},{4,5},{5,4},{6,7},{7,6},{8,9},{9,8},{10,11... | collective-permute-start | bytes 786440 | tf_op jit(solution)/shard_map/ppermute | solution.py:349
  23.8 10.7 %collective-permute-start.1 = (f32[128,256]{1,0:T(8,128)S(1)}, f32[128,256]{1,0:T(8,128)S(1)}, u32[]{:S(2)}, u32[]{:S(2)}) collective-permute-start(f32[128,256]{1,0:T(8,128)S(1)} %get-tuple-element.18), channel_id=1, source_target_pairs={{0,8},{1,9},{2,10},{3,11},{4,12},{5,13},{6,14},{7,15},{8,16},{9,17... | collective-permute-start | bytes 393224 | tf_op jit(solution)/shard_map/ppermute | solution.py:345
  27.0 8.9 %collective-permute-start.2 = (f32[128,256]{1,0:T(8,128)S(1)}, f32[128,256]{1,0:T(8,128)S(1)}, u32[]{:S(2)}, u32[]{:S(2)}) collective-permute-start(f32[128,256]{1,0:T(8,128)S(1)} %get-tuple-element.19), channel_id=1, source_target_pairs={{0,16},{1,17},{2,18},{3,19},{4,20},{5,21},{6,22},{7,23},{8,24},{9,... | collective-permute-start | bytes 393224 | tf_op jit(solution)/shard_map/ppermute | solution.py:345
  31.5 6.0 %collective-permute-start.3 = (f32[128,256]{1,0:T(8,128)S(1)}, f32[128,256]{1,0:T(8,128)S(1)}, u32[]{:S(2)}, u32[]{:S(2)}) collective-permute-start(f32[128,256]{1,0:T(8,128)S(1)} %get-tuple-element.20), channel_id=1, source_target_pairs={{0,24},{1,25},{2,26},{3,27},{4,28},{5,29},{6,30},{7,31},{8,0},{9,1... | collective-permute-start | bytes 393224 | tf_op jit(solution)/shard_map/ppermute | solution.py:345
  37.6 28.5 %collective-permute-start.4 = (f32[4,128,256]{2,1,0:T(8,128)S(1)}, f32[4,128,256]{2,1,0:T(8,128)}, u32[]{:S(2)}, u32[]{:S(2)}) collective-permute-start(f32[4,128,256]{2,1,0:T(8,128)S(1)} %pad_maximum_fusion.after_ref.p0), channel_id=1, source_target_pairs={{0,2},{1,3},{2,4},{3,5},{4,6},{5,7},{6,0},{7,1},{8,10},{9,11},{10,... | collective-permute-start | bytes 1572872 | tf_op jit(solution)/shard_map/ppermute | solution.py:345
  40.7 25.4 %collective-permute-start.5 = (f32[4,128,256]{2,1,0:T(8,128)S(1)}, f32[4,128,256]{2,1,0:T(8,128)}, u32[]{:S(2)}, u32[]{:S(2)}) collective-permute-start(f32[4,128,256]{2,1,0:T(8,128)S(1)} %pad_maximum_fusion.after_ref.p0), channel_id=1, source_target_pairs={{0,4},{1,5},{2,6},{3,7},{4,0},{5,1},{6,2},{7,3},{8,12},{9,13},{10,... | collective-permute-start | bytes 1572872 | tf_op jit(solution)/shard_map/ppermute | solution.py:345
  45.1 22.2 %collective-permute-start.6 = (f32[4,128,256]{2,1,0:T(8,128)S(1)}, f32[4,128,256]{2,1,0:T(8,128)}, u32[]{:S(2)}, u32[]{:S(2)}) collective-permute-start(f32[4,128,256]{2,1,0:T(8,128)S(1)} %pad_maximum_fusion.after_ref.p0), channel_id=1, source_target_pairs={{0,6},{1,7},{2,0},{3,1},{4,2},{5,3},{6,4},{7,5},{8,14},{9,15},{10,... | collective-permute-start | bytes 1572872 | tf_op jit(solution)/shard_map/ppermute | solution.py:345
  48.1 2.3 %copy-start = (bf16[9,2,256,512]{3,2,1,0:T(8,128)(2,1)S(1)}, bf16[9,2,256,512]{3,2,1,0:T(8,128)(2,1)}, u32[]{:S(2)}) copy-start(bf16[9,2,256,512]{3,2,1,0:T(8,128)(2,1)} %constant.58.clone.matrix_ref) | copy-start | bytes 14155780
  54.3 43.0 %copy-start.11 = (f32[3,256]{1,0:T(4,128)S(1)}, f32[3,256]{1,0:T(4,128)}, u32[]{:S(2)}) copy-start(f32[3,256]{1,0:T(4,128)} %param.14) | copy-start | bytes 9220
  54.3 44.5 %all-to-all-start.1 = ((f32[16,32,256]{2,1,0:T(8,128)}), f32[16,32,256]{2,1,0:T(8,128)S(1)}, u32[]{:S(2)}, u32[]{:S(2)}) async-start(f32[16,32,256]{2,1,0:T(8,128)} %x_lines.1.after_ref), calls=%async_computation.1 | async-start | bytes 1048576 | tf_op jit(solution)/shard_map/all_to_all | solution.py:446
  66.1 32.7 %copy-start.2 = (f32[3,2,256,128]{3,2,1,0:T(8,128)S(1)}, f32[3,2,256,128]{3,2,1,0:T(8,128)}, u32[]{:S(2)}) copy-start(f32[3,2,256,128]{3,2,1,0:T(8,128)} %fields.1) | copy-start | bytes 2359300
  66.1 32.7 %copy-start.3 = (f32[4,2,256,128]{3,2,1,0:T(8,128)S(1)}, f32[4,2,256,128]{3,2,1,0:T(8,128)}, u32[]{:S(2)}) copy-start(f32[4,2,256,128]{3,2,1,0:T(8,128)} %stretch.1) | copy-start | bytes 3145732
  66.1 32.7 %copy-start.4 = (f32[2,2,256,128]{3,2,1,0:T(8,128)S(1)}, f32[2,2,256,128]{3,2,1,0:T(8,128)}, u32[]{:S(2)}) copy-start(f32[2,2,256,128]{3,2,1,0:T(8,128)} %poles.1) | copy-start | bytes 1572868
  66.1 32.7 %copy-start.7 = (f32[3,128]{1,0:T(4,128)S(1)}, f32[3,128]{1,0:T(4,128)}, u32[]{:S(2)}) copy-start(f32[3,128]{1,0:T(4,128)} %y_prof.1) | copy-start | bytes 4612
  67.2 3.1 %copy-start.10 = (bf16[7,2,256,1024]{3,2,1,0:T(8,128)(2,1)S(1)}, bf16[7,2,256,1024]{3,2,1,0:T(8,128)(2,1)}, u32[]{:S(2)}) copy-start(bf16[7,2,256,1024]{3,2,1,0:T(8,128)(2,1)} %constant.59.clone.matrix_ref) | copy-start | bytes 22020100
  75.0 0.7 copy-start.8
  75.7 0.6 copy-start.9
  76.4 9.8 %collective-permute-start.9 = (f32[128,256]{1,0:T(8,128)}, f32[128,256]{1,0:T(8,128)S(1)}, u32[]{:S(2)}, u32[]{:S(2)}) collective-permute-start(f32[128,256]{1,0:T(8,128)} %get-tuple-element.24), channel_id=1, source_target_pairs={{0,24},{1,25},{2,26},{3,27},{4,28},{5,29},{6,30},{7,31},{8,0},{9,1... | collective-permute-start | bytes 393224 | tf_op jit(solution)/shard_map/ppermute | solution.py:345
  80.5 7.7 %collective-permute-start.8 = (f32[128,256]{1,0:T(8,128)}, f32[128,256]{1,0:T(8,128)S(1)}, u32[]{:S(2)}, u32[]{:S(2)}) collective-permute-start(f32[128,256]{1,0:T(8,128)} %copy-done.9), channel_id=1, source_target_pairs={{0,16},{1,17},{2,18},{3,19},{4,20},{5,21},{6,22},{7,23},{8,24},{9,... | collective-permute-start | bytes 393224 | tf_op jit(solution)/shard_map/ppermute | solution.py:345
  84.2 8.5 %collective-permute-start.7 = (f32[128,256]{1,0:T(8,128)}, f32[128,256]{1,0:T(8,128)S(1)}, u32[]{:S(2)}, u32[]{:S(2)}) collective-permute-start(f32[128,256]{1,0:T(8,128)} %copy-done.8), channel_id=1, source_target_pairs={{0,8},{1,9},{2,10},{3,11},{4,12},{5,13},{6,14},{7,15},{8,16},{9,17... | collective-permute-start | bytes 393224 | tf_op jit(solution)/shard_map/ppermute | solution.py:345
  93.4 5.4 %collective-permute-start.10 = (f32[4,128,128]{2,1,0:T(8,128)}, f32[4,128,128]{2,1,0:T(8,128)}, u32[]{:S(2)}, u32[]{:S(2)}) collective-permute-start(f32[4,128,128]{2,1,0:T(8,128)} %pad_maximum_fusion.1), channel_id=1, source_target_pairs={{0,1},{1,0},{2,3},{3,2},{4,5},{5,4},{6,7},{7,6},{8,9},{9,8},{10,11... | collective-permute-start | bytes 786440 | tf_op jit(solution)/shard_map/ppermute | solution.py:349
  98.8 0.9 copy-start.5
  99.7 0.9 copy-start.6

commit v2 on v1

v2 whole, which is shorter than its diff:
```python
import functools
import math

import jax
import jax.numpy as jnp
import ml_dtypes
import numpy as np
from jax import lax
from jax.experimental import pallas as pl
from jax.experimental.pallas import tpu as pltpu
from jax.sharding import PartitionSpec as P

section_step = 0.25
PERIOD = 4096
BLOCKS = 16
WIDE = PERIOD // BLOCKS
RES = BLOCKS // 2 + 1
VMEM_LIMIT = 16 * 1024 * 1024
VMEM_MOST = 49 * 1024 * 1024


@functools.lru_cache(maxsize=None)
def circulant_blocks():
    table = np.zeros(PERIOD, np.float64)
    for n in range(1, PERIOD):
        if n != PERIOD // 2:
            sign = -1.0 if n % 2 else 1.0
            table[n] = math.pi / PERIOD * sign / math.tan(math.pi * n / PERIOD)
    row = np.arange(WIDE)
    offset = row[None, :] - row[:, None]
    return [table[(WIDE * d + offset) % PERIOD] for d in range(BLOCKS)]


def split_parts(parts):
    high = parts.astype(np.float32).astype(ml_dtypes.bfloat16)
    low = (parts - high.astype(np.float64)).astype(np.float32).astype(ml_dtypes.bfloat16)
    return np.stack([high, low], 1)


@functools.lru_cache(maxsize=None)
def residue_tables():
    dft = np.zeros((1, WIDE, 2 * WIDE), np.float64)
    cosines = [math.cos(2.0 * math.pi * n / WIDE) for n in range(WIDE)]
    sines = [math.sin(2.0 * math.pi * n / WIDE) for n in range(WIDE)]
    row = np.arange(WIDE)
    product = row[:, None] * row[None, :] % WIDE
    dft[0, :, :WIDE] = np.array(cosines)[product]
    dft[0, :, WIDE:] = -np.array(sines)[product]
    vectors = np.zeros((3, RES, WIDE), np.float64)
    for r in range(RES):
        for m in range(WIDE):
            turn = 2.0 * math.pi * (r * m) / PERIOD
            vectors[0, r, m], vectors[1, r, m] = math.cos(turn), math.sin(turn)
            freq = r + BLOCKS * m
            signed = freq if freq < PERIOD // 2 else freq - PERIOD
            if freq != PERIOD // 2:
                vectors[2, r, m] = 2.0 * math.pi * signed / PERIOD / PERIOD
    return split_parts(dft)[0], vectors.astype(np.float32)


def turned(value, turn):
    real, imag = value
    turn = turn % 1.0
    if turn == 0.0:
        return real, imag
    if turn == 0.5:
        return -real, (None if imag is None else -imag)
    if turn == 0.75:
        return imag, -real
    if turn == 0.25:
        return (None if imag is None else -imag), real
    cosine, sine = math.cos(2.0 * math.pi * turn), math.sin(2.0 * math.pi * turn)
    if imag is None:
        return real * cosine, real * sine
    return real * cosine - imag * sine, real * sine + imag * cosine


def plus(a, b):
    if b is None:
        return a
    return b if a is None else a + b


def minus(a, b):
    if b is None:
        return a
    return -b if a is None else a - b


def real_dft(values):
    count = len(values)
    if count == 2:
        return [(values[0] + values[1], None), (values[0] - values[1], None)]
    even, odd = real_dft(values[0::2]), real_dft(values[1::2])
    half, quarter = count // 2, count // 4
    result = [None] * (half + 1)
    for k in range(quarter + 1):
        spun = turned(odd[k], -k / count)
        result[k] = (plus(even[k][0], spun[0]), plus(even[k][1], spun[1]))
        mirror = (minus(even[k][0], spun[0]), minus(spun[1], even[k][1]))
        if k < quarter:
            result[half - k] = mirror
    return result


def real_inverse(spectrum):
    count = 2 * (len(spectrum) - 1)
    half, quarter = count // 2, count // 4
    if count == 2:
        return [spectrum[0][0] + spectrum[1][0], spectrum[0][0] - spectrum[1][0]]
    evens, odds = [], []
    for r in range(quarter + 1):
        low, high = spectrum[r], spectrum[half - r]
        total = (plus(low[0], high[0]), minus(low[1], high[1]))
        differ = (minus(low[0], high[0]), plus(low[1], high[1]))
        evens.append(total)
        odds.append(turned(differ, r / count))
    result = [None] * count
    result[0::2] = real_inverse(evens)
    result[1::2] = real_inverse(odds)
    return result


def store_split(target, first, second, value):
    high = value.astype(jnp.bfloat16)
    target[first] = high
    target[second] = (value - high.astype(jnp.float32)).astype(jnp.bfloat16)


def wide_product(lines, matrix):
    half = lines.shape[0] // 2
    main = jnp.dot(lines[...], matrix[0], preferred_element_type=jnp.float32)
    rest = jnp.dot(lines[:half], matrix[1], preferred_element_type=jnp.float32)
    both = main[:half] + main[half:] + rest
    quarter = half // 2
    return both[:quarter, :WIDE], both[:quarter, WIDE:], both[quarter:, :WIDE], both[quarter:, WIDE:]


def residue_part(some, residues, lines, matrix, vectors):
    def put(i, place, value):
        store_split(
            lines, pl.ds(96 * place + 32 * i, 32), pl.ds(192 + 96 * place + 32 * i, 32), value
        )

    for i, r in enumerate(some):
        cosine, sine = vectors[0, r : r + 1], vectors[1, r : r + 1]
        real, imag = residues[r, 0], residues[r, 1]
        put(i, 0, real * cosine + imag * sine)
        put(i, 1, imag * cosine - real * sine)
    rc, rs, ic, is_ = wide_product(lines, matrix)
    real, imag = rc - is_, rs + ic
    for i, r in enumerate(some):
        wave, at = vectors[2, r : r + 1], slice(32 * i, 32 * i + 32)
        put(i, 0, -wave * imag[at])
        put(i, 1, wave * real[at])
    rc, rs, ic, is_ = wide_product(lines, matrix)
    real, imag = rc + is_, ic - rs
    for i, r in enumerate(some):
        cosine, sine = vectors[0, r : r + 1], vectors[1, r : r + 1]
        at = slice(32 * i, 32 * i + 32)
        residues[r, 0] = real[at] * cosine - imag[at] * sine
        residues[r, 1] = real[at] * sine + imag[at] * cosine


def x_lines_kernel(lines_ref, after_ref, matrix, vectors, out_ref, work, residues, lines, arrived, sent):
    parts = [(pl.ds(16 * g, 16), pl.ds(128 * h, 128)) for g in range(2) for h in range(2)]
    incoming, outgoing = [], []
    for i, (rows, lanes) in enumerate(parts):
        here = (slice(None), rows, lanes)
        incoming.append(pltpu.make_async_copy(lines_ref.at[here], work.at[here], arrived.at[i]))
        outgoing.append(pltpu.make_async_copy(work.at[here], out_ref.at[here], sent.at[i]))
        incoming[-1].start()
    for copy, (rows, lanes) in zip(incoming, parts):
        copy.wait()
        for r, (real, imag) in enumerate(real_dft([work[p, rows, lanes] for p in range(BLOCKS)])):
            residues[r, 0, rows, lanes] = real
            residues[r, 1, rows, lanes] = jnp.zeros_like(real) if imag is None else imag
    for first in range(0, RES, 3):
        residue_part(range(first, first + 3), residues, lines, matrix, vectors)
    for copy, (rows, lanes) in zip(outgoing, parts):
        spectrum = []
        for r in range(RES):
            imag = None if r in (0, RES - 1) else residues[r, 1, rows, lanes]
            spectrum.append((residues[r, 0, rows, lanes], imag))
        for p, value in enumerate(real_inverse(spectrum)):
            work[p, rows, lanes] = value
        copy.start()
    for copy in outgoing:
        copy.wait()


@functools.lru_cache(maxsize=None)
def ring_matrices():
    blocks = circulant_blocks()
    parts = np.zeros((16, WIDE, 4 * WIDE), np.float64)
    for own in range(4):
        for k in range(4):
            place = 4 * own + k
            for d in range(4):
                block = blocks[(4 * d + own - (own - k) % 4) % BLOCKS] / 4.0
                parts[place, :, :WIDE] += block
                parts[place, :, WIDE : 2 * WIDE] += block * (1 - 2 * (d % 2))
                parts[place, :, 2 * WIDE : 3 * WIDE] += 2.0 * block * (1, 0, -1, 0)[d]
                parts[place, :, 3 * WIDE :] -= 2.0 * block * (0, 1, 0, -1)[d]
    return split_parts(parts)


def y_lines_kernel(me_ref, p0, p1, p2, p3, after_ref, matrix_ref, o0, o1, o2, o3, matrix, lines, sums, arrived):
    first = 4 * ((me_ref[0] >> 1) & 3)
    copies = [pltpu.make_async_copy(matrix_ref.at[first + k], matrix.at[k], arrived.at[k]) for k in range(4)]
    for copy in copies:
        copy.start()

    for k, piece in enumerate((p0, p1, p2, p3)):
        slot = k % 2
        for group in range(8):
            at = pl.ds(16 * group, 16)
            w0, w1, w2, w3 = (piece[i, at, :] for i in (0, 3, 2, 1))
            values = (w0 + w2 + (w1 + w3), w0 + w2 - (w1 + w3), w0 - w2, w3 - w1)
            for value, offset, gap in zip(values, (0, 256, 512, 640), (128, 128, 256, 256)):
                high = value.astype(jnp.bfloat16)
                lines[slot, pl.ds(offset + 16 * group, 16), :] = high
                low = (value - high.astype(jnp.float32)).astype(jnp.bfloat16)
                lines[slot, pl.ds(offset + gap + 16 * group, 16), :] = low
        copies[k].wait()

        def product(offset, count, columns):
            main = jnp.dot(
                lines[slot, offset : offset + 2 * count, :],
                matrix[k, 0, :, columns],
                preferred_element_type=jnp.float32,
            )
            rest = jnp.dot(
                lines[slot, offset : offset + count, :],
                matrix[k, 1, :, columns],
                preferred_element_type=jnp.float32,
            )
            return main[:count] + main[count:] + rest

        both = product(512, 256, slice(2 * WIDE, 4 * WIDE))
        terms = (
            product(0, 128, slice(0, WIDE)),
            product(256, 128, slice(WIDE, 2 * WIDE)),
            both[:128, :WIDE] - both[128:, WIDE:],
            both[:128, WIDE:] + both[128:, :WIDE],
        )
        if k == 0:
            for i, term in enumerate(terms):
                sums[i] = term
        elif k < 3:
            for i, term in enumerate(terms):
                sums[i] += term
        else:
            z0, z2, real, imag = (sums[i] + term for i, term in enumerate(terms))
            o0[...] = z0 + z2 + real
            o1[...] = z0 - z2 - imag
            o2[...] = z0 + z2 - real
            o3[...] = z0 - z2 + imag


def whole(shape):
    return pl.BlockSpec(shape, lambda *_: (0,) * len(shape))


def any_place():
    return pl.BlockSpec(memory_space=pl.ANY)


def in_hbm():
    return pl.BlockSpec(memory_space=pltpu.HBM)


def in_vmem():
    return pl.BlockSpec(memory_space=pltpu.VMEM)


def in_smem():
    return pl.BlockSpec(memory_space=pltpu.SMEM)


def x_lines(lines, after):
    matrix, vectors = residue_tables()
    return pl.pallas_call(
        x_lines_kernel,
        in_specs=[any_place(), any_place(), in_vmem(), in_vmem()],
        out_specs=any_place(),
        out_shape=jax.ShapeDtypeStruct((BLOCKS, 32, WIDE), jnp.float32),
        scratch_shapes=[
            pltpu.VMEM((BLOCKS, 32, WIDE), jnp.float32),
            pltpu.VMEM((RES, 2, 32, WIDE), jnp.float32),
            pltpu.VMEM((384, WIDE), jnp.bfloat16),
            pltpu.SemaphoreType.DMA((4,)),
            pltpu.SemaphoreType.DMA((4,)),
        ],
        cost_estimate=pl.CostEstimate(flops=900_000_000, bytes_accessed=1_000_000, transcendentals=0),
        compiler_params=pltpu.CompilerParams(vmem_limit_bytes=VMEM_LIMIT),
        name="x_lines",
    )(lines, after, jnp.asarray(matrix), jnp.asarray(vectors))


def y_lines(me, pieces, after):
    quarter = jax.ShapeDtypeStruct((128, WIDE), jnp.float32)
    return pl.pallas_call(
        y_lines_kernel,
        in_specs=[in_smem()] + [in_vmem()] * 4 + [any_place(), in_hbm()],
        out_specs=[in_vmem()] * 4,
        out_shape=[quarter] * 4,
        scratch_shapes=[
            pltpu.VMEM((4, 2, WIDE, 4 * WIDE), jnp.bfloat16),
            pltpu.VMEM((2, 1024, WIDE), jnp.bfloat16),
            pltpu.VMEM((4, 128, WIDE), jnp.float32),
            pltpu.SemaphoreType.DMA((4,)),
        ],
        cost_estimate=pl.CostEstimate(flops=100_000_000_000, bytes_accessed=7_000_000, transcendentals=0),
        compiler_params=pltpu.CompilerParams(vmem_limit_bytes=VMEM_MOST),
        name="y_lines",
    )(me, *pieces, after, jnp.asarray(ring_matrices()))


def pack_kernel(me_ref, fields, x_ref, own_ref, sent_ref, lines, arrived):
    core = me_ref[0] & 1
    own_rows = pl.ds(pl.multiple_of(core * 128, 128), 128)
    sent_rows = pl.ds(pl.multiple_of(128 - core * 128, 128), 128)
    copies = []
    for i in range(4):
        at = (slice(None), pl.ds(8 * i, 8))
        lines[at] = fields[i // 2 * 2, i % 2].T.reshape(16, 8, 256)
        copies.append(pltpu.make_async_copy(lines.at[at], x_ref.at[at], arrived.at[i]))
        copies[-1].start()
    for i in range(4):
        own_ref[i // 2, i % 2] = fields[i // 2, i % 2, own_rows, :]
        sent_ref[i // 2, i % 2] = fields[i // 2, i % 2, sent_rows, :]
    for copy in copies:
        copy.wait()


def pack(me, fields):
    half = jax.ShapeDtypeStruct((2, 2, 128, 128), jnp.float32)
    return pl.pallas_call(
        pack_kernel,
        in_specs=[in_smem(), in_vmem()],
        out_specs=[any_place(), in_vmem(), in_vmem()],
        out_shape=[jax.ShapeDtypeStruct((16, 32, 256), jnp.float32), half, half],
        scratch_shapes=[pltpu.VMEM((16, 32, 256), jnp.float32), pltpu.SemaphoreType.DMA((4,))],
        cost_estimate=pl.CostEstimate(flops=0, bytes_accessed=2_000_000, transcendentals=0),
        compiler_params=pltpu.CompilerParams(vmem_limit_bytes=VMEM_LIMIT),
        name="pack",
    )(me, fields)


def y_pack_kernel(me_ref, own_ref, other_ref, *out_refs):
    own_y, core = me_ref[0] >> 3, me_ref[0] & 1
    here = pl.ds(pl.multiple_of(core * 128, 128), 128)
    there = pl.ds(pl.multiple_of(128 - core * 128, 128), 128)
    for j in range(4):
        rows = pl.ds(pl.multiple_of(((own_y + j) & 3) * 32, 32), 32)
        for i in range(4):
            out_refs[j][32 * i : 32 * i + 32, here] = own_ref[i // 2, i % 2, rows, :]
            out_refs[j][32 * i : 32 * i + 32, there] = other_ref[i // 2, i % 2, rows, :]


def y_pack(me, own, other):
    quarter = jax.ShapeDtypeStruct((128, WIDE), jnp.float32)
    return pl.pallas_call(
        y_pack_kernel,
        in_specs=[in_smem(), in_vmem(), in_vmem()],
        out_specs=[in_vmem()] * 4,
        out_shape=[quarter] * 4,
        cost_estimate=pl.CostEstimate(flops=100_000_000_000, bytes_accessed=1_000_000, transcendentals=0),
        compiler_params=pltpu.CompilerParams(vmem_limit_bytes=VMEM_LIMIT),
        name="y_pack",
    )(me, own, other)


def shifted(value, axis, distance):
    pairs = []
    for i in range(32):
        at = [i // 8, i // 2 % 4, i % 2]
        at[axis] = (at[axis] + distance) % 4
        pairs.append((i, at[0] * 8 + at[1] * 2 + at[2]))
    return lax.ppermute(value, "gy", pairs)


def other_core(value):
    return lax.ppermute(value, "gy", [(i, i ^ 1) for i in range(32)])


def ring_swap(quarters):
    moved = {j: shifted(quarters[j], 0, j) for j in (1, 3, 2)}
    return [quarters[0]] + [moved[j] for j in (1, 2, 3)]


def ring_gather(held):
    moved = {j: shifted(held, 1, j) for j in (1, 3, 2)}
    return [held] + [moved[j] for j in (1, 2, 3)]


def base_kernel(
    fields_ref, poles_ref, stretch_ref, eps_ref, rates_ref, x_prof, y_prof, after_ref,
    next_poles, base, scale, vectors, fields, poles, stretch, inverse_eps, rates, out, arrived, sent
):
    pairs = [(poles_ref, poles), (rates_ref, rates), (fields_ref, fields), (eps_ref, inverse_eps), (stretch_ref, stretch)]
    copies = [pltpu.make_async_copy(a, b, arrived.at[k]) for k, (a, b) in enumerate(pairs)]
    for copy in copies:
        copy.start()
    conduct_x, stretch_x, shift_x = x_prof[0:1, :], x_prof[1:2, :], x_prof[2:3, :]
    conduct_y, stretch_y, shift_y = y_prof[0:1, :], y_prof[1:2, :], y_prof[2:3, :]
    decay_y = conduct_y / stretch_y + shift_y

    def down(row):
        return jnp.broadcast_to(row, (128, 256)).T

    decay_x = down(conduct_x / stretch_x + shift_x)
    vectors[0:1, :] = 1.0 / stretch_x
    vectors[1:2, :] = section_step * conduct_x / (stretch_x * stretch_x)
    vectors[2:3, 0:128] = 1.0 / stretch_y
    vectors[3:4, 0:128] = section_step * conduct_y / (stretch_y * stretch_y)
    for copy in copies[:3]:
        copy.wait()
    for plane in range(2):
        polar, current, ez = poles[0, plane], poles[1, plane], fields[0, plane]
        damping, resonance, plasma = (rates[i].astype(jnp.float32) for i in range(3))
        out[0, plane] = polar + section_step * current
        out[1, plane] = current + section_step * (plasma * ez - damping * current - resonance * polar)
    result = pltpu.make_async_copy(out, next_poles, sent)
    result.start()
    for copy in copies[3:]:
        copy.wait()
    eps = section_step * inverse_eps[...]
    scale[...] = eps
    for plane in range(2):
        s0, s1, s2, s3 = (stretch[i, plane] for i in range(4))
        base[0, plane] = fields[0, plane] + eps * (s1 - s3 - poles[1, plane])
        base[1, plane] = fields[1, plane] - section_step * s2
        base[2, plane] = fields[2, plane] + section_step * s0
        base[3, plane] = s0 - section_step * (decay_x * s0)
        base[4, plane] = s1 - section_step * (decay_x * s1)
        base[5, plane] = s2 - section_step * (decay_y * s2)
        base[6, plane] = s3 - section_step * (decay_y * s3)
    result.wait()


def base_part(fields, pole_state, stretch_state, inverse_permittivity, pole_rates, x_profile, y_profile, after):
    return pl.pallas_call(
        base_kernel,
        in_specs=[any_place()] * 5 + [in_vmem()] * 2 + [any_place()],
        out_specs=[in_hbm(), in_vmem(), in_vmem(), in_vmem()],
        out_shape=[
            jax.ShapeDtypeStruct((2, 2, 256, 128), jnp.float32),
            jax.ShapeDtypeStruct((7, 2, 256, 128), jnp.float32),
            jax.ShapeDtypeStruct((256, 128), jnp.float32),
            jax.ShapeDtypeStruct((8, 256), jnp.float32),
        ],
        scratch_shapes=[
            pltpu.VMEM((3, 2, 256, 128), jnp.float32),
            pltpu.VMEM((2, 2, 256, 128), jnp.float32),
            pltpu.VMEM((4, 2, 256, 128), jnp.float32),
            pltpu.VMEM((256, 128), jnp.float32),
            pltpu.VMEM((3, 256, 128), jnp.bfloat16),
            pltpu.VMEM((2, 2, 256, 128), jnp.float32),
            pltpu.SemaphoreType.DMA((5,)),
            pltpu.SemaphoreType.DMA,
        ],
        cost_estimate=pl.CostEstimate(flops=3_000_000, bytes_accessed=5_000_000, transcendentals=0),
        compiler_params=pltpu.CompilerParams(vmem_limit_bytes=VMEM_LIMIT),
        name="base",
    )(fields, pole_state, stretch_state, inverse_permittivity, pole_rates, x_profile, y_profile, after)


def finish_kernel(
    me_ref, base, scale, vectors, x_deriv, q0, q1, q2, q3, other, next_fields, next_stretch, y_deriv, fields, stretch, sent
):
    own_y, core = me_ref[0] >> 3, me_ref[0] & 1
    lanes = pl.ds(pl.multiple_of(core * 128, 128), 128)
    for j, quarter in enumerate((q0, q1, q2, q3)):
        start = ((own_y - j) & 3) * 32
        own_rows = pl.ds(pl.multiple_of(core * 128 + start, 32), 32)
        other_rows = pl.ds(pl.multiple_of(128 - core * 128 + start, 32), 32)
        for i in range(4):
            y_deriv[i, own_rows, :] = quarter[32 * i : 32 * i + 32, lanes]
            y_deriv[i, other_rows, :] = other[j, 32 * i : 32 * i + 32, :]
    over_y, feed_y = vectors[2:3, 0:128], vectors[3:4, 0:128]
    over_x, feed_x = (jnp.broadcast_to(vectors[i : i + 1, :], (128, 256)).T for i in range(2))
    eps = scale[...]
    copies = []

    def send(source, target):
        copy = pltpu.make_async_copy(source, target, sent.at[len(copies)])
        copy.start()
        copies.append(copy)

    for plane in range(2):
        ez_dy, hx_dy = y_deriv[plane], y_deriv[2 + plane]
        stretch[2, plane] = base[5, plane] - feed_y * ez_dy
        stretch[3, plane] = base[6, plane] - feed_y * hx_dy
        fields[1, plane] = base[1, plane] - section_step * (over_y * ez_dy)
        send(stretch.at[pl.ds(2, 2), plane], next_stretch.at[pl.ds(2, 2), plane])
        send(fields.at[1, plane], next_fields.at[1, plane])
    for plane in range(2):
        ez_dx = x_deriv[:, 8 * plane : 8 * plane + 8, :].reshape(128, 256).T
        hy_dx = x_deriv[:, 16 + 8 * plane : 24 + 8 * plane, :].reshape(128, 256).T
        stretch[0, plane] = base[3, plane] - feed_x * ez_dx
        stretch[1, plane] = base[4, plane] - feed_x * hy_dx
        fields[2, plane] = base[2, plane] + section_step * (over_x * ez_dx)
        fields[0, plane] = base[0, plane] + eps * (over_x * hy_dx - over_y * y_deriv[2 + plane])
        send(stretch.at[pl.ds(0, 2), plane], next_stretch.at[pl.ds(0, 2), plane])
        send(fields.at[2, plane], next_fields.at[2, plane])
        send(fields.at[0, plane], next_fields.at[0, plane])
    for copy in copies:
        copy.wait()


def finish(me, base, scale, vectors, x_deriv, quarters, other):
    return pl.pallas_call(
        finish_kernel,
        in_specs=[in_smem()] + [in_vmem()] * 9,
        out_specs=[in_hbm()] * 2,
        out_shape=[jax.ShapeDtypeStruct((count, 2, 256, 128), jnp.float32) for count in (3, 4)],
        scratch_shapes=[
            pltpu.VMEM((4, 256, 128), jnp.float32),
            pltpu.VMEM((3, 2, 256, 128), jnp.float32),
            pltpu.VMEM((4, 2, 256, 128), jnp.float32),
            pltpu.SemaphoreType.DMA((10,)),
        ],
        cost_estimate=pl.CostEstimate(flops=3_000_000, bytes_accessed=5_000_000, transcendentals=0),
        compiler_params=pltpu.CompilerParams(vmem_limit_bytes=VMEM_LIMIT),
        name="finish",
    )(me, base, scale, vectors, x_deriv, *quarters, other)


def swap_x(lines):
    return lax.all_to_all(lines, "gx", split_axis=0, concat_axis=0, tiled=True)


def split_kernel(me_ref, q0, q1, q2, q3, after_ref, sent_ref):
    lanes = pl.ds(pl.multiple_of(128 - (me_ref[0] & 1) * 128, 128), 128)
    for j, quarter in enumerate((q0, q1, q2, q3)):
        sent_ref[j] = quarter[:, lanes]


def split(me, quarters, after):
    return pl.pallas_call(
        split_kernel,
        in_specs=[in_smem()] + [in_vmem()] * 4 + [any_place()],
        out_specs=in_vmem(),
        out_shape=jax.ShapeDtypeStruct((4, 128, 128), jnp.float32),
        cost_estimate=pl.CostEstimate(flops=0, bytes_accessed=500_000, transcendentals=0),
        compiler_params=pltpu.CompilerParams(vmem_limit_bytes=VMEM_LIMIT),
        name="split",
    )(me, *quarters, after)


def shards(fields, pole_state, stretch_state, inverse_permittivity, pole_rates, x_profile, y_profile):
    me = lax.axis_index("gy").astype(jnp.int32).reshape(1)
    x_packed, own, sent = pack(me, fields)
    x_sorted = swap_x(x_packed)
    y_packed = y_pack(me, own, other_core(sent))
    y_held = jnp.stack(ring_swap(y_packed))
    y_pieces = ring_gather(y_held)
    x_lined = x_lines(x_sorted, y_held)
    x_deriv = swap_x(x_lined)
    y_lined = y_lines(me, y_pieces, x_lined)
    next_poles, base, scale, vectors = base_part(
        fields, pole_state, stretch_state, inverse_permittivity, pole_rates, x_profile, y_profile, y_lined[0]
    )
    quarters = ring_swap(y_lined)
    other = other_core(split(me, quarters, vectors))
    next_fields, next_stretch = finish(me, base, scale, vectors, x_deriv, quarters, other)
    return next_fields, next_poles, next_stretch


def solution(mesh):
    return jax.shard_map(
        shards,
        mesh=mesh,
        in_specs=(
            P(None, None, "gx", "gy"),
            P(None, None, "gx", "gy"),
            P(None, None, "gx", "gy"),
            P("gx", "gy"),
            P(None, "gx", "gy"),
            P(None, "gx"),
            P(None, "gy"),
        ),
        out_specs=(P(None, None, "gx", "gy"), P(None, None, "gx", "gy"), P(None, None, "gx", "gy")),
        check_vma=False,
    )
```

time: 106 us -> 92 us (0.87)
  local copies, waits for them, and re-layouts: 9.88 us -> 1.19 us
  Pallas kernels: 14.8 us -> 10.2 us
  waiting for transfers between devices: 13.1 us -> 14.9 us
  starting transfers between devices: 65.2 us -> 64.1 us
    unnamed x25 -> x20, local copies, waits for them, and re-layouts: 9.84 us -> 1.19 us
    all_to_all x2, starting transfers between devices: 27.5 us -> 21 us  [swap_x(): return lax.all_to_all(lines, 'gx', split_axis=0, concat_axis=0, tiled=True)]
    ppermute x2, starting transfers between devices: 6.73 us -> 12.6 us  [other_core(): return lax.ppermute(value, 'gy', [(i, i ^ 1) for i in range(32)])]
    pallas_call x5 -> x7, Pallas kernels: 14.8 us -> 10.2 us  [the longest x1 3.6 us: y_lines(): pl.pallas_call(y_lines_kernel, in_specs=[in_smem()] + [in_vmem()] * 4 + [...]
    ppermute x9, waiting for transfers between devices: 10.7 us -> 13 us  [shifted(): return lax.ppermute(value, 'gy', pairs)]
    ppermute x2, waiting for transfers between devices: 2.47 us -> 1.14 us  [other_core(): return lax.ppermute(value, 'gy', [(i, i ^ 1) for i in range(32)])]
  transfers between devices with their start and end apart: 13 -> 13, of which waited for: 7 -> 6; matrix products, arithmetic and copies ran while one was open for 1% -> 0% of each run, Pallas kernels for 9% -> 9%
where the time goes in v2:
time: 92 us; the launch traced here: 91.3 us
  starting transfers between devices  64.1 us (70%)
  waiting for transfers between devices  14.9 us (16%)
  Pallas kernels  10.2 us (11%)
  local copies, waits for them, and re-layouts  1.19 us (1%)
  between operations  0.97 us (1%)
    ppermute x9, starting transfers between devices, shifted(): return lax.ppermute(value, 'gy', pairs)  30.5 us
    all_to_all x2, starting transfers between devices, swap_x(): return lax.all_to_all(lines, 'gx', split_axis=0, concat_axis=0, tiled=True)  21 us
    ppermute x9, waiting for transfers between devices, shifted(): return lax.ppermute(value, 'gy', pairs)  13 us
    ppermute x2, starting transfers between devices, other_core(): return lax.ppermute(value, 'gy', [(i, i ^ 1) for i in range(32)])  12.6 us
    pallas_call x1, Pallas kernels, y_lines(): pl.pallas_call(y_lines_kernel, in_specs=[in_smem()] + [in_vmem()] * 4 + [...  3.6 us
    pallas_call x1, Pallas kernels, x_lines(): pl.pallas_call(x_lines_kernel, in_specs=[any_place(), any_place(), in_vme...  2.48 us
  transfers between devices with their start and end apart: 13, of which 6 were waited for; matrix products, arithmetic and copies ran while one was open for 0% of the time, Pallas kernels for 9%

profile of v2, /device:TPU:1, one launch (start us, length us, event | category | flops | bytes accessed | tf_op | source)
XLA Modules:
  0.0 91.3 jit_solution(11452526459829170971)
XLA Ops:
  0.6 0.0 copy-start
  0.6 1.1 %copy-done = f32[3,2,256,128]{3,2,1,0:T(8,128)S(1)} copy-done((f32[3,2,256,128]{3,2,1,0:T(8,128)S(1)}, f32[3,2,256,128]{3,2,1,0:T(8,128)}, u32[]{:S(2)}) %copy-start) | copy-done | bytes 786456
  1.8 0.9 %pack.1 = (f32[16,32,256]{2,1,0:T(8,128)}, f32[2,2,128,128]{3,2,1,0:T(8,128)S(1)}, f32[2,2,128,128]{3,2,1,0:T(8,128)S(1)}) custom-call(s32[1]{0:T(128)} %bitcast.me_ref, f32[3,2,256,128]{3,2,1,0:T(8,128)S(1)} %copy-done), custom_call_target="tpu_custom_call" | custom-call | bytes 2000000 | tf_op jit(solution)/shard_map/pack/pallas_call | solution.py:339
  2.7 8.8 %collective-permute-start = (f32[2,2,128,128]{3,2,1,0:T(8,128)S(1)}, f32[2,2,128,128]{3,2,1,0:T(8,128)S(1)}, u32[]{:S(2)}, u32[]{:S(2)}) collective-permute-start(f32[2,2,128,128]{3,2,1,0:T(8,128)S(1)} %get-tuple-element.21), channel_id=1, source_target_pairs={{0,1},{1,0},{2,3},{3,2},{4,5},{5,4},{6,7},{7,6},{8,9},{9,8},{10,11... | collective-permute-start | bytes 786440 | tf_op jit(solution)/shard_map/ppermute | solution.py:385
  11.5 9.6 %all-to-all-start = ((f32[16,32,256]{2,1,0:T(8,128)}), f32[16,32,256]{2,1,0:T(8,128)S(1)}, u32[]{:S(2)}, u32[]{:S(2)}) async-start(f32[16,32,256]{2,1,0:T(8,128)} %get-tuple-element.26), calls=%async_computation | async-start | bytes 1048576 | tf_op jit(solution)/shard_map/all_to_all | solution.py:532
  21.1 0.0 collective-permute-done.other_ref
  21.1 0.0 copy-start.8
  21.1 0.0 copy-start.9
  21.1 3.3 %collective-permute-start.1 = (f32[128,256]{1,0:T(8,128)S(1)}, f32[128,256]{1,0:T(8,128)S(1)}, u32[]{:S(2)}, u32[]{:S(2)}) collective-permute-start(f32[128,256]{1,0:T(8,128)S(1)} %get-tuple-element.23), channel_id=1, source_target_pairs={{0,8},{1,9},{2,10},{3,11},{4,12},{5,13},{6,14},{7,15},{8,16},{9,17... | collective-permute-start | bytes 393224 | tf_op jit(solution)/shard_map/ppermute | solution.py:381
  24.5 4.5 %collective-permute-start.2 = (f32[128,256]{1,0:T(8,128)S(1)}, f32[128,256]{1,0:T(8,128)S(1)}, u32[]{:S(2)}, u32[]{:S(2)}) collective-permute-start(f32[128,256]{1,0:T(8,128)S(1)} %get-tuple-element.24), channel_id=1, source_target_pairs={{0,16},{1,17},{2,18},{3,19},{4,20},{5,21},{6,22},{7,23},{8,24},{9,... | collective-permute-start | bytes 393224 | tf_op jit(solution)/shard_map/ppermute | solution.py:381
  29.0 3.0 %collective-permute-start.3 = (f32[128,256]{1,0:T(8,128)S(1)}, f32[128,256]{1,0:T(8,128)S(1)}, u32[]{:S(2)}, u32[]{:S(2)}) collective-permute-start(f32[128,256]{1,0:T(8,128)S(1)} %get-tuple-element.25), channel_id=1, source_target_pairs={{0,24},{1,25},{2,26},{3,27},{4,28},{5,29},{6,30},{7,31},{8,0},{9,1... | collective-permute-start | bytes 393224 | tf_op jit(solution)/shard_map/ppermute | solution.py:381
  32.0 0.0 collective-permute-done.1
  32.0 1.4 %collective-permute-done.2 = f32[128,256]{1,0:T(8,128)S(1)} collective-permute-done((f32[128,256]{1,0:T(8,128)S(1)}, f32[128,256]{1,0:T(8,128)S(1)}, u32[]{:S(2)}, u32[]{:S(2)}) %collective-permute-start.2) | collective-permute-done | bytes 131104 | tf_op jit(solution)/shard_map/ppermute | solution.py:381
  33.4 1.6 %collective-permute-done.3 = f32[128,256]{1,0:T(8,128)S(1)} collective-permute-done((f32[128,256]{1,0:T(8,128)S(1)}, f32[128,256]{1,0:T(8,128)S(1)}, u32[]{:S(2)}, u32[]{:S(2)}) %collective-permute-start.3) | collective-permute-done | bytes 131104 | tf_op jit(solution)/shard_map/ppermute | solution.py:381
  35.1 4.4 %collective-permute-start.6 = (f32[4,128,256]{2,1,0:T(8,128)S(1)}, f32[4,128,256]{2,1,0:T(8,128)S(1)}, u32[]{:S(2)}, u32[]{:S(2)}) collective-permute-start(f32[4,128,256]{2,1,0:T(8,128)S(1)} %pad_maximum_fusion.after_ref.p0), channel_id=1, source_target_pairs={{0,6},{1,7},{2,0},{3,1},{4,2},{5,3},{6,4},{7,5},{8,14},{9,15},{10,... | collective-permute-start | bytes 1572872 | tf_op jit(solution)/shard_map/ppermute | solution.py:381
  39.5 2.4 %collective-permute-start.5 = (f32[4,128,256]{2,1,0:T(8,128)S(1)}, f32[4,128,256]{2,1,0:T(8,128)S(1)}, u32[]{:S(2)}, u32[]{:S(2)}) collective-permute-start(f32[4,128,256]{2,1,0:T(8,128)S(1)} %pad_maximum_fusion.after_ref.p0), channel_id=1, source_target_pairs={{0,4},{1,5},{2,6},{3,7},{4,0},{5,1},{6,2},{7,3},{8,12},{9,13},{10,... | collective-permute-start | bytes 1572872 | tf_op jit(solution)/shard_map/ppermute | solution.py:381
  41.9 2.5 %collective-permute-start.4 = (f32[4,128,256]{2,1,0:T(8,128)S(1)}, f32[4,128,256]{2,1,0:T(8,128)S(1)}, u32[]{:S(2)}, u32[]{:S(2)}) collective-permute-start(f32[4,128,256]{2,1,0:T(8,128)S(1)} %pad_maximum_fusion.after_ref.p0), channel_id=1, source_target_pairs={{0,2},{1,3},{2,4},{3,5},{4,6},{5,7},{6,0},{7,1},{8,10},{9,11},{10,... | collective-permute-start | bytes 1572872 | tf_op jit(solution)/shard_map/ppermute | solution.py:381
  44.5 0.7 all-to-all-done.lines_ref
  45.2 0.0 copy-done.8
  45.2 0.0 copy-done.9
  45.2 2.5 %x_lines.1.after_ref = f32[16,32,256]{2,1,0:T(8,128)} custom-call(f32[16,32,256]{2,1,0:T(8,128)S(1)} %all-to-all-done.lines_ref, f32[4,128,256]{2,1,0:T(8,128)S(1)} %pad_maximum_fusion.after_ref.p0, bf16[2,256,512]{2,1,0:T(8,128)(2,1)S(1)} %copy-done.8, f32[3,9,256]{2,1,0:T(8,128)S(1)} %copy-done.9), custom_call_target="tpu_custom_call" | custom-call | flops 900000000 | bytes 1000000 | tf_op jit(solution)/shard_map/x_lines/pallas_call | solution.py:283
  47.7 11.5 %all-to-all-start.1 = ((f32[16,32,256]{2,1,0:T(8,128)}), f32[16,32,256]{2,1,0:T(8,128)S(1)}, u32[]{:S(2)}, u32[]{:S(2)}) async-start(f32[16,32,256]{2,1,0:T(8,128)} %x_lines.1.after_ref), calls=%async_computation.1 | async-start | bytes 1048576 | tf_op jit(solution)/shard_map/all_to_all | solution.py:532
  59.2 0.0 copy-start.1
  59.2 0.0 copy-start.2
  59.2 0.0 copy-start.3
  59.2 0.0 copy-start.4
  59.2 0.0 copy-start.5
  59.2 0.0 copy-start.6
  59.2 0.0 copy-start.7
  59.2 0.0 collective-permute-done.6.p3
  59.3 0.0 collective-permute-done.5.p2
  59.3 8.7 %collective-permute-done.4.p1 = f32[4,128,256]{2,1,0:T(8,128)S(1)} collective-permute-done((f32[4,128,256]{2,1,0:T(8,128)S(1)}, f32[4,128,256]{2,1,0:T(8,128)S(1)}, u32[]{:S(2)}, u32[]{:S(2)}) %collective-permute-start.4) | collective-permute-done | bytes 524320 | tf_op jit(solution)/shard_map/ppermute | solution.py:381
  68.0 3.6 %y_lines.1 = (f32[128,256]{1,0:T(8,128)S(1)}, f32[128,256]{1,0:T(8,128)S(1)}, f32[128,256]{1,0:T(8,128)S(1)}, f32[128,256]{1,0:T(8,128)S(1)}) custom-call(s32[1]{0:T(128)} %bitcast.me_ref, f32[4,128,256]{2,1,0:T(8,128)S(1)} %pad_maximum_fusion.after_ref.p0, f32[4,128,256]{2,1,0:T(8,128)S(1)} %collective-permute-done.4.p1, ...), custom_call_target="tpu_custom_call" | custom-call | flops 99999997952 | bytes 7000000 | tf_op jit(solution)/shard_map/y_lines/pallas_call | solution.py:303
  71.6 4.1 %collective-permute-start.7 = (f32[128,256]{1,0:T(8,128)S(1)}, f32[128,256]{1,0:T(8,128)S(1)}, u32[]{:S(2)}, u32[]{:S(2)}) collective-permute-start(f32[128,256]{1,0:T(8,128)S(1)} %get-tuple-element.31), channel_id=1, source_target_pairs={{0,8},{1,9},{2,10},{3,11},{4,12},{5,13},{6,14},{7,15},{8,16},{9,17... | collective-permute-start | bytes 393224 | tf_op jit(solution)/shard_map/ppermute | solution.py:381
  75.7 3.2 %collective-permute-start.8 = (f32[128,256]{1,0:T(8,128)S(1)}, f32[128,256]{1,0:T(8,128)S(1)}, u32[]{:S(2)}, u32[]{:S(2)}) collective-permute-start(f32[128,256]{1,0:T(8,128)S(1)} %get-tuple-element.32), channel_id=1, source_target_pairs={{0,16},{1,17},{2,18},{3,19},{4,20},{5,21},{6,22},{7,23},{8,24},{9,... | collective-permute-start | bytes 393224 | tf_op jit(solution)/shard_map/ppermute | solution.py:381
  78.9 3.0 %collective-permute-start.9 = (f32[128,256]{1,0:T(8,128)S(1)}, f32[128,256]{1,0:T(8,128)S(1)}, u32[]{:S(2)}, u32[]{:S(2)}) collective-permute-start(f32[128,256]{1,0:T(8,128)S(1)} %get-tuple-element.33), channel_id=1, source_target_pairs={{0,24},{1,25},{2,26},{3,27},{4,28},{5,29},{6,30},{7,31},{8,0},{9,1... | collective-permute-start | bytes 393224 | tf_op jit(solution)/shard_map/ppermute | solution.py:381
  81.9 0.0 copy-done.1
  81.9 0.0 copy-done.2
  82.0 0.0 copy-done.3
  82.0 0.0 copy-done.4
  82.0 0.0 copy-done.5
  82.0 0.0 copy-done.6
  82.0 0.0 copy-done.7
  82.0 1.7 %base.1 = (f32[2,2,256,128]{3,2,1,0:T(8,128)}, f32[7,2,256,128]{3,2,1,0:T(8,128)S(1)}, f32[256,128]{1,0:T(8,128)S(1)}, f32[8,256]{1,0:T(8,128)S(1)}) custom-call(f32[3,2,256,128]{3,2,1,0:T(8,128)S(1)} %copy-done.1, f32[2,2,256,128]{3,2,1,0:T(8,128)S(1)} %copy-done.3, f32[4,2,256,128]{3,2,1,0:T(8,128)S(1)} %copy-done.2, f32[256,128]{1,0:T(8,128)S(1)} %copy-done.5, ...), custom_call_target="tpu_custom_call" | custom-call | flops 3000000 | bytes 5000000 | tf_op jit(solution)/shard_map/base/pallas_call | solution.py:444
  83.7 0.0 collective-permute-done.7.q1
  83.7 0.0 collective-permute-done.8.q2
  83.7 1.2 %collective-permute-done.9.q3 = f32[128,256]{1,0:T(8,128)S(1)} collective-permute-done((f32[128,256]{1,0:T(8,128)S(1)}, f32[128,256]{1,0:T(8,128)S(1)}, u32[]{:S(2)}, u32[]{:S(2)}) %collective-permute-start.9) | collective-permute-done | bytes 131104 | tf_op jit(solution)/shard_map/ppermute | solution.py:381
  84.9 3.8 %collective-permute-start.10 = (f32[4,128,128]{2,1,0:T(8,128)S(1)}, f32[4,128,128]{2,1,0:T(8,128)S(1)}, u32[]{:S(2)}, u32[]{:S(2)}) collective-permute-start(f32[4,128,128]{2,1,0:T(8,128)S(1)} %split.1), channel_id=1, source_target_pairs={{0,1},{1,0},{2,3},{3,2},{4,5},{5,4},{6,7},{7,6},{8,9},{9,8},{10,11... | collective-permute-start | bytes 786440 | tf_op jit(solution)/shard_map/ppermute | solution.py:385
  88.7 1.1 %collective-permute-done.10.other = f32[4,128,128]{2,1,0:T(8,128)S(1)} collective-permute-done((f32[4,128,128]{2,1,0:T(8,128)S(1)}, f32[4,128,128]{2,1,0:T(8,128)S(1)}, u32[]{:S(2)}, u32[]{:S(2)}) %collective-permute-start.10) | collective-permute-done | bytes 262176 | tf_op jit(solution)/shard_map/ppermute | solution.py:385
  89.9 0.0 all-to-all-done.1.x_deriv
  89.9 1.4 %finish.1 = (f32[3,2,256,128]{3,2,1,0:T(8,128)}, f32[4,2,256,128]{3,2,1,0:T(8,128)}) custom-call(s32[1]{0:T(128)} %bitcast.me_ref, f32[7,2,256,128]{3,2,1,0:T(8,128)S(1)} %get-tuple-element.28.base, f32[256,128]{1,0:T(8,128)S(1)} %get-tuple-element.29.scale, f32[8,256]{1,0:T(8,128)S(1)} %get-tuple-element.30.after_ref.vectors, ...), custom_call_target="tpu_custom_call" | custom-call | flops 3000000 | bytes 5000000 | tf_op jit(solution)/shard_map/finish/pallas_call | solution.py:514
  (3 shorter events, 0.1 us)
Async XLA Ops:
  0.6 1.1 %copy-start = (f32[3,2,256,128]{3,2,1,0:T(8,128)S(1)}, f32[3,2,256,128]{3,2,1,0:T(8,128)}, u32[]{:S(2)}) copy-start(f32[3,2,256,128]{3,2,1,0:T(8,128)} %fields_ref.1) | copy-start | bytes 2359300
  2.7 18.4 %collective-permute-start = (f32[2,2,128,128]{3,2,1,0:T(8,128)S(1)}, f32[2,2,128,128]{3,2,1,0:T(8,128)S(1)}, u32[]{:S(2)}, u32[]{:S(2)}) collective-permute-start(f32[2,2,128,128]{3,2,1,0:T(8,128)S(1)} %get-tuple-element.21), channel_id=1, source_target_pairs={{0,1},{1,0},{2,3},{3,2},{4,5},{5,4},{6,7},{7,6},{8,9},{9,8},{10,11... | collective-permute-start | bytes 786440 | tf_op jit(solution)/shard_map/ppermute | solution.py:385
  11.5 33.7 %all-to-all-start = ((f32[16,32,256]{2,1,0:T(8,128)}), f32[16,32,256]{2,1,0:T(8,128)S(1)}, u32[]{:S(2)}, u32[]{:S(2)}) async-start(f32[16,32,256]{2,1,0:T(8,128)} %get-tuple-element.26), calls=%async_computation | async-start | bytes 1048576 | tf_op jit(solution)/shard_map/all_to_all | solution.py:532
  21.1 24.1 %copy-start.8 = (bf16[2,256,512]{2,1,0:T(8,128)(2,1)S(1)}, bf16[2,256,512]{2,1,0:T(8,128)(2,1)}, u32[]{:S(2)}) copy-start(bf16[2,256,512]{2,1,0:T(8,128)(2,1)} %constant.10.clone.matrix) | copy-start | bytes 1572868
  21.1 24.1 %copy-start.9 = (f32[3,9,256]{2,1,0:T(8,128)S(1)}, f32[3,9,256]{2,1,0:T(8,128)}, u32[]{:S(2)}) copy-start(f32[3,9,256]{2,1,0:T(8,128)} %constant.11.clone.vectors) | copy-start | bytes 82948
  21.1 10.9 %collective-permute-start.1 = (f32[128,256]{1,0:T(8,128)S(1)}, f32[128,256]{1,0:T(8,128)S(1)}, u32[]{:S(2)}, u32[]{:S(2)}) collective-permute-start(f32[128,256]{1,0:T(8,128)S(1)} %get-tuple-element.23), channel_id=1, source_target_pairs={{0,8},{1,9},{2,10},{3,11},{4,12},{5,13},{6,14},{7,15},{8,16},{9,17... | collective-permute-start | bytes 393224 | tf_op jit(solution)/shard_map/ppermute | solution.py:381
  24.5 9.0 %collective-permute-start.2 = (f32[128,256]{1,0:T(8,128)S(1)}, f32[128,256]{1,0:T(8,128)S(1)}, u32[]{:S(2)}, u32[]{:S(2)}) collective-permute-start(f32[128,256]{1,0:T(8,128)S(1)} %get-tuple-element.24), channel_id=1, source_target_pairs={{0,16},{1,17},{2,18},{3,19},{4,20},{5,21},{6,22},{7,23},{8,24},{9,... | collective-permute-start | bytes 393224 | tf_op jit(solution)/shard_map/ppermute | solution.py:381
  29.0 6.1 %collective-permute-start.3 = (f32[128,256]{1,0:T(8,128)S(1)}, f32[128,256]{1,0:T(8,128)S(1)}, u32[]{:S(2)}, u32[]{:S(2)}) collective-permute-start(f32[128,256]{1,0:T(8,128)S(1)} %get-tuple-element.25), channel_id=1, source_target_pairs={{0,24},{1,25},{2,26},{3,27},{4,28},{5,29},{6,30},{7,31},{8,0},{9,1... | collective-permute-start | bytes 393224 | tf_op jit(solution)/shard_map/ppermute | solution.py:381
  35.1 24.1 %collective-permute-start.6 = (f32[4,128,256]{2,1,0:T(8,128)S(1)}, f32[4,128,256]{2,1,0:T(8,128)S(1)}, u32[]{:S(2)}, u32[]{:S(2)}) collective-permute-start(f32[4,128,256]{2,1,0:T(8,128)S(1)} %pad_maximum_fusion.after_ref.p0), channel_id=1, source_target_pairs={{0,6},{1,7},{2,0},{3,1},{4,2},{5,3},{6,4},{7,5},{8,14},{9,15},{10,... | collective-permute-start | bytes 1572872 | tf_op jit(solution)/shard_map/ppermute | solution.py:381
  39.5 19.8 %collective-permute-start.5 = (f32[4,128,256]{2,1,0:T(8,128)S(1)}, f32[4,128,256]{2,1,0:T(8,128)S(1)}, u32[]{:S(2)}, u32[]{:S(2)}) collective-permute-start(f32[4,128,256]{2,1,0:T(8,128)S(1)} %pad_maximum_fusion.after_ref.p0), channel_id=1, source_target_pairs={{0,4},{1,5},{2,6},{3,7},{4,0},{5,1},{6,2},{7,3},{8,12},{9,13},{10,... | collective-permute-start | bytes 1572872 | tf_op jit(solution)/shard_map/ppermute | solution.py:381
  41.9 26.0 %collective-permute-start.4 = (f32[4,128,256]{2,1,0:T(8,128)S(1)}, f32[4,128,256]{2,1,0:T(8,128)S(1)}, u32[]{:S(2)}, u32[]{:S(2)}) collective-permute-start(f32[4,128,256]{2,1,0:T(8,128)S(1)} %pad_maximum_fusion.after_ref.p0), channel_id=1, source_target_pairs={{0,2},{1,3},{2,4},{3,5},{4,6},{5,7},{6,0},{7,1},{8,10},{9,11},{10,... | collective-permute-start | bytes 1572872 | tf_op jit(solution)/shard_map/ppermute | solution.py:381
  47.7 42.2 %all-to-all-start.1 = ((f32[16,32,256]{2,1,0:T(8,128)}), f32[16,32,256]{2,1,0:T(8,128)S(1)}, u32[]{:S(2)}, u32[]{:S(2)}) async-start(f32[16,32,256]{2,1,0:T(8,128)} %x_lines.1.after_ref), calls=%async_computation.1 | async-start | bytes 1048576 | tf_op jit(solution)/shard_map/all_to_all | solution.py:532
  59.2 22.8 %copy-start.1 = (f32[3,2,256,128]{3,2,1,0:T(8,128)S(1)}, f32[3,2,256,128]{3,2,1,0:T(8,128)}, u32[]{:S(2)}) copy-start(f32[3,2,256,128]{3,2,1,0:T(8,128)} %fields_ref.1) | copy-start | bytes 2359300
  59.2 22.8 %copy-start.2 = (f32[4,2,256,128]{3,2,1,0:T(8,128)S(1)}, f32[4,2,256,128]{3,2,1,0:T(8,128)}, u32[]{:S(2)}) copy-start(f32[4,2,256,128]{3,2,1,0:T(8,128)} %stretch_ref.1) | copy-start | bytes 3145732
  59.2 22.8 %copy-start.3 = (f32[2,2,256,128]{3,2,1,0:T(8,128)S(1)}, f32[2,2,256,128]{3,2,1,0:T(8,128)}, u32[]{:S(2)}) copy-start(f32[2,2,256,128]{3,2,1,0:T(8,128)} %poles_ref.1) | copy-start | bytes 1572868
  59.2 22.8 %copy-start.4 = (bf16[3,256,128]{2,1,0:T(8,128)(2,1)S(1)}, bf16[3,256,128]{2,1,0:T(8,128)(2,1)}, u32[]{:S(2)}) copy-start(bf16[3,256,128]{2,1,0:T(8,128)(2,1)} %rates_ref.1) | copy-start | bytes 589828
  59.2 22.8 %copy-start.5 = (f32[256,128]{1,0:T(8,128)S(1)}, f32[256,128]{1,0:T(8,128)}, u32[]{:S(2)}) copy-start(f32[256,128]{1,0:T(8,128)} %eps_ref.1) | copy-start | bytes 393220
  59.2 22.8 %copy-start.6 = (f32[3,256]{1,0:T(4,128)S(1)}, f32[3,256]{1,0:T(4,128)}, u32[]{:S(2)}) copy-start(f32[3,256]{1,0:T(4,128)} %x_prof.1) | copy-start | bytes 9220
  59.2 22.8 %copy-start.7 = (f32[3,128]{1,0:T(4,128)S(1)}, f32[3,128]{1,0:T(4,128)}, u32[]{:S(2)}) copy-start(f32[3,128]{1,0:T(4,128)} %y_prof.1) | copy-start | bytes 4612
  71.6 12.1 %collective-permute-start.7 = (f32[128,256]{1,0:T(8,128)S(1)}, f32[128,256]{1,0:T(8,128)S(1)}, u32[]{:S(2)}, u32[]{:S(2)}) collective-permute-start(f32[128,256]{1,0:T(8,128)S(1)} %get-tuple-element.31), channel_id=1, source_target_pairs={{0,8},{1,9},{2,10},{3,11},{4,12},{5,13},{6,14},{7,15},{8,16},{9,17... | collective-permute-start | bytes 393224 | tf_op jit(solution)/shard_map/ppermute | solution.py:381
  75.7 8.0 %collective-permute-start.8 = (f32[128,256]{1,0:T(8,128)S(1)}, f32[128,256]{1,0:T(8,128)S(1)}, u32[]{:S(2)}, u32[]{:S(2)}) collective-permute-start(f32[128,256]{1,0:T(8,128)S(1)} %get-tuple-element.32), channel_id=1, source_target_pairs={{0,16},{1,17},{2,18},{3,19},{4,20},{5,21},{6,22},{7,23},{8,24},{9,... | collective-permute-start | bytes 393224 | tf_op jit(solution)/shard_map/ppermute | solution.py:381
  78.9 6.0 %collective-permute-start.9 = (f32[128,256]{1,0:T(8,128)S(1)}, f32[128,256]{1,0:T(8,128)S(1)}, u32[]{:S(2)}, u32[]{:S(2)}) collective-permute-start(f32[128,256]{1,0:T(8,128)S(1)} %get-tuple-element.33), channel_id=1, source_target_pairs={{0,24},{1,25},{2,26},{3,27},{4,28},{5,29},{6,30},{7,31},{8,0},{9,1... | collective-permute-start | bytes 393224 | tf_op jit(solution)/shard_map/ppermute | solution.py:381
  84.9 5.0 %collective-permute-start.10 = (f32[4,128,128]{2,1,0:T(8,128)S(1)}, f32[4,128,128]{2,1,0:T(8,128)S(1)}, u32[]{:S(2)}, u32[]{:S(2)}) collective-permute-start(f32[4,128,128]{2,1,0:T(8,128)S(1)} %split.1), channel_id=1, source_target_pairs={{0,1},{1,0},{2,3},{3,2},{4,5},{5,4},{6,7},{7,6},{8,9},{9,8},{10,11... | collective-permute-start | bytes 786440 | tf_op jit(solution)/shard_map/ppermute | solution.py:385

commit v3 on v2

--- a/solution.py
+++ b/solution.py
@@ -15,6 +15,8 @@
 BLOCKS = 16
 WIDE = PERIOD // BLOCKS
 RES = BLOCKS // 2 + 1
+RING = (0, 1, 3, 5, 7, 9, 11, 13, 15, 14, 12, 10, 8, 6, 4, 2)
+PLACE = tuple(RING.index(p) for p in range(BLOCKS))
 VMEM_LIMIT = 16 * 1024 * 1024
 VMEM_MOST = 49 * 1024 * 1024
 
@@ -162,17 +164,13 @@
         residues[r, 1] = real[at] * sine + imag[at] * cosine
 
 
-def x_lines_kernel(lines_ref, after_ref, matrix, vectors, out_ref, work, residues, lines, arrived, sent):
+def x_lines_kernel(lines_ref, after_ref, matrix, vectors, out_ref, work, residues, lines, sent):
     parts = [(pl.ds(16 * g, 16), pl.ds(128 * h, 128)) for g in range(2) for h in range(2)]
-    incoming, outgoing = [], []
+    outgoing = []
     for i, (rows, lanes) in enumerate(parts):
         here = (slice(None), rows, lanes)
-        incoming.append(pltpu.make_async_copy(lines_ref.at[here], work.at[here], arrived.at[i]))
         outgoing.append(pltpu.make_async_copy(work.at[here], out_ref.at[here], sent.at[i]))
-        incoming[-1].start()
-    for copy, (rows, lanes) in zip(incoming, parts):
-        copy.wait()
-        for r, (real, imag) in enumerate(real_dft([work[p, rows, lanes] for p in range(BLOCKS)])):
+        for r, (real, imag) in enumerate(real_dft([lines_ref[PLACE[p], rows, lanes] for p in range(BLOCKS)])):
             residues[r, 0, rows, lanes] = real
             residues[r, 1, rows, lanes] = jnp.zeros_like(real) if imag is None else imag
     for first in range(0, RES, 3):
@@ -183,7 +181,7 @@
             imag = None if r in (0, RES - 1) else residues[r, 1, rows, lanes]
             spectrum.append((residues[r, 0, rows, lanes], imag))
         for p, value in enumerate(real_inverse(spectrum)):
-            work[p, rows, lanes] = value
+            work[PLACE[p], rows, lanes] = value
         copy.start()
     for copy in outgoing:
         copy.wait()
@@ -194,68 +192,72 @@
     blocks = circulant_blocks()
     parts = np.zeros((16, WIDE, 4 * WIDE), np.float64)
     for own in range(4):
-        for k in range(4):
-            place = 4 * own + k
-            for d in range(4):
-                block = blocks[(4 * d + own - (own - k) % 4) % BLOCKS] / 4.0
-                parts[place, :, :WIDE] += block
-                parts[place, :, WIDE : 2 * WIDE] += block * (1 - 2 * (d % 2))
-                parts[place, :, 2 * WIDE : 3 * WIDE] += 2.0 * block * (1, 0, -1, 0)[d]
-                parts[place, :, 3 * WIDE :] -= 2.0 * block * (0, 1, 0, -1)[d]
+        for core in range(2):
+            rows = slice(128 * core, 128 * core + 128)
+            order = np.concatenate([np.arange(128) + 128 * core, np.arange(128) + 128 * (1 - core)])
+            for k in range(4):
+                target = parts[4 * own + 2 * core + k // 2, 128 * (k % 2) : 128 * (k % 2) + 128]
+                for d in range(4):
+                    block = blocks[(4 * d + own - (own - k) % 4) % BLOCKS][rows][:, order] / 4.0
+                    target[:, :WIDE] += block
+                    target[:, WIDE : 2 * WIDE] += block * (1 - 2 * (d % 2))
+                    target[:, 2 * WIDE : 3 * WIDE] += 2.0 * block * (1, 0, -1, 0)[d]
+                    target[:, 3 * WIDE :] -= 2.0 * block * (0, 1, 0, -1)[d]
     return split_parts(parts)
 
 
-def y_lines_kernel(me_ref, p0, p1, p2, p3, after_ref, matrix_ref, o0, o1, o2, o3, matrix, lines, sums, arrived):
-    first = 4 * ((me_ref[0] >> 1) & 3)
-    copies = [pltpu.make_async_copy(matrix_ref.at[first + k], matrix.at[k], arrived.at[k]) for k in range(4)]
-    for copy in copies:
-        copy.start()
-
-    for k, piece in enumerate((p0, p1, p2, p3)):
-        slot = k % 2
-        for group in range(8):
+def load_kernel(me_ref, after_ref, matrix_ref, matrix, arrived):
+    first = 2 * (me_ref[0] & 7)
+    copy = pltpu.make_async_copy(matrix_ref.at[pl.ds(first, 2)], matrix, arrived)
+    copy.start()
+    copy.wait()
+
+
+def ring_terms(pair, pieces, matrix, lines):
+    for half, piece in enumerate(pieces):
+        lanes = pl.ds(128 * half, 128)
+        for group in range(16):
             at = pl.ds(16 * group, 16)
             w0, w1, w2, w3 = (piece[i, at, :] for i in (0, 3, 2, 1))
             values = (w0 + w2 + (w1 + w3), w0 + w2 - (w1 + w3), w0 - w2, w3 - w1)
-            for value, offset, gap in zip(values, (0, 256, 512, 640), (128, 128, 256, 256)):
-                high = value.astype(jnp.bfloat16)
-                lines[slot, pl.ds(offset + 16 * group, 16), :] = high
-                low = (value - high.astype(jnp.float32)).astype(jnp.bfloat16)
-                lines[slot, pl.ds(offset + gap + 16 * group, 16), :] = low
-        copies[k].wait()
-
-        def product(offset, count, columns):
-            main = jnp.dot(
-                lines[slot, offset : offset + 2 * count, :],
-                matrix[k, 0, :, columns],
-                preferred_element_type=jnp.float32,
-            )
-            rest = jnp.dot(
-                lines[slot, offset : offset + count, :],
-                matrix[k, 1, :, columns],
-                preferred_element_type=jnp.float32,
-            )
-            return main[:count] + main[count:] + rest
-
-        both = product(512, 256, slice(2 * WIDE, 4 * WIDE))
-        terms = (
-            product(0, 128, slice(0, WIDE)),
-            product(256, 128, slice(WIDE, 2 * WIDE)),
-            both[:128, :WIDE] - both[128:, WIDE:],
-            both[:128, WIDE:] + both[128:, :WIDE],
+            for value, offset, gap in zip(values, (0, 512, 1024, 1280), (256, 256, 512, 512)):
+                store_split(
+                    lines, (pl.ds(offset + 16 * group, 16), lanes), (pl.ds(offset + gap + 16 * group, 16), lanes), value
+                )
+
+    def product(offset, count, columns):
+        main = jnp.dot(
+            lines[offset : offset + 2 * count, :], matrix[pair, 0, :, columns], preferred_element_type=jnp.float32
         )
-        if k == 0:
-            for i, term in enumerate(terms):
-                sums[i] = term
-        elif k < 3:
-            for i, term in enumerate(terms):
-                sums[i] += term
-        else:
-            z0, z2, real, imag = (sums[i] + term for i, term in enumerate(terms))
-            o0[...] = z0 + z2 + real
-            o1[...] = z0 - z2 - imag
-            o2[...] = z0 + z2 - real
-            o3[...] = z0 - z2 + imag
+        rest = jnp.dot(
+            lines[offset : offset + count, :], matrix[pair, 1, :, columns], preferred_element_type=jnp.float32
+        )
+        return main[:count] + main[count:] + rest
+
+    both = product(1024, 512, slice(2 * WIDE, 4 * WIDE))
+    return (
+        product(0, 256, slice(0, WIDE)),
+        product(512, 256, slice(WIDE, 2 * WIDE)),
+        both[:256, :WIDE] - both[256:, WIDE:],
+        both[:256, WIDE:] + both[256:, :WIDE],
+    )
+
+
+def y_first_kernel(p2, p3, matrix, sums, lines):
+    for i, term in enumerate(ring_terms(1, (p2, p3), matrix, lines)):
+        sums[i] = term
+
+
+def y_lines_kernel(p0, p1, matrix, sums, own_ref, sent_ref, lines):
+    z0, z2, real, imag = (sums[i] + term for i, term in enumerate(ring_terms(0, (p0, p1), matrix, lines)))
+    for j, value in enumerate((z0 + z2 + real, z0 - z2 - imag, z0 + z2 - real, z0 - z2 + imag)):
+        own_ref[j] = value[:, :128]
+        sent_ref[j] = value[:, 128:]
+
+
+def add_kernel(own_ref, other_ref, *out_refs):
+    for j, out_ref in enumerate(out_refs):
+        out_ref[...] = own_ref[j] + other_ref[j]
 
 
 def whole(shape):
@@ -282,7 +284,7 @@
     matrix, vectors = residue_tables()
     return pl.pallas_call(
         x_lines_kernel,
-        in_specs=[any_place(), any_place(), in_vmem(), in_vmem()],
+        in_specs=[in_vmem(), any_place(), in_vmem(), in_vmem()],
         out_specs=any_place(),
         out_shape=jax.ShapeDtypeStruct((BLOCKS, 32, WIDE), jnp.float32),
         scratch_shapes=[
@@ -290,7 +292,6 @@
             pltpu.VMEM((RES, 2, 32, WIDE), jnp.float32),
             pltpu.VMEM((384, WIDE), jnp.bfloat16),
             pltpu.SemaphoreType.DMA((4,)),
-            pltpu.SemaphoreType.DMA((4,)),
         ],
         cost_estimate=pl.CostEstimate(flops=900_000_000, bytes_accessed=1_000_000, transcendentals=0),
         compiler_params=pltpu.CompilerParams(vmem_limit_bytes=VMEM_LIMIT),
@@ -298,78 +299,87 @@
     )(lines, after, jnp.asarray(matrix), jnp.asarray(vectors))
 
 
-def y_lines(me, pieces, after):
-    quarter = jax.ShapeDtypeStruct((128, WIDE), jnp.float32)
+def load(me, after):
+    matrices = ring_matrices()
+    return pl.pallas_call(
+        load_kernel,
+        in_specs=[in_smem(), any_place(), in_hbm()],
+        out_specs=in_vmem(),
+        out_shape=jax.ShapeDtypeStruct((2,) + matrices.shape[1:], jnp.bfloat16),
+        scratch_shapes=[pltpu.SemaphoreType.DMA],
+        cost_estimate=pl.CostEstimate(flops=0, bytes_accessed=2_000_000, transcendentals=0),
+        compiler_params=pltpu.CompilerParams(vmem_limit_bytes=VMEM_MOST),
+        name="load",
+    )(me, after, jnp.asarray(matrices))
+
+
+def y_first(pieces, matrices):
+    return pl.pallas_call(
+        y_first_kernel,
+        in_specs=[in_vmem()] * 3,
+        out_specs=in_vmem(),
+        out_shape=jax.ShapeDtypeStruct((4, 256, WIDE), jnp.float32),
+        scratch_shapes=[pltpu.VMEM((2048, WIDE), jnp.bfloat16)],
+        cost_estimate=pl.CostEstimate(flops=1_000_000_000, bytes_accessed=3_000_000, transcendentals=0),
+        compiler_params=pltpu.CompilerParams(vmem_limit_bytes=VMEM_LIMIT),
+        name="y_first",
+    )(*pieces, matrices)
+
+
+def y_lines(pieces, matrices, sums):
+    half = jax.ShapeDtypeStruct((4, 256, 128), jnp.float32)
     return pl.pallas_call(
         y_lines_kernel,
-        in_specs=[in_smem()] + [in_vmem()] * 4 + [any_place(), in_hbm()],
+        in_specs=[in_vmem()] * 4,
+        out_specs=[in_vmem()] * 2,
+        out_shape=[half] * 2,
+        scratch_shapes=[pltpu.VMEM((2048, WIDE), jnp.bfloat16)],
+        cost_estimate=pl.CostEstimate(flops=100_000_000_000, bytes_accessed=4_000_000, transcendentals=0),
+        compiler_params=pltpu.CompilerParams(vmem_limit_bytes=VMEM_LIMIT),
+        name="y_lines",
+    )(*pieces, matrices, sums)
+
+
+def add(own, other):
+    return pl.pallas_call(
+        add_kernel,
+        in_specs=[in_vmem()] * 2,
         out_specs=[in_vmem()] * 4,
-        out_shape=[quarter] * 4,
-        scratch_shapes=[
-            pltpu.VMEM((4, 2, WIDE, 4 * WIDE), jnp.bfloat16),
-            pltpu.VMEM((2, 1024, WIDE), jnp.bfloat16),
-            pltpu.VMEM((4, 128, WIDE), jnp.float32),
-            pltpu.SemaphoreType.DMA((4,)),
-        ],
-        cost_estimate=pl.CostEstimate(flops=100_000_000_000, bytes_accessed=7_000_000, transcendentals=0),
-        compiler_params=pltpu.CompilerParams(vmem_limit_bytes=VMEM_MOST),
-        name="y_lines",
-    )(me, *pieces, after, jnp.asarray(ring_matrices()))
-
-
-def pack_kernel(me_ref, fields, x_ref, own_ref, sent_ref, lines, arrived):
-    core = me_ref[0] & 1
-    own_rows = pl.ds(pl.multiple_of(core * 128, 128), 128)
-    sent_rows = pl.ds(pl.multiple_of(128 - core * 128, 128), 128)
+        out_shape=[jax.ShapeDtypeStruct((256, 128), jnp.float32)] * 4,
+        cost_estimate=pl.CostEstimate(flops=200_000, bytes_accessed=1_500_000, transcendentals=0),
+        compiler_params=pltpu.CompilerParams(vmem_limit_bytes=VMEM_LIMIT),
+        name="add",
+    )(own, other)
+
+
+def pack_kernel(me_ref, fields, x_ref, q0, q1, q2, q3, lines, arrived):
+    own_y = me_ref[0] >> 3
     copies = []
     for i in range(4):
         at = (slice(None), pl.ds(8 * i, 8))
         lines[at] = fields[i // 2 * 2, i % 2].T.reshape(16, 8, 256)
         copies.append(pltpu.make_async_copy(lines.at[at], x_ref.at[at], arrived.at[i]))
         copies[-1].start()
-    for i in range(4):
-        own_ref[i // 2, i % 2] = fields[i // 2, i % 2, own_rows, :]
-        sent_ref[i // 2, i % 2] = fields[i // 2, i % 2, sent_rows, :]
+    for j, quarter in enumerate((q0, q1, q2, q3)):
+        rows = pl.ds(pl.multiple_of(((own_y + j) & 3) * 64, 64), 64)
+        for i in range(4):
+            quarter[64 * i : 64 * i + 64, :] = fields[i // 2, i % 2, rows, :]
     for copy in copies:
         copy.wait()
 
 
 def pack(me, fields):
-    half = jax.ShapeDtypeStruct((2, 2, 128, 128), jnp.float32)
+    quarter = jax.ShapeDtypeStruct((256, 128), jnp.float32)
     return pl.pallas_call(
         pack_kernel,
         in_specs=[in_smem(), in_vmem()],
-        out_specs=[any_place(), in_vmem(), in_vmem()],
-        out_shape=[jax.ShapeDtypeStruct((16, 32, 256), jnp.float32), half, half],
+        out_specs=[any_place()] + [in_vmem()] * 4,
+        out_shape=[jax.ShapeDtypeStruct((16, 32, 256), jnp.float32)] + [quarter] * 4,
         scratch_shapes=[pltpu.VMEM((16, 32, 256), jnp.float32), pltpu.SemaphoreType.DMA((4,))],
         cost_estimate=pl.CostEstimate(flops=0, bytes_accessed=2_000_000, transcendentals=0),
         compiler_params=pltpu.CompilerParams(vmem_limit_bytes=VMEM_LIMIT),
         name="pack",
     )(me, fields)
-
-
-def y_pack_kernel(me_ref, own_ref, other_ref, *out_refs):
-    own_y, core = me_ref[0] >> 3, me_ref[0] & 1
-    here = pl.ds(pl.multiple_of(core * 128, 128), 128)
-    there = pl.ds(pl.multiple_of(128 - core * 128, 128), 128)
-    for j in range(4):
-        rows = pl.ds(pl.multiple_of(((own_y + j) & 3) * 32, 32), 32)
-        for i in range(4):
-            out_refs[j][32 * i : 32 * i + 32, here] = own_ref[i // 2, i % 2, rows, :]
-            out_refs[j][32 * i : 32 * i + 32, there] = other_ref[i // 2, i % 2, rows, :]
-
-
-def y_pack(me, own, other):
-    quarter = jax.ShapeDtypeStruct((128, WIDE), jnp.float32)
-    return pl.pallas_call(
-        y_pack_kernel,
-        in_specs=[in_smem(), in_vmem(), in_vmem()],
-        out_specs=[in_vmem()] * 4,
-        out_shape=[quarter] * 4,
-        cost_estimate=pl.CostEstimate(flops=100_000_000_000, bytes_accessed=1_000_000, transcendentals=0),
-        compiler_params=pltpu.CompilerParams(vmem_limit_bytes=VMEM_LIMIT),
-        name="y_pack",
-    )(me, own, other)
 
 
 def shifted(value, axis, distance):
@@ -468,17 +478,13 @@
 
 
 def finish_kernel(
-    me_ref, base, scale, vectors, x_deriv, q0, q1, q2, q3, other, next_fields, next_stretch, y_deriv, fields, stretch, sent
+    me_ref, base, scale, vectors, x_deriv, q0, q1, q2, q3, next_fields, next_stretch, y_deriv, fields, stretch, sent
 ):
-    own_y, core = me_ref[0] >> 3, me_ref[0] & 1
-    lanes = pl.ds(pl.multiple_of(core * 128, 128), 128)
+    own_y = me_ref[0] >> 3
     for j, quarter in enumerate((q0, q1, q2, q3)):
-        start = ((own_y - j) & 3) * 32
-        own_rows = pl.ds(pl.multiple_of(core * 128 + start, 32), 32)
-        other_rows = pl.ds(pl.multiple_of(128 - core * 128 + start, 32), 32)
+        rows = pl.ds(pl.multiple_of(((own_y - j) & 3) * 64, 64), 64)
         for i in range(4):
-            y_deriv[i, own_rows, :] = quarter[32 * i : 32 * i + 32, lanes]
-            y_deriv[i, other_rows, :] = other[j, 32 * i : 32 * i + 32, :]
+            y_deriv[i, rows, :] = quarter[64 * i : 64 * i + 64, :]
     over_y, feed_y = vectors[2:3, 0:128], vectors[3:4, 0:128]
     over_x, feed_x = (jnp.broadcast_to(vectors[i : i + 1, :], (128, 256)).T for i in range(2))
     eps = scale[...]
@@ -510,10 +516,10 @@
         copy.wait()
 
 
-def finish(me, base, scale, vectors, x_deriv, quarters, other):
+def finish(me, base, scale, vectors, x_deriv, quarters):
     return pl.pallas_call(
         finish_kernel,
-        in_specs=[in_smem()] + [in_vmem()] * 9,
+        in_specs=[in_smem()] + [in_vmem()] * 8,
         out_specs=[in_hbm()] * 2,
         out_shape=[jax.ShapeDtypeStruct((count, 2, 256, 128), jnp.float32) for count in (3, 4)],
         scratch_shapes=[
@@ -525,47 +531,28 @@
         cost_estimate=pl.CostEstimate(flops=3_000_000, bytes_accessed=5_000_000, transcendentals=0),
         compiler_params=pltpu.CompilerParams(vmem_limit_bytes=VMEM_LIMIT),
         name="finish",
-    )(me, base, scale, vectors, x_deriv, *quarters, other)
+    )(me, base, scale, vectors, x_deriv, *quarters)
 
 
 def swap_x(lines):
-    return lax.all_to_all(lines, "gx", split_axis=0, concat_axis=0, tiled=True)
-
-
-def split_kernel(me_ref, q0, q1, q2, q3, after_ref, sent_ref):
-    lanes = pl.ds(pl.multiple_of(128 - (me_ref[0] & 1) * 128, 128), 128)
-    for j, quarter in enumerate((q0, q1, q2, q3)):
-        sent_ref[j] = quarter[:, lanes]
-
-
-def split(me, quarters, after):
-    return pl.pallas_call(
-        split_kernel,
-        in_specs=[in_smem()] + [in_vmem()] * 4 + [any_place()],
-        out_specs=in_vmem(),
-        out_shape=jax.ShapeDtypeStruct((4, 128, 128), jnp.float32),
-        cost_estimate=pl.CostEstimate(flops=0, bytes_accessed=500_000, transcendentals=0),
-        compiler_params=pltpu.CompilerParams(vmem_limit_bytes=VMEM_LIMIT),
-        name="split",
-    )(me, *quarters, after)
+    return lax.all_to_all(lines, "gx", split_axis=0, concat_axis=0, tiled=True, axis_index_groups=[list(RING)])
 
 
 def shards(fields, pole_state, stretch_state, inverse_permittivity, pole_rates, x_profile, y_profile):
     me = lax.axis_index("gy").astype(jnp.int32).reshape(1)
-    x_packed, own, sent = pack(me, fields)
+    x_packed, *y_packed = pack(me, fields)
     x_sorted = swap_x(x_packed)
-    y_packed = y_pack(me, own, other_core(sent))
     y_held = jnp.stack(ring_swap(y_packed))
     y_pieces = ring_gather(y_held)
     x_lined = x_lines(x_sorted, y_held)
     x_deriv = swap_x(x_lined)
-    y_lined = y_lines(me, y_pieces, x_lined)
+    matrices = load(me, x_lined)
+    own, sent = y_lines(y_pieces[:2], matrices, y_first(y_pieces[2:], matrices))
+    y_lined = add(own, other_core(sent))
     next_poles, base, scale, vectors = base_part(
         fields, pole_state, stretch_state, inverse_permittivity, pole_rates, x_profile, y_profile, y_lined[0]
     )
-    quarters = ring_swap(y_lined)
-    other = other_core(split(me, quarters, vectors))
-    next_fields, next_stretch = finish(me, base, scale, vectors, x_deriv, quarters, other)
+    next_fields, next_stretch = finish(me, base, scale, vectors, x_deriv, ring_swap(y_lined))
     return next_fields, next_poles, next_stretch
 
 

time: 92 us -> 86.7 us (0.942)
  the two profiles are of different devices: /device:TPU:1 before, /device:TPU:124 now
where the time goes in v3:
time: 86.7 us; the launch traced here: 86.1 us
  starting transfers between devices  47.9 us (55%)
  waiting for transfers between devices  26.2 us (30%)
  Pallas kernels  9.75 us (11%)
  local copies, waits for them, and re-layouts  1.18 us (1%)
  between operations  0.93 us (1%)
    ppermute x9, starting transfers between devices, shifted(): return lax.ppermute(value, 'gy', pairs)  25.8 us
    all_to_all x2, starting transfers between devices, swap_x(): lax.all_to_all(lines, 'gx', split_axis=0, concat_axis=0, tiled=True, axis...  20.2 us
    ppermute x9, waiting for transfers between devices, shifted(): return lax.ppermute(value, 'gy', pairs)  13 us
    all_to_all x2, waiting for transfers between devices, swap_x(): lax.all_to_all(lines, 'gx', split_axis=0, concat_axis=0, tiled=True, axis...  11.4 us
    pallas_call x1, Pallas kernels, x_lines(): pl.pallas_call(x_lines_kernel, in_specs=[in_vmem(), any_place(), in_vmem(...  2.38 us
    ppermute x1, starting transfers between devices, other_core(): return lax.ppermute(value, 'gy', [(i, i ^ 1) for i in range(32)])  1.93 us
    ppermute x1, waiting for transfers between devices, other_core(): return lax.ppermute(value, 'gy', [(i, i ^ 1) for i in range(32)])  1.87 us
  transfers between devices with their start and end apart: 12, of which 8 were waited for; matrix products, arithmetic and copies ran while one was open for 0% of the time, Pallas kernels for 9%

profile of v3, /device:TPU:124, one launch (start us, length us, event | category | flops | bytes accessed | tf_op | source)
XLA Modules:
  0.0 86.1 jit_solution(11617302614236484789)
XLA Ops:
  0.6 0.0 copy-start
  0.6 1.1 %copy-done = f32[3,2,256,128]{3,2,1,0:T(8,128)S(1)} copy-done((f32[3,2,256,128]{3,2,1,0:T(8,128)S(1)}, f32[3,2,256,128]{3,2,1,0:T(8,128)}, u32[]{:S(2)}) %copy-start) | copy-done | bytes 786456
  1.8 0.0 copy-start.8
  1.8 0.0 copy-start.9
  1.8 0.9 %pack.1 = (f32[16,32,256]{2,1,0:T(8,128)}, f32[256,128]{1,0:T(8,128)S(1)}, f32[256,128]{1,0:T(8,128)S(1)}, f32[256,128]{1,0:T(8,128)S(1)}, f32[256,128]{1,0:T(8,128)S(1)}) custom-call(s32[1]{0:T(128)} %bitcast.me_ref, f32[3,2,256,128]{3,2,1,0:T(8,128)S(1)} %copy-done), custom_call_target="tpu_custom_call" | custom-call | bytes 2000000 | tf_op jit(solution)/shard_map/pack/pallas_call | solution.py:373
  2.7 14.3 %all-to-all-start = ((f32[16,32,256]{2,1,0:T(8,128)}), f32[16,32,256]{2,1,0:T(8,128)S(1)}, u32[]{:S(2)}, u32[]{:S(2)}) async-start(f32[16,32,256]{2,1,0:T(8,128)} %get-tuple-element.24), calls=%async_computation | async-start | bytes 1048576 | tf_op jit(solution)/shard_map/all_to_all | solution.py:538
  17.0 2.1 %collective-permute-start = (f32[256,128]{1,0:T(8,128)S(1)}, f32[256,128]{1,0:T(8,128)S(1)}, u32[]{:S(2)}, u32[]{:S(2)}) collective-permute-start(f32[256,128]{1,0:T(8,128)S(1)} %get-tuple-element.21), channel_id=1, source_target_pairs={{0,8},{1,9},{2,10},{3,11},{4,12},{5,13},{6,14},{7,15},{8,16},{9,17... | collective-permute-start | bytes 393224 | tf_op jit(solution)/shard_map/ppermute | solution.py:391
  19.1 4.5 %collective-permute-start.1 = (f32[256,128]{1,0:T(8,128)S(1)}, f32[256,128]{1,0:T(8,128)S(1)}, u32[]{:S(2)}, u32[]{:S(2)}) collective-permute-start(f32[256,128]{1,0:T(8,128)S(1)} %get-tuple-element.22), channel_id=1, source_target_pairs={{0,16},{1,17},{2,18},{3,19},{4,20},{5,21},{6,22},{7,23},{8,24},{9,... | collective-permute-start | bytes 393224 | tf_op jit(solution)/shard_map/ppermute | solution.py:391
  23.6 1.9 %collective-permute-start.2 = (f32[256,128]{1,0:T(8,128)S(1)}, f32[256,128]{1,0:T(8,128)S(1)}, u32[]{:S(2)}, u32[]{:S(2)}) collective-permute-start(f32[256,128]{1,0:T(8,128)S(1)} %get-tuple-element.23), channel_id=1, source_target_pairs={{0,24},{1,25},{2,26},{3,27},{4,28},{5,29},{6,30},{7,31},{8,0},{9,1... | collective-permute-start | bytes 393224 | tf_op jit(solution)/shard_map/ppermute | solution.py:391
  25.6 0.0 collective-permute-done
  25.6 1.9 %collective-permute-done.1 = f32[256,128]{1,0:T(8,128)S(1)} collective-permute-done((f32[256,128]{1,0:T(8,128)S(1)}, f32[256,128]{1,0:T(8,128)S(1)}, u32[]{:S(2)}, u32[]{:S(2)}) %collective-permute-start.1) | collective-permute-done | bytes 131104 | tf_op jit(solution)/shard_map/ppermute | solution.py:391
  27.5 4.2 %collective-permute-done.2 = f32[256,128]{1,0:T(8,128)S(1)} collective-permute-done((f32[256,128]{1,0:T(8,128)S(1)}, f32[256,128]{1,0:T(8,128)S(1)}, u32[]{:S(2)}, u32[]{:S(2)}) %collective-permute-start.2) | collective-permute-done | bytes 131104 | tf_op jit(solution)/shard_map/ppermute | solution.py:391
  31.8 2.4 %collective-permute-start.5 = (f32[4,256,128]{2,1,0:T(8,128)S(1)}, f32[4,256,128]{2,1,0:T(8,128)S(1)}, u32[]{:S(2)}, u32[]{:S(2)}) collective-permute-start(f32[4,256,128]{2,1,0:T(8,128)S(1)} %pad_maximum_fusion.after_ref.p0), channel_id=1, source_target_pairs={{0,6},{1,7},{2,0},{3,1},{4,2},{5,3},{6,4},{7,5},{8,14},{9,15},{10,... | collective-permute-start | bytes 1572872 | tf_op jit(solution)/shard_map/ppermute | solution.py:391
  34.2 4.6 %collective-permute-start.4 = (f32[4,256,128]{2,1,0:T(8,128)S(1)}, f32[4,256,128]{2,1,0:T(8,128)S(1)}, u32[]{:S(2)}, u32[]{:S(2)}) collective-permute-start(f32[4,256,128]{2,1,0:T(8,128)S(1)} %pad_maximum_fusion.after_ref.p0), channel_id=1, source_target_pairs={{0,4},{1,5},{2,6},{3,7},{4,0},{5,1},{6,2},{7,3},{8,12},{9,13},{10,... | collective-permute-start | bytes 1572872 | tf_op jit(solution)/shard_map/ppermute | solution.py:391
  38.9 1.9 %collective-permute-start.3 = (f32[4,256,128]{2,1,0:T(8,128)S(1)}, f32[4,256,128]{2,1,0:T(8,128)S(1)}, u32[]{:S(2)}, u32[]{:S(2)}) collective-permute-start(f32[4,256,128]{2,1,0:T(8,128)S(1)} %pad_maximum_fusion.after_ref.p0), channel_id=1, source_target_pairs={{0,2},{1,3},{2,4},{3,5},{4,6},{5,7},{6,0},{7,1},{8,10},{9,11},{10,... | collective-permute-start | bytes 1572872 | tf_op jit(solution)/shard_map/ppermute | solution.py:391
  40.8 6.2 %all-to-all-done.lines_ref = f32[16,32,256]{2,1,0:T(8,128)S(1)} async-done(((f32[16,32,256]{2,1,0:T(8,128)}), f32[16,32,256]{2,1,0:T(8,128)S(1)}, u32[]{:S(2)}, u32[]{:S(2)}) %all-to-all-start) | async-done | bytes 524320 | tf_op jit(solution)/shard_map/all_to_all | solution.py:538
  46.9 0.0 copy-done.8
  46.9 0.0 copy-done.9
  47.0 2.4 %x_lines.1.after_ref = f32[16,32,256]{2,1,0:T(8,128)} custom-call(f32[16,32,256]{2,1,0:T(8,128)S(1)} %all-to-all-done.lines_ref, f32[4,256,128]{2,1,0:T(8,128)S(1)} %pad_maximum_fusion.after_ref.p0, bf16[2,256,512]{2,1,0:T(8,128)(2,1)S(1)} %copy-done.8, f32[3,9,256]{2,1,0:T(8,128)S(1)} %copy-done.9), custom_call_target="tpu_custom_call" | custom-call | flops 900000000 | bytes 1000000 | tf_op jit(solution)/shard_map/x_lines/pallas_call | solution.py:285
  49.3 5.9 %all-to-all-start.1 = ((f32[16,32,256]{2,1,0:T(8,128)}), f32[16,32,256]{2,1,0:T(8,128)S(1)}, u32[]{:S(2)}, u32[]{:S(2)}) async-start(f32[16,32,256]{2,1,0:T(8,128)} %x_lines.1.after_ref), calls=%async_computation.1 | async-start | bytes 1048576 | tf_op jit(solution)/shard_map/all_to_all | solution.py:538
  55.3 1.6 %load.1.matrix = bf16[2,2,256,1024]{3,2,1,0:T(8,128)(2,1)S(1)} custom-call(s32[1]{0:T(128)} %bitcast.me_ref, f32[16,32,256]{2,1,0:T(8,128)} %x_lines.1.after_ref, bf16[16,2,256,1024]{3,2,1,0:T(8,128)(2,1)} %constant.12.clone.matrix_ref), custom_call_target="tpu_custom_call" | custom-call | bytes 2000000 | tf_op jit(solution)/shard_map/load/pallas_call | solution.py:304
  56.9 0.0 collective-permute-done.5.p3
  56.9 0.0 collective-permute-done.4.p2
  56.9 0.8 y_first.1.sums
  57.7 0.0 copy-start.1
  57.7 0.0 copy-start.2
  57.8 0.0 copy-start.3
  57.8 0.0 copy-start.4
  57.8 0.0 copy-start.5
  57.8 0.0 copy-start.6
  57.8 0.0 copy-start.7
  57.8 2.4 %collective-permute-done.3.p1 = f32[4,256,128]{2,1,0:T(8,128)S(1)} collective-permute-done((f32[4,256,128]{2,1,0:T(8,128)S(1)}, f32[4,256,128]{2,1,0:T(8,128)S(1)}, u32[]{:S(2)}, u32[]{:S(2)}) %collective-permute-start.3) | collective-permute-done | bytes 524320 | tf_op jit(solution)/shard_map/ppermute | solution.py:391
  60.3 0.9 %y_lines.1 = (f32[4,256,128]{2,1,0:T(8,128)S(1)}, f32[4,256,128]{2,1,0:T(8,128)S(1)}) custom-call(f32[4,256,128]{2,1,0:T(8,128)S(1)} %pad_maximum_fusion.after_ref.p0, f32[4,256,128]{2,1,0:T(8,128)S(1)} %collective-permute-done.3.p1, bf16[2,2,256,1024]{3,2,1,0:T(8,128)(2,1)S(1)} %load.1.matrix, f32[4,256,256]{2,1,0:T(8,128)S(1)} %y_first.1.sums), custom_call_target="tpu_custom_call" | custom-call | flops 99999997952 | bytes 4000000 | tf_op jit(solution)/shard_map/y_lines/pallas_call | solution.py:331
  61.1 1.9 %collective-permute-start.6 = (f32[4,256,128]{2,1,0:T(8,128)S(1)}, f32[4,256,128]{2,1,0:T(8,128)S(1)}, u32[]{:S(2)}, u32[]{:S(2)}) collective-permute-start(f32[4,256,128]{2,1,0:T(8,128)S(1)} %get-tuple-element.26), channel_id=1, source_target_pairs={{0,1},{1,0},{2,3},{3,2},{4,5},{5,4},{6,7},{7,6},{8,9},{9,8},{10,11... | collective-permute-start | bytes 1572872 | tf_op jit(solution)/shard_map/ppermute | solution.py:395
  63.1 1.9 %collective-permute-done.6.other_ref = f32[4,256,128]{2,1,0:T(8,128)S(1)} collective-permute-done((f32[4,256,128]{2,1,0:T(8,128)S(1)}, f32[4,256,128]{2,1,0:T(8,128)S(1)}, u32[]{:S(2)}, u32[]{:S(2)}) %collective-permute-start.6) | collective-permute-done | bytes 524320 | tf_op jit(solution)/shard_map/ppermute | solution.py:395
  65.0 0.1 add.1
  65.0 2.6 %collective-permute-start.7 = (f32[256,128]{1,0:T(8,128)S(1)}, f32[256,128]{1,0:T(8,128)S(1)}, u32[]{:S(2)}, u32[]{:S(2)}) collective-permute-start(f32[256,128]{1,0:T(8,128)S(1)} %get-tuple-element.31), channel_id=1, source_target_pairs={{0,8},{1,9},{2,10},{3,11},{4,12},{5,13},{6,14},{7,15},{8,16},{9,17... | collective-permute-start | bytes 393224 | tf_op jit(solution)/shard_map/ppermute | solution.py:391
  67.6 3.7 %collective-permute-start.8 = (f32[256,128]{1,0:T(8,128)S(1)}, f32[256,128]{1,0:T(8,128)S(1)}, u32[]{:S(2)}, u32[]{:S(2)}) collective-permute-start(f32[256,128]{1,0:T(8,128)S(1)} %get-tuple-element.32), channel_id=1, source_target_pairs={{0,16},{1,17},{2,18},{3,19},{4,20},{5,21},{6,22},{7,23},{8,24},{9,... | collective-permute-start | bytes 393224 | tf_op jit(solution)/shard_map/ppermute | solution.py:391
  71.3 1.9 %collective-permute-start.9 = (f32[256,128]{1,0:T(8,128)S(1)}, f32[256,128]{1,0:T(8,128)S(1)}, u32[]{:S(2)}, u32[]{:S(2)}) collective-permute-start(f32[256,128]{1,0:T(8,128)S(1)} %get-tuple-element.33), channel_id=1, source_target_pairs={{0,24},{1,25},{2,26},{3,27},{4,28},{5,29},{6,30},{7,31},{8,0},{9,1... | collective-permute-start | bytes 393224 | tf_op jit(solution)/shard_map/ppermute | solution.py:391
  73.3 0.0 copy-done.1
  73.3 0.0 copy-done.2
  73.3 0.0 copy-done.3
  73.3 0.0 copy-done.4
  73.3 0.0 copy-done.5
  73.3 0.0 copy-done.6
  73.3 0.0 copy-done.7
  73.3 1.7 %base.1 = (f32[2,2,256,128]{3,2,1,0:T(8,128)}, f32[7,2,256,128]{3,2,1,0:T(8,128)S(1)}, f32[256,128]{1,0:T(8,128)S(1)}, f32[8,256]{1,0:T(8,128)S(1)}) custom-call(f32[3,2,256,128]{3,2,1,0:T(8,128)S(1)} %copy-done.1, f32[2,2,256,128]{3,2,1,0:T(8,128)S(1)} %copy-done.3, f32[4,2,256,128]{3,2,1,0:T(8,128)S(1)} %copy-done.2, f32[256,128]{1,0:T(8,128)S(1)} %copy-done.5, ...), custom_call_target="tpu_custom_call" | custom-call | flops 3000000 | bytes 5000000 | tf_op jit(solution)/shard_map/base/pallas_call | solution.py:454
  75.0 0.0 collective-permute-done.7.q1
  75.0 1.2 %collective-permute-done.8.q2 = f32[256,128]{1,0:T(8,128)S(1)} collective-permute-done((f32[256,128]{1,0:T(8,128)S(1)}, f32[256,128]{1,0:T(8,128)S(1)}, u32[]{:S(2)}, u32[]{:S(2)}) %collective-permute-start.8) | collective-permute-done | bytes 131104 | tf_op jit(solution)/shard_map/ppermute | solution.py:391
  76.3 3.2 %collective-permute-done.9.q3 = f32[256,128]{1,0:T(8,128)S(1)} collective-permute-done((f32[256,128]{1,0:T(8,128)S(1)}, f32[256,128]{1,0:T(8,128)S(1)}, u32[]{:S(2)}, u32[]{:S(2)}) %collective-permute-start.9) | collective-permute-done | bytes 131104 | tf_op jit(solution)/shard_map/ppermute | solution.py:391
  79.4 5.2 %all-to-all-done.1.x_deriv = f32[16,32,256]{2,1,0:T(8,128)S(1)} async-done(((f32[16,32,256]{2,1,0:T(8,128)}), f32[16,32,256]{2,1,0:T(8,128)S(1)}, u32[]{:S(2)}, u32[]{:S(2)}) %all-to-all-start.1) | async-done | bytes 524320 | tf_op jit(solution)/shard_map/all_to_all | solution.py:538
  84.6 1.4 %finish.1 = (f32[3,2,256,128]{3,2,1,0:T(8,128)}, f32[4,2,256,128]{3,2,1,0:T(8,128)}) custom-call(s32[1]{0:T(128)} %bitcast.me_ref, f32[7,2,256,128]{3,2,1,0:T(8,128)S(1)} %get-tuple-element.28.base, f32[256,128]{1,0:T(8,128)S(1)} %get-tuple-element.29.scale, f32[8,256]{1,0:T(8,128)S(1)} %get-tuple-element.30.vectors, ...), custom_call_target="tpu_custom_call" | custom-call | flops 3000000 | bytes 5000000 | tf_op jit(solution)/shard_map/finish/pallas_call | solution.py:520
  (1 shorter events, 0.0 us)
Async XLA Ops:
  0.6 1.1 %copy-start = (f32[3,2,256,128]{3,2,1,0:T(8,128)S(1)}, f32[3,2,256,128]{3,2,1,0:T(8,128)}, u32[]{:S(2)}) copy-start(f32[3,2,256,128]{3,2,1,0:T(8,128)} %fields_ref.1) | copy-start | bytes 2359300
  1.8 45.2 %copy-start.8 = (bf16[2,256,512]{2,1,0:T(8,128)(2,1)S(1)}, bf16[2,256,512]{2,1,0:T(8,128)(2,1)}, u32[]{:S(2)}) copy-start(bf16[2,256,512]{2,1,0:T(8,128)(2,1)} %constant.10.clone.matrix) | copy-start | bytes 1572868
  1.8 45.2 %copy-start.9 = (f32[3,9,256]{2,1,0:T(8,128)S(1)}, f32[3,9,256]{2,1,0:T(8,128)}, u32[]{:S(2)}) copy-start(f32[3,9,256]{2,1,0:T(8,128)} %constant.11.clone.vectors) | copy-start | bytes 82948
  2.7 44.2 %all-to-all-start = ((f32[16,32,256]{2,1,0:T(8,128)}), f32[16,32,256]{2,1,0:T(8,128)S(1)}, u32[]{:S(2)}, u32[]{:S(2)}) async-start(f32[16,32,256]{2,1,0:T(8,128)} %get-tuple-element.24), calls=%async_computation | async-start | bytes 1048576 | tf_op jit(solution)/shard_map/all_to_all | solution.py:538
  17.0 8.6 %collective-permute-start = (f32[256,128]{1,0:T(8,128)S(1)}, f32[256,128]{1,0:T(8,128)S(1)}, u32[]{:S(2)}, u32[]{:S(2)}) collective-permute-start(f32[256,128]{1,0:T(8,128)S(1)} %get-tuple-element.21), channel_id=1, source_target_pairs={{0,8},{1,9},{2,10},{3,11},{4,12},{5,13},{6,14},{7,15},{8,16},{9,17... | collective-permute-start | bytes 393224 | tf_op jit(solution)/shard_map/ppermute | solution.py:391
  19.1 8.4 %collective-permute-start.1 = (f32[256,128]{1,0:T(8,128)S(1)}, f32[256,128]{1,0:T(8,128)S(1)}, u32[]{:S(2)}, u32[]{:S(2)}) collective-permute-start(f32[256,128]{1,0:T(8,128)S(1)} %get-tuple-element.22), channel_id=1, source_target_pairs={{0,16},{1,17},{2,18},{3,19},{4,20},{5,21},{6,22},{7,23},{8,24},{9,... | collective-permute-start | bytes 393224 | tf_op jit(solution)/shard_map/ppermute | solution.py:391
  23.6 8.1 %collective-permute-start.2 = (f32[256,128]{1,0:T(8,128)S(1)}, f32[256,128]{1,0:T(8,128)S(1)}, u32[]{:S(2)}, u32[]{:S(2)}) collective-permute-start(f32[256,128]{1,0:T(8,128)S(1)} %get-tuple-element.23), channel_id=1, source_target_pairs={{0,24},{1,25},{2,26},{3,27},{4,28},{5,29},{6,30},{7,31},{8,0},{9,1... | collective-permute-start | bytes 393224 | tf_op jit(solution)/shard_map/ppermute | solution.py:391
  31.8 25.1 %collective-permute-start.5 = (f32[4,256,128]{2,1,0:T(8,128)S(1)}, f32[4,256,128]{2,1,0:T(8,128)S(1)}, u32[]{:S(2)}, u32[]{:S(2)}) collective-permute-start(f32[4,256,128]{2,1,0:T(8,128)S(1)} %pad_maximum_fusion.after_ref.p0), channel_id=1, source_target_pairs={{0,6},{1,7},{2,0},{3,1},{4,2},{5,3},{6,4},{7,5},{8,14},{9,15},{10,... | collective-permute-start | bytes 1572872 | tf_op jit(solution)/shard_map/ppermute | solution.py:391
  34.2 22.7 %collective-permute-start.4 = (f32[4,256,128]{2,1,0:T(8,128)S(1)}, f32[4,256,128]{2,1,0:T(8,128)S(1)}, u32[]{:S(2)}, u32[]{:S(2)}) collective-permute-start(f32[4,256,128]{2,1,0:T(8,128)S(1)} %pad_maximum_fusion.after_ref.p0), channel_id=1, source_target_pairs={{0,4},{1,5},{2,6},{3,7},{4,0},{5,1},{6,2},{7,3},{8,12},{9,13},{10,... | collective-permute-start | bytes 1572872 | tf_op jit(solution)/shard_map/ppermute | solution.py:391
  38.9 21.4 %collective-permute-start.3 = (f32[4,256,128]{2,1,0:T(8,128)S(1)}, f32[4,256,128]{2,1,0:T(8,128)S(1)}, u32[]{:S(2)}, u32[]{:S(2)}) collective-permute-start(f32[4,256,128]{2,1,0:T(8,128)S(1)} %pad_maximum_fusion.after_ref.p0), channel_id=1, source_target_pairs={{0,2},{1,3},{2,4},{3,5},{4,6},{5,7},{6,0},{7,1},{8,10},{9,11},{10,... | collective-permute-start | bytes 1572872 | tf_op jit(solution)/shard_map/ppermute | solution.py:391
  49.3 35.3 %all-to-all-start.1 = ((f32[16,32,256]{2,1,0:T(8,128)}), f32[16,32,256]{2,1,0:T(8,128)S(1)}, u32[]{:S(2)}, u32[]{:S(2)}) async-start(f32[16,32,256]{2,1,0:T(8,128)} %x_lines.1.after_ref), calls=%async_computation.1 | async-start | bytes 1048576 | tf_op jit(solution)/shard_map/all_to_all | solution.py:538
  57.7 15.6 %copy-start.1 = (f32[3,2,256,128]{3,2,1,0:T(8,128)S(1)}, f32[3,2,256,128]{3,2,1,0:T(8,128)}, u32[]{:S(2)}) copy-start(f32[3,2,256,128]{3,2,1,0:T(8,128)} %fields_ref.1) | copy-start | bytes 2359300
  57.7 15.6 %copy-start.2 = (f32[4,2,256,128]{3,2,1,0:T(8,128)S(1)}, f32[4,2,256,128]{3,2,1,0:T(8,128)}, u32[]{:S(2)}) copy-start(f32[4,2,256,128]{3,2,1,0:T(8,128)} %stretch_ref.1) | copy-start | bytes 3145732
  57.8 15.5 %copy-start.3 = (f32[2,2,256,128]{3,2,1,0:T(8,128)S(1)}, f32[2,2,256,128]{3,2,1,0:T(8,128)}, u32[]{:S(2)}) copy-start(f32[2,2,256,128]{3,2,1,0:T(8,128)} %poles_ref.1) | copy-start | bytes 1572868
  57.8 15.5 %copy-start.4 = (bf16[3,256,128]{2,1,0:T(8,128)(2,1)S(1)}, bf16[3,256,128]{2,1,0:T(8,128)(2,1)}, u32[]{:S(2)}) copy-start(bf16[3,256,128]{2,1,0:T(8,128)(2,1)} %rates_ref.1) | copy-start | bytes 589828
  57.8 15.5 %copy-start.5 = (f32[256,128]{1,0:T(8,128)S(1)}, f32[256,128]{1,0:T(8,128)}, u32[]{:S(2)}) copy-start(f32[256,128]{1,0:T(8,128)} %eps_ref.1) | copy-start | bytes 393220
  57.8 15.5 %copy-start.6 = (f32[3,256]{1,0:T(4,128)S(1)}, f32[3,256]{1,0:T(4,128)}, u32[]{:S(2)}) copy-start(f32[3,256]{1,0:T(4,128)} %x_prof.1) | copy-start | bytes 9220
  57.8 15.5 %copy-start.7 = (f32[3,128]{1,0:T(4,128)S(1)}, f32[3,128]{1,0:T(4,128)}, u32[]{:S(2)}) copy-start(f32[3,128]{1,0:T(4,128)} %y_prof.1) | copy-start | bytes 4612
  61.1 3.8 %collective-permute-start.6 = (f32[4,256,128]{2,1,0:T(8,128)S(1)}, f32[4,256,128]{2,1,0:T(8,128)S(1)}, u32[]{:S(2)}, u32[]{:S(2)}) collective-permute-start(f32[4,256,128]{2,1,0:T(8,128)S(1)} %get-tuple-element.26), channel_id=1, source_target_pairs={{0,1},{1,0},{2,3},{3,2},{4,5},{5,4},{6,7},{7,6},{8,9},{9,8},{10,11... | collective-permute-start | bytes 1572872 | tf_op jit(solution)/shard_map/ppermute | solution.py:395
  65.0 10.0 %collective-permute-start.7 = (f32[256,128]{1,0:T(8,128)S(1)}, f32[256,128]{1,0:T(8,128)S(1)}, u32[]{:S(2)}, u32[]{:S(2)}) collective-permute-start(f32[256,128]{1,0:T(8,128)S(1)} %get-tuple-element.31), channel_id=1, source_target_pairs={{0,8},{1,9},{2,10},{3,11},{4,12},{5,13},{6,14},{7,15},{8,16},{9,17... | collective-permute-start | bytes 393224 | tf_op jit(solution)/shard_map/ppermute | solution.py:391
  67.6 8.7 %collective-permute-start.8 = (f32[256,128]{1,0:T(8,128)S(1)}, f32[256,128]{1,0:T(8,128)S(1)}, u32[]{:S(2)}, u32[]{:S(2)}) collective-permute-start(f32[256,128]{1,0:T(8,128)S(1)} %get-tuple-element.32), channel_id=1, source_target_pairs={{0,16},{1,17},{2,18},{3,19},{4,20},{5,21},{6,22},{7,23},{8,24},{9,... | collective-permute-start | bytes 393224 | tf_op jit(solution)/shard_map/ppermute | solution.py:391
  71.3 8.1 %collective-permute-start.9 = (f32[256,128]{1,0:T(8,128)S(1)}, f32[256,128]{1,0:T(8,128)S(1)}, u32[]{:S(2)}, u32[]{:S(2)}) collective-permute-start(f32[256,128]{1,0:T(8,128)S(1)} %get-tuple-element.33), channel_id=1, source_target_pairs={{0,24},{1,25},{2,26},{3,27},{4,28},{5,29},{6,30},{7,31},{8,0},{9,1... | collective-permute-start | bytes 393224 | tf_op jit(solution)/shard_map/ppermute | solution.py:391

commit v4 on v3

--- a/solution.py
+++ b/solution.py
@@ -15,7 +15,7 @@
 BLOCKS = 16
 WIDE = PERIOD // BLOCKS
 RES = BLOCKS // 2 + 1
-RING = (0, 1, 3, 5, 7, 9, 11, 13, 15, 14, 12, 10, 8, 6, 4, 2)
+RING = (12, 13, 14, 15, 11, 10, 9, 8, 4, 5, 6, 7, 3, 2, 1, 0)
 PLACE = tuple(RING.index(p) for p in range(BLOCKS))
 VMEM_LIMIT = 16 * 1024 * 1024
 VMEM_MOST = 49 * 1024 * 1024

time: 86.7 us -> 85.4 us (0.985)
  the two profiles are of different devices: /device:TPU:124 before, /device:TPU:1 now
where the time goes in v4:
time: 85.4 us; the launch traced here: 84.6 us
  starting transfers between devices  60 us (70%)
  waiting for transfers between devices  12.7 us (15%)
  Pallas kernels  9.75 us (11%)
  local copies, waits for them, and re-layouts  1.18 us (1%)
  between operations  0.95 us (1%)
    ppermute x9, starting transfers between devices, shifted(): return lax.ppermute(value, 'gy', pairs)  30 us
    all_to_all x2, starting transfers between devices, swap_x(): lax.all_to_all(lines, 'gx', split_axis=0, concat_axis=0, tiled=True, axis...  27.6 us
    ppermute x9, waiting for transfers between devices, shifted(): return lax.ppermute(value, 'gy', pairs)  11.2 us
    ppermute x1, starting transfers between devices, other_core(): return lax.ppermute(value, 'gy', [(i, i ^ 1) for i in range(32)])  2.4 us
    pallas_call x1, Pallas kernels, x_lines(): pl.pallas_call(x_lines_kernel, in_specs=[in_vmem(), any_place(), in_vmem(...  2.39 us
  transfers between devices with their start and end apart: 12, of which 5 were waited for; matrix products, arithmetic and copies ran while one was open for 0% of the time, Pallas kernels for 9%

profile of v4, /device:TPU:1, one launch (start us, length us, event | category | flops | bytes accessed | tf_op | source)
XLA Modules:
  0.0 84.6 jit_solution(11794829832319114928)
XLA Ops:
  0.6 0.0 copy-start
  0.6 1.1 %copy-done = f32[3,2,256,128]{3,2,1,0:T(8,128)S(1)} copy-done((f32[3,2,256,128]{3,2,1,0:T(8,128)S(1)}, f32[3,2,256,128]{3,2,1,0:T(8,128)}, u32[]{:S(2)}) %copy-start) | copy-done | bytes 786456
  1.8 0.0 copy-start.8
  1.8 0.0 copy-start.9
  1.8 0.9 %pack.1 = (f32[16,32,256]{2,1,0:T(8,128)}, f32[256,128]{1,0:T(8,128)S(1)}, f32[256,128]{1,0:T(8,128)S(1)}, f32[256,128]{1,0:T(8,128)S(1)}, f32[256,128]{1,0:T(8,128)S(1)}) custom-call(s32[1]{0:T(128)} %bitcast.me_ref, f32[3,2,256,128]{3,2,1,0:T(8,128)S(1)} %copy-done), custom_call_target="tpu_custom_call" | custom-call | bytes 2000000 | tf_op jit(solution)/shard_map/pack/pallas_call | solution.py:373
  2.7 16.0 %all-to-all-start = ((f32[16,32,256]{2,1,0:T(8,128)}), f32[16,32,256]{2,1,0:T(8,128)S(1)}, u32[]{:S(2)}, u32[]{:S(2)}) async-start(f32[16,32,256]{2,1,0:T(8,128)} %get-tuple-element.24), calls=%async_computation | async-start | bytes 1048576 | tf_op jit(solution)/shard_map/all_to_all | solution.py:538
  18.7 3.2 %collective-permute-start = (f32[256,128]{1,0:T(8,128)S(1)}, f32[256,128]{1,0:T(8,128)S(1)}, u32[]{:S(2)}, u32[]{:S(2)}) collective-permute-start(f32[256,128]{1,0:T(8,128)S(1)} %get-tuple-element.21), channel_id=1, source_target_pairs={{0,8},{1,9},{2,10},{3,11},{4,12},{5,13},{6,14},{7,15},{8,16},{9,17... | collective-permute-start | bytes 393224 | tf_op jit(solution)/shard_map/ppermute | solution.py:391
  21.9 4.5 %collective-permute-start.1 = (f32[256,128]{1,0:T(8,128)S(1)}, f32[256,128]{1,0:T(8,128)S(1)}, u32[]{:S(2)}, u32[]{:S(2)}) collective-permute-start(f32[256,128]{1,0:T(8,128)S(1)} %get-tuple-element.22), channel_id=1, source_target_pairs={{0,16},{1,17},{2,18},{3,19},{4,20},{5,21},{6,22},{7,23},{8,24},{9,... | collective-permute-start | bytes 393224 | tf_op jit(solution)/shard_map/ppermute | solution.py:391
  26.4 3.0 %collective-permute-start.2 = (f32[256,128]{1,0:T(8,128)S(1)}, f32[256,128]{1,0:T(8,128)S(1)}, u32[]{:S(2)}, u32[]{:S(2)}) collective-permute-start(f32[256,128]{1,0:T(8,128)S(1)} %get-tuple-element.23), channel_id=1, source_target_pairs={{0,24},{1,25},{2,26},{3,27},{4,28},{5,29},{6,30},{7,31},{8,0},{9,1... | collective-permute-start | bytes 393224 | tf_op jit(solution)/shard_map/ppermute | solution.py:391
  29.4 0.0 collective-permute-done
  29.4 1.0 %collective-permute-done.1 = f32[256,128]{1,0:T(8,128)S(1)} collective-permute-done((f32[256,128]{1,0:T(8,128)S(1)}, f32[256,128]{1,0:T(8,128)S(1)}, u32[]{:S(2)}, u32[]{:S(2)}) %collective-permute-start.1) | collective-permute-done | bytes 131104 | tf_op jit(solution)/shard_map/ppermute | solution.py:391
  30.4 2.0 %collective-permute-done.2 = f32[256,128]{1,0:T(8,128)S(1)} collective-permute-done((f32[256,128]{1,0:T(8,128)S(1)}, f32[256,128]{1,0:T(8,128)S(1)}, u32[]{:S(2)}, u32[]{:S(2)}) %collective-permute-start.2) | collective-permute-done | bytes 131104 | tf_op jit(solution)/shard_map/ppermute | solution.py:391
  32.4 4.4 %collective-permute-start.5 = (f32[4,256,128]{2,1,0:T(8,128)S(1)}, f32[4,256,128]{2,1,0:T(8,128)S(1)}, u32[]{:S(2)}, u32[]{:S(2)}) collective-permute-start(f32[4,256,128]{2,1,0:T(8,128)S(1)} %pad_maximum_fusion.after_ref.p0), channel_id=1, source_target_pairs={{0,6},{1,7},{2,0},{3,1},{4,2},{5,3},{6,4},{7,5},{8,14},{9,15},{10,... | collective-permute-start | bytes 1572872 | tf_op jit(solution)/shard_map/ppermute | solution.py:391
  36.8 2.4 %collective-permute-start.4 = (f32[4,256,128]{2,1,0:T(8,128)S(1)}, f32[4,256,128]{2,1,0:T(8,128)S(1)}, u32[]{:S(2)}, u32[]{:S(2)}) collective-permute-start(f32[4,256,128]{2,1,0:T(8,128)S(1)} %pad_maximum_fusion.after_ref.p0), channel_id=1, source_target_pairs={{0,4},{1,5},{2,6},{3,7},{4,0},{5,1},{6,2},{7,3},{8,12},{9,13},{10,... | collective-permute-start | bytes 1572872 | tf_op jit(solution)/shard_map/ppermute | solution.py:391
  39.3 2.5 %collective-permute-start.3 = (f32[4,256,128]{2,1,0:T(8,128)S(1)}, f32[4,256,128]{2,1,0:T(8,128)S(1)}, u32[]{:S(2)}, u32[]{:S(2)}) collective-permute-start(f32[4,256,128]{2,1,0:T(8,128)S(1)} %pad_maximum_fusion.after_ref.p0), channel_id=1, source_target_pairs={{0,2},{1,3},{2,4},{3,5},{4,6},{5,7},{6,0},{7,1},{8,10},{9,11},{10,... | collective-permute-start | bytes 1572872 | tf_op jit(solution)/shard_map/ppermute | solution.py:391
  41.8 0.0 all-to-all-done.lines_ref
  41.8 0.0 copy-done.8
  41.8 0.0 copy-done.9
  41.8 2.4 %x_lines.1.after_ref = f32[16,32,256]{2,1,0:T(8,128)} custom-call(f32[16,32,256]{2,1,0:T(8,128)S(1)} %all-to-all-done.lines_ref, f32[4,256,128]{2,1,0:T(8,128)S(1)} %pad_maximum_fusion.after_ref.p0, bf16[2,256,512]{2,1,0:T(8,128)(2,1)S(1)} %copy-done.8, f32[3,9,256]{2,1,0:T(8,128)S(1)} %copy-done.9), custom_call_target="tpu_custom_call" | custom-call | flops 900000000 | bytes 1000000 | tf_op jit(solution)/shard_map/x_lines/pallas_call | solution.py:285
  44.2 11.6 %all-to-all-start.1 = ((f32[16,32,256]{2,1,0:T(8,128)}), f32[16,32,256]{2,1,0:T(8,128)S(1)}, u32[]{:S(2)}, u32[]{:S(2)}) async-start(f32[16,32,256]{2,1,0:T(8,128)} %x_lines.1.after_ref), calls=%async_computation.1 | async-start | bytes 1048576 | tf_op jit(solution)/shard_map/all_to_all | solution.py:538
  55.8 1.6 %load.1.matrix = bf16[2,2,256,1024]{3,2,1,0:T(8,128)(2,1)S(1)} custom-call(s32[1]{0:T(128)} %bitcast.me_ref, f32[16,32,256]{2,1,0:T(8,128)} %x_lines.1.after_ref, bf16[16,2,256,1024]{3,2,1,0:T(8,128)(2,1)} %constant.12.clone.matrix_ref), custom_call_target="tpu_custom_call" | custom-call | bytes 2000000 | tf_op jit(solution)/shard_map/load/pallas_call | solution.py:304
  57.4 0.0 collective-permute-done.5.p3
  57.5 0.0 collective-permute-done.4.p2
  57.5 0.8 y_first.1.sums
  58.3 0.0 copy-start.1
  58.3 0.0 copy-start.2
  58.3 0.0 copy-start.3
  58.3 0.0 copy-start.4
  58.4 0.0 copy-start.5
  58.4 0.0 copy-start.6
  58.4 0.0 copy-start.7
  58.4 6.9 %collective-permute-done.3.p1 = f32[4,256,128]{2,1,0:T(8,128)S(1)} collective-permute-done((f32[4,256,128]{2,1,0:T(8,128)S(1)}, f32[4,256,128]{2,1,0:T(8,128)S(1)}, u32[]{:S(2)}, u32[]{:S(2)}) %collective-permute-start.3) | collective-permute-done | bytes 524320 | tf_op jit(solution)/shard_map/ppermute | solution.py:391
  65.3 0.9 %y_lines.1 = (f32[4,256,128]{2,1,0:T(8,128)S(1)}, f32[4,256,128]{2,1,0:T(8,128)S(1)}) custom-call(f32[4,256,128]{2,1,0:T(8,128)S(1)} %pad_maximum_fusion.after_ref.p0, f32[4,256,128]{2,1,0:T(8,128)S(1)} %collective-permute-done.3.p1, bf16[2,2,256,1024]{3,2,1,0:T(8,128)(2,1)S(1)} %load.1.matrix, f32[4,256,256]{2,1,0:T(8,128)S(1)} %y_first.1.sums), custom_call_target="tpu_custom_call" | custom-call | flops 99999997952 | bytes 4000000 | tf_op jit(solution)/shard_map/y_lines/pallas_call | solution.py:331
  66.2 2.4 %collective-permute-start.6 = (f32[4,256,128]{2,1,0:T(8,128)S(1)}, f32[4,256,128]{2,1,0:T(8,128)S(1)}, u32[]{:S(2)}, u32[]{:S(2)}) collective-permute-start(f32[4,256,128]{2,1,0:T(8,128)S(1)} %get-tuple-element.26), channel_id=1, source_target_pairs={{0,1},{1,0},{2,3},{3,2},{4,5},{5,4},{6,7},{7,6},{8,9},{9,8},{10,11... | collective-permute-start | bytes 1572872 | tf_op jit(solution)/shard_map/ppermute | solution.py:395
  68.6 1.5 %collective-permute-done.6.other_ref = f32[4,256,128]{2,1,0:T(8,128)S(1)} collective-permute-done((f32[4,256,128]{2,1,0:T(8,128)S(1)}, f32[4,256,128]{2,1,0:T(8,128)S(1)}, u32[]{:S(2)}, u32[]{:S(2)}) %collective-permute-start.6) | collective-permute-done | bytes 524320 | tf_op jit(solution)/shard_map/ppermute | solution.py:395
  70.1 0.1 add.1
  70.2 2.6 %collective-permute-start.7 = (f32[256,128]{1,0:T(8,128)S(1)}, f32[256,128]{1,0:T(8,128)S(1)}, u32[]{:S(2)}, u32[]{:S(2)}) collective-permute-start(f32[256,128]{1,0:T(8,128)S(1)} %get-tuple-element.31), channel_id=1, source_target_pairs={{0,8},{1,9},{2,10},{3,11},{4,12},{5,13},{6,14},{7,15},{8,16},{9,17... | collective-permute-start | bytes 393224 | tf_op jit(solution)/shard_map/ppermute | solution.py:391
  72.8 4.7 %collective-permute-start.8 = (f32[256,128]{1,0:T(8,128)S(1)}, f32[256,128]{1,0:T(8,128)S(1)}, u32[]{:S(2)}, u32[]{:S(2)}) collective-permute-start(f32[256,128]{1,0:T(8,128)S(1)} %get-tuple-element.32), channel_id=1, source_target_pairs={{0,16},{1,17},{2,18},{3,19},{4,20},{5,21},{6,22},{7,23},{8,24},{9,... | collective-permute-start | bytes 393224 | tf_op jit(solution)/shard_map/ppermute | solution.py:391
  77.5 2.7 %collective-permute-start.9 = (f32[256,128]{1,0:T(8,128)S(1)}, f32[256,128]{1,0:T(8,128)S(1)}, u32[]{:S(2)}, u32[]{:S(2)}) collective-permute-start(f32[256,128]{1,0:T(8,128)S(1)} %get-tuple-element.33), channel_id=1, source_target_pairs={{0,24},{1,25},{2,26},{3,27},{4,28},{5,29},{6,30},{7,31},{8,0},{9,1... | collective-permute-start | bytes 393224 | tf_op jit(solution)/shard_map/ppermute | solution.py:391
  80.2 0.0 copy-done.1
  80.2 0.0 copy-done.2
  80.2 0.0 copy-done.3
  80.2 0.0 copy-done.4
  80.2 0.0 copy-done.5
  80.2 0.0 copy-done.6
  80.2 0.0 copy-done.7
  80.2 1.7 %base.1 = (f32[2,2,256,128]{3,2,1,0:T(8,128)}, f32[7,2,256,128]{3,2,1,0:T(8,128)S(1)}, f32[256,128]{1,0:T(8,128)S(1)}, f32[8,256]{1,0:T(8,128)S(1)}) custom-call(f32[3,2,256,128]{3,2,1,0:T(8,128)S(1)} %copy-done.1, f32[2,2,256,128]{3,2,1,0:T(8,128)S(1)} %copy-done.3, f32[4,2,256,128]{3,2,1,0:T(8,128)S(1)} %copy-done.2, f32[256,128]{1,0:T(8,128)S(1)} %copy-done.5, ...), custom_call_target="tpu_custom_call" | custom-call | flops 3000000 | bytes 5000000 | tf_op jit(solution)/shard_map/base/pallas_call | solution.py:454
  81.9 0.0 collective-permute-done.7.q1
  81.9 0.0 collective-permute-done.8.q2
  81.9 1.3 %collective-permute-done.9.q3 = f32[256,128]{1,0:T(8,128)S(1)} collective-permute-done((f32[256,128]{1,0:T(8,128)S(1)}, f32[256,128]{1,0:T(8,128)S(1)}, u32[]{:S(2)}, u32[]{:S(2)}) %collective-permute-start.9) | collective-permute-done | bytes 131104 | tf_op jit(solution)/shard_map/ppermute | solution.py:391
  83.2 0.0 all-to-all-done.1.x_deriv
  83.2 1.4 %finish.1 = (f32[3,2,256,128]{3,2,1,0:T(8,128)}, f32[4,2,256,128]{3,2,1,0:T(8,128)}) custom-call(s32[1]{0:T(128)} %bitcast.me_ref, f32[7,2,256,128]{3,2,1,0:T(8,128)S(1)} %get-tuple-element.28.base, f32[256,128]{1,0:T(8,128)S(1)} %get-tuple-element.29.scale, f32[8,256]{1,0:T(8,128)S(1)} %get-tuple-element.30.vectors, ...), custom_call_target="tpu_custom_call" | custom-call | flops 3000000 | bytes 5000000 | tf_op jit(solution)/shard_map/finish/pallas_call | solution.py:520
  (1 shorter events, 0.0 us)
Async XLA Ops:
  0.6 1.1 %copy-start = (f32[3,2,256,128]{3,2,1,0:T(8,128)S(1)}, f32[3,2,256,128]{3,2,1,0:T(8,128)}, u32[]{:S(2)}) copy-start(f32[3,2,256,128]{3,2,1,0:T(8,128)} %fields_ref.1) | copy-start | bytes 2359300
  1.8 40.0 %copy-start.8 = (bf16[2,256,512]{2,1,0:T(8,128)(2,1)S(1)}, bf16[2,256,512]{2,1,0:T(8,128)(2,1)}, u32[]{:S(2)}) copy-start(bf16[2,256,512]{2,1,0:T(8,128)(2,1)} %constant.10.clone.matrix) | copy-start | bytes 1572868
  1.8 40.0 %copy-start.9 = (f32[3,9,256]{2,1,0:T(8,128)S(1)}, f32[3,9,256]{2,1,0:T(8,128)}, u32[]{:S(2)}) copy-start(f32[3,9,256]{2,1,0:T(8,128)} %constant.11.clone.vectors) | copy-start | bytes 82948
  2.7 39.1 %all-to-all-start = ((f32[16,32,256]{2,1,0:T(8,128)}), f32[16,32,256]{2,1,0:T(8,128)S(1)}, u32[]{:S(2)}, u32[]{:S(2)}) async-start(f32[16,32,256]{2,1,0:T(8,128)} %get-tuple-element.24), calls=%async_computation | async-start | bytes 1048576 | tf_op jit(solution)/shard_map/all_to_all | solution.py:538
  18.7 10.7 %collective-permute-start = (f32[256,128]{1,0:T(8,128)S(1)}, f32[256,128]{1,0:T(8,128)S(1)}, u32[]{:S(2)}, u32[]{:S(2)}) collective-permute-start(f32[256,128]{1,0:T(8,128)S(1)} %get-tuple-element.21), channel_id=1, source_target_pairs={{0,8},{1,9},{2,10},{3,11},{4,12},{5,13},{6,14},{7,15},{8,16},{9,17... | collective-permute-start | bytes 393224 | tf_op jit(solution)/shard_map/ppermute | solution.py:391
  21.9 8.5 %collective-permute-start.1 = (f32[256,128]{1,0:T(8,128)S(1)}, f32[256,128]{1,0:T(8,128)S(1)}, u32[]{:S(2)}, u32[]{:S(2)}) collective-permute-start(f32[256,128]{1,0:T(8,128)S(1)} %get-tuple-element.22), channel_id=1, source_target_pairs={{0,16},{1,17},{2,18},{3,19},{4,20},{5,21},{6,22},{7,23},{8,24},{9,... | collective-permute-start | bytes 393224 | tf_op jit(solution)/shard_map/ppermute | solution.py:391
  26.4 6.0 %collective-permute-start.2 = (f32[256,128]{1,0:T(8,128)S(1)}, f32[256,128]{1,0:T(8,128)S(1)}, u32[]{:S(2)}, u32[]{:S(2)}) collective-permute-start(f32[256,128]{1,0:T(8,128)S(1)} %get-tuple-element.23), channel_id=1, source_target_pairs={{0,24},{1,25},{2,26},{3,27},{4,28},{5,29},{6,30},{7,31},{8,0},{9,1... | collective-permute-start | bytes 393224 | tf_op jit(solution)/shard_map/ppermute | solution.py:391
  32.4 25.0 %collective-permute-start.5 = (f32[4,256,128]{2,1,0:T(8,128)S(1)}, f32[4,256,128]{2,1,0:T(8,128)S(1)}, u32[]{:S(2)}, u32[]{:S(2)}) collective-permute-start(f32[4,256,128]{2,1,0:T(8,128)S(1)} %pad_maximum_fusion.after_ref.p0), channel_id=1, source_target_pairs={{0,6},{1,7},{2,0},{3,1},{4,2},{5,3},{6,4},{7,5},{8,14},{9,15},{10,... | collective-permute-start | bytes 1572872 | tf_op jit(solution)/shard_map/ppermute | solution.py:391
  36.8 20.6 %collective-permute-start.4 = (f32[4,256,128]{2,1,0:T(8,128)S(1)}, f32[4,256,128]{2,1,0:T(8,128)S(1)}, u32[]{:S(2)}, u32[]{:S(2)}) collective-permute-start(f32[4,256,128]{2,1,0:T(8,128)S(1)} %pad_maximum_fusion.after_ref.p0), channel_id=1, source_target_pairs={{0,4},{1,5},{2,6},{3,7},{4,0},{5,1},{6,2},{7,3},{8,12},{9,13},{10,... | collective-permute-start | bytes 1572872 | tf_op jit(solution)/shard_map/ppermute | solution.py:391
  39.3 26.0 %collective-permute-start.3 = (f32[4,256,128]{2,1,0:T(8,128)S(1)}, f32[4,256,128]{2,1,0:T(8,128)S(1)}, u32[]{:S(2)}, u32[]{:S(2)}) collective-permute-start(f32[4,256,128]{2,1,0:T(8,128)S(1)} %pad_maximum_fusion.after_ref.p0), channel_id=1, source_target_pairs={{0,2},{1,3},{2,4},{3,5},{4,6},{5,7},{6,0},{7,1},{8,10},{9,11},{10,... | collective-permute-start | bytes 1572872 | tf_op jit(solution)/shard_map/ppermute | solution.py:391
  44.2 39.0 %all-to-all-start.1 = ((f32[16,32,256]{2,1,0:T(8,128)}), f32[16,32,256]{2,1,0:T(8,128)S(1)}, u32[]{:S(2)}, u32[]{:S(2)}) async-start(f32[16,32,256]{2,1,0:T(8,128)} %x_lines.1.after_ref), calls=%async_computation.1 | async-start | bytes 1048576 | tf_op jit(solution)/shard_map/all_to_all | solution.py:538
  58.3 21.9 %copy-start.1 = (f32[3,2,256,128]{3,2,1,0:T(8,128)S(1)}, f32[3,2,256,128]{3,2,1,0:T(8,128)}, u32[]{:S(2)}) copy-start(f32[3,2,256,128]{3,2,1,0:T(8,128)} %fields_ref.1) | copy-start | bytes 2359300
  58.3 21.9 %copy-start.2 = (f32[4,2,256,128]{3,2,1,0:T(8,128)S(1)}, f32[4,2,256,128]{3,2,1,0:T(8,128)}, u32[]{:S(2)}) copy-start(f32[4,2,256,128]{3,2,1,0:T(8,128)} %stretch_ref.1) | copy-start | bytes 3145732
  58.3 21.9 %copy-start.3 = (f32[2,2,256,128]{3,2,1,0:T(8,128)S(1)}, f32[2,2,256,128]{3,2,1,0:T(8,128)}, u32[]{:S(2)}) copy-start(f32[2,2,256,128]{3,2,1,0:T(8,128)} %poles_ref.1) | copy-start | bytes 1572868
  58.3 21.9 %copy-start.4 = (bf16[3,256,128]{2,1,0:T(8,128)(2,1)S(1)}, bf16[3,256,128]{2,1,0:T(8,128)(2,1)}, u32[]{:S(2)}) copy-start(bf16[3,256,128]{2,1,0:T(8,128)(2,1)} %rates_ref.1) | copy-start | bytes 589828
  58.4 21.9 %copy-start.5 = (f32[256,128]{1,0:T(8,128)S(1)}, f32[256,128]{1,0:T(8,128)}, u32[]{:S(2)}) copy-start(f32[256,128]{1,0:T(8,128)} %eps_ref.1) | copy-start | bytes 393220
  58.4 21.8 %copy-start.6 = (f32[3,256]{1,0:T(4,128)S(1)}, f32[3,256]{1,0:T(4,128)}, u32[]{:S(2)}) copy-start(f32[3,256]{1,0:T(4,128)} %x_prof.1) | copy-start | bytes 9220
  58.4 21.8 %copy-start.7 = (f32[3,128]{1,0:T(4,128)S(1)}, f32[3,128]{1,0:T(4,128)}, u32[]{:S(2)}) copy-start(f32[3,128]{1,0:T(4,128)} %y_prof.1) | copy-start | bytes 4612
  66.2 3.9 %collective-permute-start.6 = (f32[4,256,128]{2,1,0:T(8,128)S(1)}, f32[4,256,128]{2,1,0:T(8,128)S(1)}, u32[]{:S(2)}, u32[]{:S(2)}) collective-permute-start(f32[4,256,128]{2,1,0:T(8,128)S(1)} %get-tuple-element.26), channel_id=1, source_target_pairs={{0,1},{1,0},{2,3},{3,2},{4,5},{5,4},{6,7},{7,6},{8,9},{9,8},{10,11... | collective-permute-start | bytes 1572872 | tf_op jit(solution)/shard_map/ppermute | solution.py:395
  70.2 11.7 %collective-permute-start.7 = (f32[256,128]{1,0:T(8,128)S(1)}, f32[256,128]{1,0:T(8,128)S(1)}, u32[]{:S(2)}, u32[]{:S(2)}) collective-permute-start(f32[256,128]{1,0:T(8,128)S(1)} %get-tuple-element.31), channel_id=1, source_target_pairs={{0,8},{1,9},{2,10},{3,11},{4,12},{5,13},{6,14},{7,15},{8,16},{9,17... | collective-permute-start | bytes 393224 | tf_op jit(solution)/shard_map/ppermute | solution.py:391
  72.8 9.1 %collective-permute-start.8 = (f32[256,128]{1,0:T(8,128)S(1)}, f32[256,128]{1,0:T(8,128)S(1)}, u32[]{:S(2)}, u32[]{:S(2)}) collective-permute-start(f32[256,128]{1,0:T(8,128)S(1)} %get-tuple-element.32), channel_id=1, source_target_pairs={{0,16},{1,17},{2,18},{3,19},{4,20},{5,21},{6,22},{7,23},{8,24},{9,... | collective-permute-start | bytes 393224 | tf_op jit(solution)/shard_map/ppermute | solution.py:391
  77.5 5.7 %collective-permute-start.9 = (f32[256,128]{1,0:T(8,128)S(1)}, f32[256,128]{1,0:T(8,128)S(1)}, u32[]{:S(2)}, u32[]{:S(2)}) collective-permute-start(f32[256,128]{1,0:T(8,128)S(1)} %get-tuple-element.33), channel_id=1, source_target_pairs={{0,24},{1,25},{2,26},{3,27},{4,28},{5,29},{6,30},{7,31},{8,0},{9,1... | collective-permute-start | bytes 393224 | tf_op jit(solution)/shard_map/ppermute | solution.py:391

commit v5 on v4

--- a/solution.py
+++ b/solution.py
@@ -478,16 +478,10 @@
 
 
 def finish_kernel(
-    me_ref, base, scale, vectors, x_deriv, q0, q1, q2, q3, next_fields, next_stretch, y_deriv, fields, stretch, sent
+    me_ref, base, scale, vectors, x_deriv, q0, q1, q2, q3, next_fields, next_stretch, fields, stretch, sent
 ):
     own_y = me_ref[0] >> 3
-    for j, quarter in enumerate((q0, q1, q2, q3)):
-        rows = pl.ds(pl.multiple_of(((own_y - j) & 3) * 64, 64), 64)
-        for i in range(4):
-            y_deriv[i, rows, :] = quarter[64 * i : 64 * i + 64, :]
     over_y, feed_y = vectors[2:3, 0:128], vectors[3:4, 0:128]
-    over_x, feed_x = (jnp.broadcast_to(vectors[i : i + 1, :], (128, 256)).T for i in range(2))
-    eps = scale[...]
     copies = []
 
     def send(source, target):
@@ -496,21 +490,27 @@
         copies.append(copy)
 
     for plane in range(2):
-        ez_dy, hx_dy = y_deriv[plane], y_deriv[2 + plane]
-        stretch[2, plane] = base[5, plane] - feed_y * ez_dy
-        stretch[3, plane] = base[6, plane] - feed_y * hx_dy
-        fields[1, plane] = base[1, plane] - section_step * (over_y * ez_dy)
+        for j, quarter in enumerate((q0, q1, q2, q3)):
+            rows = pl.ds(pl.multiple_of(((own_y - j) & 3) * 64, 64), 64)
+            ez_dy = quarter[64 * plane : 64 * plane + 64, :]
+            hx_dy = quarter[128 + 64 * plane : 192 + 64 * plane, :]
+            stretch[2, plane, rows, :] = base[5, plane, rows, :] - feed_y * ez_dy
+            stretch[3, plane, rows, :] = base[6, plane, rows, :] - feed_y * hx_dy
+            fields[1, plane, rows, :] = base[1, plane, rows, :] - section_step * (over_y * ez_dy)
+            fields[0, plane, rows, :] = base[0, plane, rows, :] - scale[rows, :] * (over_y * hx_dy)
         send(stretch.at[pl.ds(2, 2), plane], next_stretch.at[pl.ds(2, 2), plane])
         send(fields.at[1, plane], next_fields.at[1, plane])
+    over_x, feed_x = (jnp.broadcast_to(vectors[i : i + 1, :], (128, 256)).T for i in range(2))
+    eps = scale[...]
     for plane in range(2):
         ez_dx = x_deriv[:, 8 * plane : 8 * plane + 8, :].reshape(128, 256).T
         hy_dx = x_deriv[:, 16 + 8 * plane : 24 + 8 * plane, :].reshape(128, 256).T
         stretch[0, plane] = base[3, plane] - feed_x * ez_dx
         stretch[1, plane] = base[4, plane] - feed_x * hy_dx
+        send(stretch.at[pl.ds(0, 2), plane], next_stretch.at[pl.ds(0, 2), plane])
         fields[2, plane] = base[2, plane] + section_step * (over_x * ez_dx)
-        fields[0, plane] = base[0, plane] + eps * (over_x * hy_dx - over_y * y_deriv[2 + plane])
-        send(stretch.at[pl.ds(0, 2), plane], next_stretch.at[pl.ds(0, 2), plane])
         send(fields.at[2, plane], next_fields.at[2, plane])
+        fields[0, plane] += eps * (over_x * hy_dx)
         send(fields.at[0, plane], next_fields.at[0, plane])
     for copy in copies:
         copy.wait()
@@ -523,7 +523,6 @@
         out_specs=[in_hbm()] * 2,
         out_shape=[jax.ShapeDtypeStruct((count, 2, 256, 128), jnp.float32) for count in (3, 4)],
         scratch_shapes=[
-            pltpu.VMEM((4, 256, 128), jnp.float32),
             pltpu.VMEM((3, 2, 256, 128), jnp.float32),
             pltpu.VMEM((4, 2, 256, 128), jnp.float32),
             pltpu.SemaphoreType.DMA((10,)),

time: 85.4 us -> 85.4 us (level)
  no operation moved by 1% of the time
where the time goes in v5:
time: 85.4 us; the launch traced here: 84.6 us
  starting transfers between devices  60 us (70%)
  waiting for transfers between devices  12.7 us (15%)
  Pallas kernels  9.73 us (11%)
  local copies, waits for them, and re-layouts  1.18 us (1%)
  between operations  0.95 us (1%)
    ppermute x9, starting transfers between devices, shifted(): return lax.ppermute(value, 'gy', pairs)  30 us
    all_to_all x2, starting transfers between devices, swap_x(): lax.all_to_all(lines, 'gx', split_axis=0, concat_axis=0, tiled=True, axis...  27.6 us
    ppermute x9, waiting for transfers between devices, shifted(): return lax.ppermute(value, 'gy', pairs)  11.2 us
    ppermute x1, starting transfers between devices, other_core(): return lax.ppermute(value, 'gy', [(i, i ^ 1) for i in range(32)])  2.4 us
    pallas_call x1, Pallas kernels, x_lines(): pl.pallas_call(x_lines_kernel, in_specs=[in_vmem(), any_place(), in_vmem(...  2.39 us
  transfers between devices with their start and end apart: 12, of which 5 were waited for; matrix products, arithmetic and copies ran while one was open for 0% of the time, Pallas kernels for 9%

profile of v5, /device:TPU:1, one launch (start us, length us, event | category | flops | bytes accessed | tf_op | source)
XLA Modules:
  0.0 84.6 jit_solution(14966471708658666158)
XLA Ops:
  0.6 0.0 copy-start
  0.6 1.1 %copy-done = f32[3,2,256,128]{3,2,1,0:T(8,128)S(1)} copy-done((f32[3,2,256,128]{3,2,1,0:T(8,128)S(1)}, f32[3,2,256,128]{3,2,1,0:T(8,128)}, u32[]{:S(2)}) %copy-start) | copy-done | bytes 786456
  1.8 0.0 copy-start.8
  1.8 0.0 copy-start.9
  1.8 0.9 %pack.1 = (f32[16,32,256]{2,1,0:T(8,128)}, f32[256,128]{1,0:T(8,128)S(1)}, f32[256,128]{1,0:T(8,128)S(1)}, f32[256,128]{1,0:T(8,128)S(1)}, f32[256,128]{1,0:T(8,128)S(1)}) custom-call(s32[1]{0:T(128)} %bitcast.me_ref, f32[3,2,256,128]{3,2,1,0:T(8,128)S(1)} %copy-done), custom_call_target="tpu_custom_call" | custom-call | bytes 2000000 | tf_op jit(solution)/shard_map/pack/pallas_call | solution.py:373
  2.7 16.0 %all-to-all-start = ((f32[16,32,256]{2,1,0:T(8,128)}), f32[16,32,256]{2,1,0:T(8,128)S(1)}, u32[]{:S(2)}, u32[]{:S(2)}) async-start(f32[16,32,256]{2,1,0:T(8,128)} %get-tuple-element.24), calls=%async_computation | async-start | bytes 1048576 | tf_op jit(solution)/shard_map/all_to_all | solution.py:537
  18.7 3.2 %collective-permute-start = (f32[256,128]{1,0:T(8,128)S(1)}, f32[256,128]{1,0:T(8,128)S(1)}, u32[]{:S(2)}, u32[]{:S(2)}) collective-permute-start(f32[256,128]{1,0:T(8,128)S(1)} %get-tuple-element.21), channel_id=1, source_target_pairs={{0,8},{1,9},{2,10},{3,11},{4,12},{5,13},{6,14},{7,15},{8,16},{9,17... | collective-permute-start | bytes 393224 | tf_op jit(solution)/shard_map/ppermute | solution.py:391
  21.9 4.5 %collective-permute-start.1 = (f32[256,128]{1,0:T(8,128)S(1)}, f32[256,128]{1,0:T(8,128)S(1)}, u32[]{:S(2)}, u32[]{:S(2)}) collective-permute-start(f32[256,128]{1,0:T(8,128)S(1)} %get-tuple-element.22), channel_id=1, source_target_pairs={{0,16},{1,17},{2,18},{3,19},{4,20},{5,21},{6,22},{7,23},{8,24},{9,... | collective-permute-start | bytes 393224 | tf_op jit(solution)/shard_map/ppermute | solution.py:391
  26.4 3.0 %collective-permute-start.2 = (f32[256,128]{1,0:T(8,128)S(1)}, f32[256,128]{1,0:T(8,128)S(1)}, u32[]{:S(2)}, u32[]{:S(2)}) collective-permute-start(f32[256,128]{1,0:T(8,128)S(1)} %get-tuple-element.23), channel_id=1, source_target_pairs={{0,24},{1,25},{2,26},{3,27},{4,28},{5,29},{6,30},{7,31},{8,0},{9,1... | collective-permute-start | bytes 393224 | tf_op jit(solution)/shard_map/ppermute | solution.py:391
  29.4 0.0 collective-permute-done
  29.4 1.0 %collective-permute-done.1 = f32[256,128]{1,0:T(8,128)S(1)} collective-permute-done((f32[256,128]{1,0:T(8,128)S(1)}, f32[256,128]{1,0:T(8,128)S(1)}, u32[]{:S(2)}, u32[]{:S(2)}) %collective-permute-start.1) | collective-permute-done | bytes 131104 | tf_op jit(solution)/shard_map/ppermute | solution.py:391
  30.4 2.0 %collective-permute-done.2 = f32[256,128]{1,0:T(8,128)S(1)} collective-permute-done((f32[256,128]{1,0:T(8,128)S(1)}, f32[256,128]{1,0:T(8,128)S(1)}, u32[]{:S(2)}, u32[]{:S(2)}) %collective-permute-start.2) | collective-permute-done | bytes 131104 | tf_op jit(solution)/shard_map/ppermute | solution.py:391
  32.4 4.4 %collective-permute-start.5 = (f32[4,256,128]{2,1,0:T(8,128)S(1)}, f32[4,256,128]{2,1,0:T(8,128)S(1)}, u32[]{:S(2)}, u32[]{:S(2)}) collective-permute-start(f32[4,256,128]{2,1,0:T(8,128)S(1)} %pad_maximum_fusion.after_ref.p0), channel_id=1, source_target_pairs={{0,6},{1,7},{2,0},{3,1},{4,2},{5,3},{6,4},{7,5},{8,14},{9,15},{10,... | collective-permute-start | bytes 1572872 | tf_op jit(solution)/shard_map/ppermute | solution.py:391
  36.8 2.4 %collective-permute-start.4 = (f32[4,256,128]{2,1,0:T(8,128)S(1)}, f32[4,256,128]{2,1,0:T(8,128)S(1)}, u32[]{:S(2)}, u32[]{:S(2)}) collective-permute-start(f32[4,256,128]{2,1,0:T(8,128)S(1)} %pad_maximum_fusion.after_ref.p0), channel_id=1, source_target_pairs={{0,4},{1,5},{2,6},{3,7},{4,0},{5,1},{6,2},{7,3},{8,12},{9,13},{10,... | collective-permute-start | bytes 1572872 | tf_op jit(solution)/shard_map/ppermute | solution.py:391
  39.3 2.5 %collective-permute-start.3 = (f32[4,256,128]{2,1,0:T(8,128)S(1)}, f32[4,256,128]{2,1,0:T(8,128)S(1)}, u32[]{:S(2)}, u32[]{:S(2)}) collective-permute-start(f32[4,256,128]{2,1,0:T(8,128)S(1)} %pad_maximum_fusion.after_ref.p0), channel_id=1, source_target_pairs={{0,2},{1,3},{2,4},{3,5},{4,6},{5,7},{6,0},{7,1},{8,10},{9,11},{10,... | collective-permute-start | bytes 1572872 | tf_op jit(solution)/shard_map/ppermute | solution.py:391
  41.8 0.0 all-to-all-done.lines_ref
  41.8 0.0 copy-done.8
  41.8 0.0 copy-done.9
  41.8 2.4 %x_lines.1.after_ref = f32[16,32,256]{2,1,0:T(8,128)} custom-call(f32[16,32,256]{2,1,0:T(8,128)S(1)} %all-to-all-done.lines_ref, f32[4,256,128]{2,1,0:T(8,128)S(1)} %pad_maximum_fusion.after_ref.p0, bf16[2,256,512]{2,1,0:T(8,128)(2,1)S(1)} %copy-done.8, f32[3,9,256]{2,1,0:T(8,128)S(1)} %copy-done.9), custom_call_target="tpu_custom_call" | custom-call | flops 900000000 | bytes 1000000 | tf_op jit(solution)/shard_map/x_lines/pallas_call | solution.py:285
  44.2 11.6 %all-to-all-start.1 = ((f32[16,32,256]{2,1,0:T(8,128)}), f32[16,32,256]{2,1,0:T(8,128)S(1)}, u32[]{:S(2)}, u32[]{:S(2)}) async-start(f32[16,32,256]{2,1,0:T(8,128)} %x_lines.1.after_ref), calls=%async_computation.1 | async-start | bytes 1048576 | tf_op jit(solution)/shard_map/all_to_all | solution.py:537
  55.8 1.6 %load.1.matrix = bf16[2,2,256,1024]{3,2,1,0:T(8,128)(2,1)S(1)} custom-call(s32[1]{0:T(128)} %bitcast.me_ref, f32[16,32,256]{2,1,0:T(8,128)} %x_lines.1.after_ref, bf16[16,2,256,1024]{3,2,1,0:T(8,128)(2,1)} %constant.12.clone.matrix_ref), custom_call_target="tpu_custom_call" | custom-call | bytes 2000000 | tf_op jit(solution)/shard_map/load/pallas_call | solution.py:304
  57.4 0.0 collective-permute-done.5.p3
  57.5 0.0 collective-permute-done.4.p2
  57.5 0.8 y_first.1.sums
  58.3 0.0 copy-start.1
  58.3 0.0 copy-start.2
  58.3 0.0 copy-start.3
  58.3 0.0 copy-start.4
  58.4 0.0 copy-start.5
  58.4 0.0 copy-start.6
  58.4 0.0 copy-start.7
  58.4 6.9 %collective-permute-done.3.p1 = f32[4,256,128]{2,1,0:T(8,128)S(1)} collective-permute-done((f32[4,256,128]{2,1,0:T(8,128)S(1)}, f32[4,256,128]{2,1,0:T(8,128)S(1)}, u32[]{:S(2)}, u32[]{:S(2)}) %collective-permute-start.3) | collective-permute-done | bytes 524320 | tf_op jit(solution)/shard_map/ppermute | solution.py:391
  65.3 0.9 %y_lines.1 = (f32[4,256,128]{2,1,0:T(8,128)S(1)}, f32[4,256,128]{2,1,0:T(8,128)S(1)}) custom-call(f32[4,256,128]{2,1,0:T(8,128)S(1)} %pad_maximum_fusion.after_ref.p0, f32[4,256,128]{2,1,0:T(8,128)S(1)} %collective-permute-done.3.p1, bf16[2,2,256,1024]{3,2,1,0:T(8,128)(2,1)S(1)} %load.1.matrix, f32[4,256,256]{2,1,0:T(8,128)S(1)} %y_first.1.sums), custom_call_target="tpu_custom_call" | custom-call | flops 99999997952 | bytes 4000000 | tf_op jit(solution)/shard_map/y_lines/pallas_call | solution.py:331
  66.2 2.4 %collective-permute-start.6 = (f32[4,256,128]{2,1,0:T(8,128)S(1)}, f32[4,256,128]{2,1,0:T(8,128)S(1)}, u32[]{:S(2)}, u32[]{:S(2)}) collective-permute-start(f32[4,256,128]{2,1,0:T(8,128)S(1)} %get-tuple-element.26), channel_id=1, source_target_pairs={{0,1},{1,0},{2,3},{3,2},{4,5},{5,4},{6,7},{7,6},{8,9},{9,8},{10,11... | collective-permute-start | bytes 1572872 | tf_op jit(solution)/shard_map/ppermute | solution.py:395
  68.6 1.5 %collective-permute-done.6.other_ref = f32[4,256,128]{2,1,0:T(8,128)S(1)} collective-permute-done((f32[4,256,128]{2,1,0:T(8,128)S(1)}, f32[4,256,128]{2,1,0:T(8,128)S(1)}, u32[]{:S(2)}, u32[]{:S(2)}) %collective-permute-start.6) | collective-permute-done | bytes 524320 | tf_op jit(solution)/shard_map/ppermute | solution.py:395
  70.1 0.1 add.1
  70.2 2.6 %collective-permute-start.7 = (f32[256,128]{1,0:T(8,128)S(1)}, f32[256,128]{1,0:T(8,128)S(1)}, u32[]{:S(2)}, u32[]{:S(2)}) collective-permute-start(f32[256,128]{1,0:T(8,128)S(1)} %get-tuple-element.31), channel_id=1, source_target_pairs={{0,8},{1,9},{2,10},{3,11},{4,12},{5,13},{6,14},{7,15},{8,16},{9,17... | collective-permute-start | bytes 393224 | tf_op jit(solution)/shard_map/ppermute | solution.py:391
  72.8 4.7 %collective-permute-start.8 = (f32[256,128]{1,0:T(8,128)S(1)}, f32[256,128]{1,0:T(8,128)S(1)}, u32[]{:S(2)}, u32[]{:S(2)}) collective-permute-start(f32[256,128]{1,0:T(8,128)S(1)} %get-tuple-element.32), channel_id=1, source_target_pairs={{0,16},{1,17},{2,18},{3,19},{4,20},{5,21},{6,22},{7,23},{8,24},{9,... | collective-permute-start | bytes 393224 | tf_op jit(solution)/shard_map/ppermute | solution.py:391
  77.5 2.7 %collective-permute-start.9 = (f32[256,128]{1,0:T(8,128)S(1)}, f32[256,128]{1,0:T(8,128)S(1)}, u32[]{:S(2)}, u32[]{:S(2)}) collective-permute-start(f32[256,128]{1,0:T(8,128)S(1)} %get-tuple-element.33), channel_id=1, source_target_pairs={{0,24},{1,25},{2,26},{3,27},{4,28},{5,29},{6,30},{7,31},{8,0},{9,1... | collective-permute-start | bytes 393224 | tf_op jit(solution)/shard_map/ppermute | solution.py:391
  80.2 0.0 copy-done.1
  80.2 0.0 copy-done.2
  80.2 0.0 copy-done.3
  80.2 0.0 copy-done.4
  80.2 0.0 copy-done.5
  80.2 0.0 copy-done.6
  80.2 0.0 copy-done.7
  80.2 1.7 %base.1 = (f32[2,2,256,128]{3,2,1,0:T(8,128)}, f32[7,2,256,128]{3,2,1,0:T(8,128)S(1)}, f32[256,128]{1,0:T(8,128)S(1)}, f32[8,256]{1,0:T(8,128)S(1)}) custom-call(f32[3,2,256,128]{3,2,1,0:T(8,128)S(1)} %copy-done.1, f32[2,2,256,128]{3,2,1,0:T(8,128)S(1)} %copy-done.3, f32[4,2,256,128]{3,2,1,0:T(8,128)S(1)} %copy-done.2, f32[256,128]{1,0:T(8,128)S(1)} %copy-done.5, ...), custom_call_target="tpu_custom_call" | custom-call | flops 3000000 | bytes 5000000 | tf_op jit(solution)/shard_map/base/pallas_call | solution.py:454
  81.9 0.0 collective-permute-done.7.q1
  81.9 0.0 collective-permute-done.8.q2
  81.9 1.3 %collective-permute-done.9.q3 = f32[256,128]{1,0:T(8,128)S(1)} collective-permute-done((f32[256,128]{1,0:T(8,128)S(1)}, f32[256,128]{1,0:T(8,128)S(1)}, u32[]{:S(2)}, u32[]{:S(2)}) %collective-permute-start.9) | collective-permute-done | bytes 131104 | tf_op jit(solution)/shard_map/ppermute | solution.py:391
  83.2 0.0 all-to-all-done.1.x_deriv
  83.2 1.4 %finish.1 = (f32[3,2,256,128]{3,2,1,0:T(8,128)}, f32[4,2,256,128]{3,2,1,0:T(8,128)}) custom-call(s32[1]{0:T(128)} %bitcast.me_ref, f32[7,2,256,128]{3,2,1,0:T(8,128)S(1)} %get-tuple-element.28.base, f32[256,128]{1,0:T(8,128)S(1)} %get-tuple-element.29.scale, f32[8,256]{1,0:T(8,128)S(1)} %get-tuple-element.30.vectors, ...), custom_call_target="tpu_custom_call" | custom-call | flops 3000000 | bytes 5000000 | tf_op jit(solution)/shard_map/finish/pallas_call | solution.py:520
  (1 shorter events, 0.0 us)
Async XLA Ops:
  0.6 1.1 %copy-start = (f32[3,2,256,128]{3,2,1,0:T(8,128)S(1)}, f32[3,2,256,128]{3,2,1,0:T(8,128)}, u32[]{:S(2)}) copy-start(f32[3,2,256,128]{3,2,1,0:T(8,128)} %fields_ref.1) | copy-start | bytes 2359300
  1.8 40.0 %copy-start.8 = (bf16[2,256,512]{2,1,0:T(8,128)(2,1)S(1)}, bf16[2,256,512]{2,1,0:T(8,128)(2,1)}, u32[]{:S(2)}) copy-start(bf16[2,256,512]{2,1,0:T(8,128)(2,1)} %constant.10.clone.matrix) | copy-start | bytes 1572868
  1.8 40.0 %copy-start.9 = (f32[3,9,256]{2,1,0:T(8,128)S(1)}, f32[3,9,256]{2,1,0:T(8,128)}, u32[]{:S(2)}) copy-start(f32[3,9,256]{2,1,0:T(8,128)} %constant.11.clone.vectors) | copy-start | bytes 82948
  2.7 39.1 %all-to-all-start = ((f32[16,32,256]{2,1,0:T(8,128)}), f32[16,32,256]{2,1,0:T(8,128)S(1)}, u32[]{:S(2)}, u32[]{:S(2)}) async-start(f32[16,32,256]{2,1,0:T(8,128)} %get-tuple-element.24), calls=%async_computation | async-start | bytes 1048576 | tf_op jit(solution)/shard_map/all_to_all | solution.py:537
  18.7 10.7 %collective-permute-start = (f32[256,128]{1,0:T(8,128)S(1)}, f32[256,128]{1,0:T(8,128)S(1)}, u32[]{:S(2)}, u32[]{:S(2)}) collective-permute-start(f32[256,128]{1,0:T(8,128)S(1)} %get-tuple-element.21), channel_id=1, source_target_pairs={{0,8},{1,9},{2,10},{3,11},{4,12},{5,13},{6,14},{7,15},{8,16},{9,17... | collective-permute-start | bytes 393224 | tf_op jit(solution)/shard_map/ppermute | solution.py:391
  21.9 8.5 %collective-permute-start.1 = (f32[256,128]{1,0:T(8,128)S(1)}, f32[256,128]{1,0:T(8,128)S(1)}, u32[]{:S(2)}, u32[]{:S(2)}) collective-permute-start(f32[256,128]{1,0:T(8,128)S(1)} %get-tuple-element.22), channel_id=1, source_target_pairs={{0,16},{1,17},{2,18},{3,19},{4,20},{5,21},{6,22},{7,23},{8,24},{9,... | collective-permute-start | bytes 393224 | tf_op jit(solution)/shard_map/ppermute | solution.py:391
  26.4 6.0 %collective-permute-start.2 = (f32[256,128]{1,0:T(8,128)S(1)}, f32[256,128]{1,0:T(8,128)S(1)}, u32[]{:S(2)}, u32[]{:S(2)}) collective-permute-start(f32[256,128]{1,0:T(8,128)S(1)} %get-tuple-element.23), channel_id=1, source_target_pairs={{0,24},{1,25},{2,26},{3,27},{4,28},{5,29},{6,30},{7,31},{8,0},{9,1... | collective-permute-start | bytes 393224 | tf_op jit(solution)/shard_map/ppermute | solution.py:391
  32.4 25.0 %collective-permute-start.5 = (f32[4,256,128]{2,1,0:T(8,128)S(1)}, f32[4,256,128]{2,1,0:T(8,128)S(1)}, u32[]{:S(2)}, u32[]{:S(2)}) collective-permute-start(f32[4,256,128]{2,1,0:T(8,128)S(1)} %pad_maximum_fusion.after_ref.p0), channel_id=1, source_target_pairs={{0,6},{1,7},{2,0},{3,1},{4,2},{5,3},{6,4},{7,5},{8,14},{9,15},{10,... | collective-permute-start | bytes 1572872 | tf_op jit(solution)/shard_map/ppermute | solution.py:391
  36.8 20.6 %collective-permute-start.4 = (f32[4,256,128]{2,1,0:T(8,128)S(1)}, f32[4,256,128]{2,1,0:T(8,128)S(1)}, u32[]{:S(2)}, u32[]{:S(2)}) collective-permute-start(f32[4,256,128]{2,1,0:T(8,128)S(1)} %pad_maximum_fusion.after_ref.p0), channel_id=1, source_target_pairs={{0,4},{1,5},{2,6},{3,7},{4,0},{5,1},{6,2},{7,3},{8,12},{9,13},{10,... | collective-permute-start | bytes 1572872 | tf_op jit(solution)/shard_map/ppermute | solution.py:391
  39.3 26.0 %collective-permute-start.3 = (f32[4,256,128]{2,1,0:T(8,128)S(1)}, f32[4,256,128]{2,1,0:T(8,128)S(1)}, u32[]{:S(2)}, u32[]{:S(2)}) collective-permute-start(f32[4,256,128]{2,1,0:T(8,128)S(1)} %pad_maximum_fusion.after_ref.p0), channel_id=1, source_target_pairs={{0,2},{1,3},{2,4},{3,5},{4,6},{5,7},{6,0},{7,1},{8,10},{9,11},{10,... | collective-permute-start | bytes 1572872 | tf_op jit(solution)/shard_map/ppermute | solution.py:391
  44.2 39.0 %all-to-all-start.1 = ((f32[16,32,256]{2,1,0:T(8,128)}), f32[16,32,256]{2,1,0:T(8,128)S(1)}, u32[]{:S(2)}, u32[]{:S(2)}) async-start(f32[16,32,256]{2,1,0:T(8,128)} %x_lines.1.after_ref), calls=%async_computation.1 | async-start | bytes 1048576 | tf_op jit(solution)/shard_map/all_to_all | solution.py:537
  58.3 21.9 %copy-start.1 = (f32[3,2,256,128]{3,2,1,0:T(8,128)S(1)}, f32[3,2,256,128]{3,2,1,0:T(8,128)}, u32[]{:S(2)}) copy-start(f32[3,2,256,128]{3,2,1,0:T(8,128)} %fields_ref.1) | copy-start | bytes 2359300
  58.3 21.9 %copy-start.2 = (f32[4,2,256,128]{3,2,1,0:T(8,128)S(1)}, f32[4,2,256,128]{3,2,1,0:T(8,128)}, u32[]{:S(2)}) copy-start(f32[4,2,256,128]{3,2,1,0:T(8,128)} %stretch_ref.1) | copy-start | bytes 3145732
  58.3 21.9 %copy-start.3 = (f32[2,2,256,128]{3,2,1,0:T(8,128)S(1)}, f32[2,2,256,128]{3,2,1,0:T(8,128)}, u32[]{:S(2)}) copy-start(f32[2,2,256,128]{3,2,1,0:T(8,128)} %poles_ref.1) | copy-start | bytes 1572868
  58.3 21.9 %copy-start.4 = (bf16[3,256,128]{2,1,0:T(8,128)(2,1)S(1)}, bf16[3,256,128]{2,1,0:T(8,128)(2,1)}, u32[]{:S(2)}) copy-start(bf16[3,256,128]{2,1,0:T(8,128)(2,1)} %rates_ref.1) | copy-start | bytes 589828
  58.4 21.9 %copy-start.5 = (f32[256,128]{1,0:T(8,128)S(1)}, f32[256,128]{1,0:T(8,128)}, u32[]{:S(2)}) copy-start(f32[256,128]{1,0:T(8,128)} %eps_ref.1) | copy-start | bytes 393220
  58.4 21.8 %copy-start.6 = (f32[3,256]{1,0:T(4,128)S(1)}, f32[3,256]{1,0:T(4,128)}, u32[]{:S(2)}) copy-start(f32[3,256]{1,0:T(4,128)} %x_prof.1) | copy-start | bytes 9220
  58.4 21.8 %copy-start.7 = (f32[3,128]{1,0:T(4,128)S(1)}, f32[3,128]{1,0:T(4,128)}, u32[]{:S(2)}) copy-start(f32[3,128]{1,0:T(4,128)} %y_prof.1) | copy-start | bytes 4612
  66.2 3.9 %collective-permute-start.6 = (f32[4,256,128]{2,1,0:T(8,128)S(1)}, f32[4,256,128]{2,1,0:T(8,128)S(1)}, u32[]{:S(2)}, u32[]{:S(2)}) collective-permute-start(f32[4,256,128]{2,1,0:T(8,128)S(1)} %get-tuple-element.26), channel_id=1, source_target_pairs={{0,1},{1,0},{2,3},{3,2},{4,5},{5,4},{6,7},{7,6},{8,9},{9,8},{10,11... | collective-permute-start | bytes 1572872 | tf_op jit(solution)/shard_map/ppermute | solution.py:395
  70.2 11.7 %collective-permute-start.7 = (f32[256,128]{1,0:T(8,128)S(1)}, f32[256,128]{1,0:T(8,128)S(1)}, u32[]{:S(2)}, u32[]{:S(2)}) collective-permute-start(f32[256,128]{1,0:T(8,128)S(1)} %get-tuple-element.31), channel_id=1, source_target_pairs={{0,8},{1,9},{2,10},{3,11},{4,12},{5,13},{6,14},{7,15},{8,16},{9,17... | collective-permute-start | bytes 393224 | tf_op jit(solution)/shard_map/ppermute | solution.py:391
  72.8 9.1 %collective-permute-start.8 = (f32[256,128]{1,0:T(8,128)S(1)}, f32[256,128]{1,0:T(8,128)S(1)}, u32[]{:S(2)}, u32[]{:S(2)}) collective-permute-start(f32[256,128]{1,0:T(8,128)S(1)} %get-tuple-element.32), channel_id=1, source_target_pairs={{0,16},{1,17},{2,18},{3,19},{4,20},{5,21},{6,22},{7,23},{8,24},{9,... | collective-permute-start | bytes 393224 | tf_op jit(solution)/shard_map/ppermute | solution.py:391
  77.5 5.7 %collective-permute-start.9 = (f32[256,128]{1,0:T(8,128)S(1)}, f32[256,128]{1,0:T(8,128)S(1)}, u32[]{:S(2)}, u32[]{:S(2)}) collective-permute-start(f32[256,128]{1,0:T(8,128)S(1)} %get-tuple-element.33), channel_id=1, source_target_pairs={{0,24},{1,25},{2,26},{3,27},{4,28},{5,29},{6,30},{7,31},{8,0},{9,1... | collective-permute-start | bytes 393224 | tf_op jit(solution)/shard_map/ppermute | solution.py:391
